TPU v7x, 128 devices: a whole 4x4x4 slice. The times are simulated.
128 devices in a mesh: batch: 8 (over x, core), seq: 16 (over y, z).
Axes of the slice: x: 4, y: 4, z: 4, core: 2. Of those that a mesh axis runs over, the one named last changes fastest.
Arguments:
- item_feats: bfloat16 [32768, 512], P(('batch', 'seq')), may hold values from -6 to 6
- item_weight: bfloat16 [512, 512], replicated, may hold values from -0.25 to 0.25
- send_rows: int32 [128, 256], P(('batch', 'seq')), may hold values from 0 to 255
- event_slot: int32 [49152], P(('batch', 'seq')), may hold values from 0 to 255
- user_blocks: int32 [8, 4], P('batch'), may hold values from 1 to 24, 48 in all within a row
- tail_len: int32 [8, 4], P('batch'), may hold values from 1 to 128
- block_order: int32 [8, 48], P('batch'), may hold values from 0 to 47, each once within a row
- gain_in: float32 [512], replicated, may hold values from 0.1 to 1.9
- gain_mid: float32 [512], replicated, may hold values from 0.1 to 1.9
- w_in: bfloat16 [512, 2048], replicated, may hold values from -0.22097087 to 0.22097087
- w_out: bfloat16 [512, 512], replicated, may hold values from -0.25 to 0.25
- cot_out: bfloat16 [49152, 512], P(('batch', 'seq')), may hold values from -6 to 6
Outputs:
- layer_out: bfloat16 [49152, 512], P(('batch', 'seq'))
- item_grad: float32 [32768, 512], P(('batch', 'seq'))
Inputs may be any that keep to these rules, and one draw needn't show every extreme that they name: `user_blocks`: each batch index's 4 users fill its 48 blocks, none more than 24. `block_order`: each row holds every block once.
All inputs are finite; a program needn't handle non-finite values.
Results may differ from a plain program's by a relative error of at most 0.04.
Values may be sent and summed in bfloat16 or wider, within the bound.
A program may use at most 256 MiB of HBM per device.

v0:
```python
import jax
import jax.numpy as jnp
from jax import lax
from jax.sharding import PartitionSpec as P

HEAD_DIM = 128
BLOCK = 128


def layer_norm(values, gain):
    mean = jnp.mean(values, axis=-1, keepdims=True)
    centred = values - mean
    spread = jnp.mean(centred * centred, axis=-1, keepdims=True)
    return centred * lax.rsqrt(spread + 1e-05) * gain


def norm_back(values, gain, upstream):
    mean = jnp.mean(values, axis=-1, keepdims=True)
    centred = values - mean
    spread = jnp.mean(centred * centred, axis=-1, keepdims=True)
    inverse = lax.rsqrt(spread + 1e-05)
    normal = centred * inverse
    scaled = upstream * gain
    return inverse * (
        scaled
        - jnp.mean(scaled, axis=-1, keepdims=True)
        - normal * jnp.mean(scaled * normal, axis=-1, keepdims=True)
    )


def silu_slope(pre):
    sig = jax.nn.sigmoid(pre)
    return sig * (1.0 + pre * (1.0 - sig))


def event_meta(lengths_row, tails_row, order_row, block):
    users = lengths_row.shape[0]
    ends = jnp.cumsum(lengths_row)
    starts = ends - lengths_row
    user_of = jnp.sum((order_row[:, None] >= ends[None, :]).astype(jnp.int32), axis=1)
    onehot = (user_of[:, None] == jnp.arange(users, dtype=jnp.int32)[None, :]).astype(jnp.int32)
    start_of = jnp.sum(onehot * starts[None, :], axis=1)
    count_of = jnp.sum(onehot * lengths_row[None, :], axis=1)
    tail_of = jnp.sum(onehot * tails_row[None, :], axis=1)
    rank = order_row - start_of
    offsets = jnp.arange(block, dtype=jnp.int32)
    position = rank[:, None] * block + offsets[None, :]
    valid = (rank[:, None] < count_of[:, None] - 1) | (offsets[None, :] < tail_of[:, None])
    user = jnp.broadcast_to(user_of[:, None], (order_row.shape[0], block))
    return (user.reshape(-1), position.reshape(-1), valid.reshape(-1))


def visible_mask(user_q, pos_q, user_k, pos_k, valid_k):
    return (
        (user_q[:, None] == user_k[None, :]) & (pos_k[None, :] <= pos_q[:, None]) & valid_k[None, :]
    )


def attend(query, key, value, mask, head_dim):
    scale = head_dim ** (-0.5)
    outputs = []
    for head in range(query.shape[1] // head_dim):
        cols = slice(head * head_dim, (head + 1) * head_dim)
        scores = jnp.dot(query[:, cols], key[:, cols].T, preferred_element_type=jnp.float32) * scale
        weights = jnp.where(mask, scores * jax.nn.sigmoid(scores), 0.0).astype(jnp.bfloat16)
        outputs.append(jnp.dot(weights, value[:, cols], preferred_element_type=jnp.float32))
    return jnp.concatenate(outputs, axis=1)


def attend_back(query, key, value, d_mixed, mask, head_dim):
    scale = head_dim ** (-0.5)
    d_query, d_key, d_value = ([], [], [])
    for head in range(query.shape[1] // head_dim):
        cols = slice(head * head_dim, (head + 1) * head_dim)
        scores = jnp.dot(query[:, cols], key[:, cols].T, preferred_element_type=jnp.float32) * scale
        sig = jax.nn.sigmoid(scores)
        weights = jnp.where(mask, scores * sig, 0.0).astype(jnp.bfloat16)
        d_value.append(jnp.dot(weights.T, d_mixed[:, cols], preferred_element_type=jnp.float32))
        d_weights = jnp.dot(d_mixed[:, cols], value[:, cols].T, preferred_element_type=jnp.float32)
        d_scores = jnp.where(mask, d_weights * sig * (1.0 + scores * (1.0 - sig)), 0.0).astype(
            jnp.bfloat16
        )
        d_query.append(jnp.dot(d_scores, key[:, cols], preferred_element_type=jnp.float32) * scale)
        d_key.append(
            jnp.dot(d_scores.T, query[:, cols], preferred_element_type=jnp.float32) * scale
        )
    return (
        jnp.concatenate(d_query, axis=1),
        jnp.concatenate(d_key, axis=1),
        jnp.concatenate(d_value, axis=1),
    )


def per_device(
    item_feats,
    item_weight,
    send_rows,
    event_slot,
    user_blocks,
    tail_len,
    block_order,
    gain_in,
    gain_mid,
    w_in,
    w_out,
    cot_out,
):
    width = item_weight.shape[0]
    slots = send_rows.shape[1]
    rows = event_slot.shape[0]
    item_pre = jnp.dot(item_feats, item_weight, preferred_element_type=jnp.float32)
    embedded = jax.nn.silu(item_pre).astype(jnp.bfloat16)
    outgoing = embedded[send_rows[0]]
    arrived = lax.all_to_all(outgoing, ("batch", "seq"), split_axis=0, concat_axis=0, tiled=True)
    tokens = arrived[event_slot]
    user, position, valid = event_meta(user_blocks[0], tail_len[0], block_order[0], BLOCK)
    first = lax.axis_index("seq") * rows
    own_user = lax.dynamic_slice_in_dim(user, first, rows, 0)
    own_pos = lax.dynamic_slice_in_dim(position, first, rows, 0)
    x_full = tokens.astype(jnp.float32)
    normed = layer_norm(x_full, gain_in).astype(jnp.bfloat16)
    pre = jnp.dot(normed, w_in, preferred_element_type=jnp.float32)
    hidden = jax.nn.silu(pre).astype(jnp.bfloat16)
    gate = hidden[:, :width]
    value = hidden[:, width : 2 * width]
    query = hidden[:, 2 * width : 3 * width]
    key = hidden[:, 3 * width :]
    key_all, value_all = (
        lax.all_gather(key, "seq", axis=0, tiled=True),
        lax.all_gather(value, "seq", axis=0, tiled=True),
    )
    mask = visible_mask(own_user, own_pos, user, position, valid)
    mixed = attend(query, key_all, value_all, mask, HEAD_DIM)
    normed_mid = layer_norm(mixed, gain_mid)
    gated = (normed_mid * gate.astype(jnp.float32)).astype(jnp.bfloat16)
    layer_out = (x_full + jnp.dot(gated, w_out, preferred_element_type=jnp.float32)).astype(
        jnp.bfloat16
    )
    d_gated = jnp.dot(cot_out, w_out.T, preferred_element_type=jnp.float32).astype(jnp.bfloat16)
    d_gate = d_gated.astype(jnp.float32) * normed_mid
    d_mixed = norm_back(
        mixed, gain_mid, d_gated.astype(jnp.float32) * gate.astype(jnp.float32)
    ).astype(jnp.bfloat16)
    d_query, key_part, value_part = attend_back(query, key_all, value_all, d_mixed, mask, HEAD_DIM)
    summed = lax.psum_scatter(
        jnp.concatenate([key_part, value_part], axis=1).astype(jnp.bfloat16),
        "seq",
        scatter_dimension=0,
        tiled=True,
    ).astype(jnp.float32)
    d_key = summed[:, :width]
    d_value = summed[:, width:]
    d_hidden = jnp.concatenate([d_gate, d_value, d_query, d_key], axis=1)
    d_pre = (d_hidden * silu_slope(pre)).astype(jnp.bfloat16)
    d_normed = jnp.dot(d_pre, w_in.T, preferred_element_type=jnp.float32)
    d_tokens = cot_out.astype(jnp.float32) + norm_back(x_full, gain_in, d_normed)
    slot_grads = jax.ops.segment_sum(d_tokens, event_slot, num_segments=slots)
    returned = lax.all_to_all(
        slot_grads.astype(jnp.bfloat16), ("batch", "seq"), split_axis=0, concat_axis=0, tiled=True
    ).astype(slot_grads.dtype)
    d_embedded = jax.ops.segment_sum(returned, send_rows[0], num_segments=item_feats.shape[0])
    d_item = (d_embedded * silu_slope(item_pre)).astype(jnp.bfloat16)
    item_grad = jnp.dot(d_item, item_weight.T, preferred_element_type=jnp.float32)
    return (layer_out, item_grad)


def solution(mesh):
    return jax.shard_map(
        per_device,
        mesh=mesh,
        in_specs=(
            P(("batch", "seq"), None),
            P(),
            P(("batch", "seq"), None),
            P(("batch", "seq")),
            P("batch", None),
            P("batch", None),
            P("batch", None),
            P(),
            P(),
            P(),
            P(),
            P(("batch", "seq"), None),
        ),
        out_specs=(P(("batch", "seq"), None), P(("batch", "seq"), None)),
        check_vma=False,
    )
```

profile of v0, /device:TPU:1, one launch (start us, length us, event | category | flops | bytes accessed | tf_op | source)
XLA Modules:
  0.0 403.6 jit_solution(18289224862815037805)
XLA Ops:
  7.2 0.8 compare_select_fusion
  8.0 2.2 multiply_convert_fusion.7
  10.3 1.2 gather_fusion
  11.4 0.8 all_to_all.14
  12.2 11.5 %all-to-all-start = ((bf16[128,2,512]{2,1,0:T(2,128)(2,1)}), bf16[128,2,512]{2,1,0:T(2,128)(2,1)S(1)}, u32[]{:S(2)}, u32[]{:S(2)}) async-start(bf16[128,2,512]{2,1,0:T(2,128)(2,1)} %all_to_all.14), calls=%async_computation | async-start | bytes 524288 | tf_op jit(solution)/shard_map/all_to_all | solution.py:114
  23.8 11.2 %all-to-all-done = bf16[128,2,512]{2,1,0:T(2,128)(2,1)S(1)} async-done(((bf16[128,2,512]{2,1,0:T(2,128)(2,1)}), bf16[128,2,512]{2,1,0:T(2,128)(2,1)S(1)}, u32[]{:S(2)}, u32[]{:S(2)}) %all-to-all-start) | async-done | bytes 262176 | tf_op jit(solution)/shard_map/all_to_all | solution.py:114
  35.0 0.1 all_to_all.16
  35.1 2.1 gather_fusion.1
  37.2 0.1 convert_reduce_fusion
  37.3 0.3 fusion.76
  37.7 3.1 multiply_convert_fusion.1
  40.8 1.2 copy-done.7
  41.9 0.9 fusion.121
  42.9 0.7 all-gather.5.cloned.1.call-update
  43.7 0.2 reduce-window.4
  44.4 56.0 %all-gather.3.cloned.1.call-done = bf16[6144,512]{1,0:T(8,128)(2,1)} async-done(((bf16[384,512]{1,0:T(8,128)(2,1)}), bf16[6144,512]{1,0:T(8,128)(2,1)}) %all-gather.3.cloned.1.call-update) | async-done | bytes 6291472 | tf_op jit(solution)/shard_map/all_gather | solution.py:129
  100.4 3.0 convolution_multiply_fusion
  103.4 0.3 copy-done.4
  103.7 6.4 %convolution_multiply_fusion.1 = f32[384,6144]{1,0:T(8,128)} fusion(bf16[6144,512]{1,0:T(8,128)(2,1)S(1)} %copy-done.4, bf16[384,2048]{1,0:T(8,128)(2,1)} %copy-done.7), kind=kOutput, calls=%fused_computation.18 | convolution fusion | flops 606339072 | bytes 11108352 | tf_op jit(solution)/shard_map/dot_general | solution.py:64
  110.1 6.0 %convolution_multiply_fusion.3 = f32[384,6144]{1,0:T(8,128)} fusion(bf16[6144,512]{1,0:T(8,128)(2,1)S(1)} %copy-done.4, bf16[384,2048]{1,0:T(8,128)(2,1)} %copy-done.7), kind=kOutput, calls=%fused_computation.20 | convolution fusion | flops 606339072 | bytes 11108352 | tf_op jit(solution)/shard_map/dot_general | solution.py:64
  116.1 23.6 %select_convert_fusion.6 = (bf16[384,6144]{1,0:T(8,128)(2,1)}, bf16[384,6144]{1,0:T(8,128)(2,1)}, bf16[384,6144]{1,0:T(8,128)(2,1)}, bf16[384,6144]{1,0:T(8,128)(2,1)}, f32[384,6144]{1,0:T(8,128)}) fusion(pred[6144]{0:T(1024)(128)(4,1)S(1)} %fusion.116, s32[384]{0:T(512)S(1)} %dynamic_slice.7, s32[6144]{0:T(1024)S(1)} %get-tuple-element.32, ...), kind=kOutput, calls=%fused_computation.12 | convolution fusion | flops 672399360 | bytes 58352640 | tf_op jit(solution)/shard_map/dot_general | solution.py:64
  139.7 24.5 %all-gather.5.cloned.1.call-done = bf16[6144,512]{1,0:T(8,128)(2,1)} async-done(((bf16[384,512]{1,0:T(8,128)(2,1)}), bf16[6144,512]{1,0:T(8,128)(2,1)}) %all-gather.5.cloned.1.call-update) | async-done | bytes 6291472 | tf_op jit(solution)/shard_map/all_gather | solution.py:130
  164.2 4.3 %fusion.125 = (f32[384]{0:T(512)S(1)}, f32[384,128]{0,1:T(8,128)S(1)}) fusion(bf16[384,6144]{1,0:T(8,128)(2,1)} %get-tuple-element.13, bf16[6144,512]{1,0:T(8,128)(2,1)} %all-gather.5.cloned.1.call-done), kind=kOutput, calls=%fused_computation.177 | convolution fusion | flops 604028544 | bytes 6489600 | tf_op jit(solution)/shard_map/dot_general | solution.py:66
  168.4 0.1 copy.39
  168.6 4.3 %fusion.123 = (f32[384]{0:T(512)S(1)}, f32[384,128]{0,1:T(8,128)S(1)}) fusion(bf16[384,6144]{1,0:T(8,128)(2,1)} %get-tuple-element.14, bf16[6144,512]{1,0:T(8,128)(2,1)} %all-gather.5.cloned.1.call-done), kind=kOutput, calls=%fused_computation.175 | convolution fusion | flops 604028544 | bytes 6489600 | tf_op jit(solution)/shard_map/dot_general | solution.py:66
  172.8 0.1 copy.40
  173.0 4.3 %fusion.122 = (f32[384]{0:T(512)S(1)}, f32[384,128]{0,1:T(8,128)S(1)}) fusion(bf16[384,6144]{1,0:T(8,128)(2,1)} %get-tuple-element.15, bf16[6144,512]{1,0:T(8,128)(2,1)} %all-gather.5.cloned.1.call-done), kind=kOutput, calls=%fused_computation.174 | convolution fusion | flops 604028544 | bytes 6489600 | tf_op jit(solution)/shard_map/dot_general | solution.py:66
  177.2 0.1 copy.41
  177.4 4.3 %fusion.124 = (f32[384]{0:T(512)S(1)}, f32[384,128]{0,1:T(8,128)S(1)}) fusion(bf16[384,6144]{1,0:T(8,128)(2,1)} %get-tuple-element.16, bf16[6144,512]{1,0:T(8,128)(2,1)} %all-gather.5.cloned.1.call-done), kind=kOutput, calls=%fused_computation.176 | convolution fusion | flops 604028544 | bytes 6489600 | tf_op jit(solution)/shard_map/dot_general | solution.py:66
  181.7 0.1 copy.38
  181.9 0.2 multiply_reduce_fusion.1
  182.2 2.1 fusion.98
  184.3 1.3 multiply_convert_fusion.5
  185.6 8.7 %select_convert_fusion.3 = bf16[384,6144]{1,0:T(8,128)(2,1)S(1)} fusion(f32[384,6144]{1,0:T(8,128)} %convolution_multiply_fusion.3, bf16[6144,512]{1,0:T(8,128)(2,1)} %all-gather.5.cloned.1.call-done, bf16[384,512]{1,0:T(8,128)(2,1)S(1)} %get-tuple-element.9, pred[6144]{0:T(1024)(128)(4,1)S(1)} %fusion.116, s32[384]{0:T(512)S(1)} %dynamic_slice.7, ...), kind=kOutput, calls=%fused_computation.7 | convolution fusion | flops 637009920 | bytes 15886336 | tf_op jit(solution)/shard_map/dot_general | solution.py:79
  194.4 2.8 fusion.5
  197.2 0.3 copy-done.21
  197.5 8.2 %select_convert_fusion.2 = bf16[384,6144]{1,0:T(8,128)(2,1)S(1)} fusion(f32[384,6144]{1,0:T(8,128)} %get-tuple-element.21, bf16[6144,512]{1,0:T(8,128)(2,1)S(1)} %bitcast.60, bf16[384,512]{1,0:T(8,128)(2,1)S(1)} %get-tuple-element.9, pred[6144]{0:T(1024)(128)(4,1)S(1)} %fusion.116, s32[384]{0:T(512)S(1)} %dynamic_slice.7, s32[6144]{0:T(1024)S(1)} %get-tuple-element.32, ...), kind=kOutput, calls=%fused_computation.6 | convolution fusion | flops 637009920 | bytes 15886336 | tf_op jit(solution)/shard_map/dot_general | solution.py:79
  205.8 2.1 copy-done.20
  207.9 2.8 fusion.7
  210.7 7.3 %select_convert_fusion.1 = bf16[384,6144]{1,0:T(8,128)(2,1)} fusion(f32[384,6144]{1,0:T(8,128)S(1)} %bitcast.58, bf16[6144,512]{1,0:T(8,128)(2,1)S(1)} %bitcast.60, bf16[384,512]{1,0:T(8,128)(2,1)S(1)} %get-tuple-element.9, pred[6144]{0:T(1024)(128)(4,1)S(1)} %fusion.116, s32[384]{0:T(512)S(1)} %dynamic_slice.7, s32[6144]{0:T(1024)S(1)} %get-tuple-element.32, ...), kind=kOutput, calls=%fused_computation.5 | convolution fusion | flops 637009920 | bytes 15886336 | tf_op jit(solution)/shard_map/dot_general | solution.py:79
  218.0 5.3 %fusion.9 = bf16[6144,1024]{1,0:T(8,128)(2,1)} fusion(bf16[6144,1024]{1,0:T(8,128)(2,1)} %fusion.7, bf16[384,6144]{1,0:T(8,128)(2,1)} %select_convert_fusion.1, bf16[384,2048]{1,0:T(8,128)(2,1)S(1)} %copy-done.8), kind=kOutput, calls=%fused_computation.38 | convolution fusion | flops 605552640 | bytes 6389760 | tf_op jit(solution)/shard_map/dot_general | solution.py:85
  223.3 7.4 %select_convert_fusion = bf16[384,6144]{1,0:T(8,128)(2,1)} fusion(f32[384,6144]{1,0:T(8,128)S(1)} %bitcast.56, bf16[6144,512]{1,0:T(8,128)(2,1)S(1)} %bitcast.60, bf16[384,512]{1,0:T(8,128)(2,1)S(1)} %get-tuple-element.9, pred[6144]{0:T(1024)(128)(4,1)S(1)} %fusion.116, s32[384]{0:T(512)S(1)} %dynamic_slice.7, s32[6144]{0:T(1024)S(1)} %get-tuple-element.32, ...), kind=kOutput, calls=%fused_computation.4 | convolution fusion | flops 637009920 | bytes 15886336 | tf_op jit(solution)/shard_map/dot_general | solution.py:79
  230.7 5.2 %fusion.11 = bf16[6144,1024]{1,0:T(8,128)(2,1)} fusion(bf16[6144,1024]{1,0:T(8,128)(2,1)} %fusion.9, bf16[384,6144]{1,0:T(8,128)(2,1)} %select_convert_fusion, bf16[384,2048]{1,0:T(8,128)(2,1)S(1)} %copy-done.8), kind=kOutput, calls=%fused_computation.40 | convolution fusion | flops 605552640 | bytes 6389760 | tf_op jit(solution)/shard_map/dot_general | solution.py:85
  235.9 2.7 fusion
  238.7 2.8 fusion.1
  241.4 2.8 fusion.2
  244.2 2.7 fusion.3
  246.9 94.2 %reduce-scatter.2.cloned.1.call-done = bf16[384,1024]{1,0:T(8,128)(2,1)} async-done(((bf16[6144,1024]{1,0:T(8,128)(2,1)}), bf16[384,1024]{1,0:T(8,128)(2,1)}) %reduce-scatter.2.cloned.1.call-update) | async-done | bytes 786448 | tf_op jit(solution)/shard_map/reduce_scatter | solution.py:145
  341.1 1.3 convert_element_type.106
  342.5 1.0 slice_dynamic-update-slice_fusion.1
  343.4 5.5 %fusion.43 = f32[384,2048]{1,0:T(8,128)} fusion(f32[384,2048]{1,0:T(8,128)} %slice_dynamic-update-slice_fusion.1, bf16[384,6144]{1,0:T(8,128)(2,1)} %copy-done.21, bf16[6144,512]{1,0:T(8,128)(2,1)} %all-gather.3.cloned.1.call-done), kind=kOutput, calls=%fused_computation.77 | convolution fusion | flops 604028928 | bytes 6488064 | tf_op jit(solution)/shard_map/dot_general | solution.py:83
  348.9 5.0 %fusion.49 = f32[384,2048]{1,0:T(8,128)} fusion(f32[384,2048]{1,0:T(8,128)} %fusion.43, bf16[384,6144]{1,0:T(8,128)(2,1)} %copy-done.20, bf16[6144,512]{1,0:T(8,128)(2,1)} %all-gather.3.cloned.1.call-done), kind=kOutput, calls=%fused_computation.79 | convolution fusion | flops 604028928 | bytes 6488064 | tf_op jit(solution)/shard_map/dot_general | solution.py:83
  353.9 3.5 fusion.55
  357.4 3.6 fusion.61
  361.1 1.3 slice_dynamic-update-slice_fusion
  362.4 4.3 %fusion.120 = (f32[384]{0:T(512)S(1)}, f32[384]{0:T(512)S(1)}, f32[384,512]{1,0:T(8,128)}) fusion(f32[384]{0:T(512)S(1)} %copy-done.12, f32[384]{0:T(512)S(1)} %copy-done.10, bf16[384,512]{1,0:T(8,128)(2,1)S(1)} %copy-done.3, f32[512]{0:T(512)S(1)} %copy-done.19, bf16[512,2048]{1,0:T(8,128)(2,1)S(1)} %copy-done, ...), kind=kOutput, calls=%fused_computation.172 | convolution fusion | flops 813759744 | bytes 9576448 | tf_op jit(solution)/shard_map/dot_general | solution.py:155
  366.7 4.0 scatter_custom_fusion
  370.6 0.7 convert_element_type.108
  371.4 1.8 all_to_all.17
  373.1 7.5 %all-to-all-start.1 = ((bf16[128,2,512]{2,1,0:T(2,128)(2,1)}), bf16[128,2,512]{2,1,0:T(2,128)(2,1)S(1)}, u32[]{:S(2)}, u32[]{:S(2)}) async-start(bf16[128,2,512]{2,1,0:T(2,128)(2,1)} %all_to_all.17), calls=%async_computation.2 | async-start | bytes 524288 | tf_op jit(solution)/shard_map/all_to_all | solution.py:158
  380.6 2.5 fusion.38
  383.1 8.7 %all-to-all-done.1 = bf16[128,2,512]{2,1,0:T(2,128)(2,1)S(1)} async-done(((bf16[128,2,512]{2,1,0:T(2,128)(2,1)}), bf16[128,2,512]{2,1,0:T(2,128)(2,1)S(1)}, u32[]{:S(2)}, u32[]{:S(2)}) %all-to-all-start.1) | async-done | bytes 262176 | tf_op jit(solution)/shard_map/all_to_all | solution.py:158
  391.9 2.3 scatter_custom_fusion.1
  394.3 2.4 fusion.97
  (117 shorter events, 1.0 us)
Async XLA Ops:
  7.2 30.5 %copy-start = (bf16[512,2048]{1,0:T(8,128)(2,1)S(1)}, bf16[512,2048]{1,0:T(8,128)(2,1)}, u32[]{:S(2)}) copy-start(bf16[512,2048]{1,0:T(8,128)(2,1)} %param.21) | copy-start | bytes 6291460
  7.2 16.6 %copy-start.13 = (s32[384]{0:T(512)S(1)}, s32[384]{0:T(512)}, u32[]{:S(2)}) copy-start(s32[384]{0:T(512)} %param.15) | copy-start | bytes 4612
  10.3 27.4 %copy-start.18 = (f32[512]{0:T(512)S(1)}, f32[512]{0:T(512)}, u32[]{:S(2)}) copy-start(f32[512]{0:T(512)} %param.19) | copy-start | bytes 6148
  12.2 22.7 %all-to-all-start = ((bf16[128,2,512]{2,1,0:T(2,128)(2,1)}), bf16[128,2,512]{2,1,0:T(2,128)(2,1)S(1)}, u32[]{:S(2)}, u32[]{:S(2)}) async-start(bf16[128,2,512]{2,1,0:T(2,128)(2,1)} %all_to_all.14), calls=%async_computation | async-start | bytes 524288 | tf_op jit(solution)/shard_map/all_to_all | solution.py:114
  23.7 76.6 %all-gather.3.cloned.1.call-start = ((), (), s32[]{:S(2)}) async-start(), calls=%async_computation.3 | async-start | bytes 6684672 | tf_op jit(solution)/shard_map/all_gather | solution.py:129
  37.2 3.6 copy-start.2
  37.3 3.4 copy-start.9
  37.6 3.1 copy-start.11
  37.6 6.0 %copy-start.15 = (s32[1,4]{1,0:T(1,128)S(1)}, s32[1,4]{1,0:T(1,128)}, u32[]{:S(2)}) copy-start(s32[1,4]{1,0:T(1,128)} %param.16) | copy-start | bytes 52
  37.7 6.2 %copy-start.17 = (s32[1,48]{1,0:T(1,128)S(1)}, s32[1,48]{1,0:T(1,128)}, u32[]{:S(2)}) copy-start(s32[1,48]{1,0:T(1,128)} %param.18) | copy-start | bytes 580
  37.7 6.3 %copy-start.16 = (s32[1,4]{1,0:T(1,128)S(1)}, s32[1,4]{1,0:T(1,128)}, u32[]{:S(2)}) copy-start(s32[1,4]{1,0:T(1,128)} %param.17) | copy-start | bytes 52
  40.8 1.2 copy-start.7
  42.9 121.3 %all-gather.5.cloned.1.call-start = ((), (), s32[]{:S(2)}) async-start(), calls=%async_computation.4 | async-start | bytes 6684672 | tf_op jit(solution)/shard_map/all_gather | solution.py:130
  43.6 297.5 %reduce-scatter.2.cloned.1.call-start = ((), (), s32[]{:S(2)}) async-start(), calls=%async_computation.5 | async-start | bytes 13369344 | tf_op jit(solution)/shard_map/reduce_scatter | solution.py:145
  100.4 3.3 copy-start.4
  103.7 12.4 %copy-start.1 = (f32[384,6144]{1,0:T(8,128)}, f32[384,6144]{1,0:T(8,128)S(1)}, u32[]{:S(2)}) copy-start(f32[384,6144]{1,0:T(8,128)S(1)} %convolution_multiply_fusion) | copy-start | bytes 28311556
  177.4 6.9 %copy-start.5 = (f32[384,128]{1,0:T(8,128)}, f32[384,128]{1,0:T(8,128)S(1)}, u32[]{:S(2)}) copy-start(f32[384,128]{1,0:T(8,128)S(1)} %copy.41) | copy-start | bytes 589828
  177.4 4.8 %copy-start.14 = (f32[512]{0:T(512)S(1)}, f32[512]{0:T(512)}, u32[]{:S(2)}) copy-start(f32[512]{0:T(512)} %param.20) | copy-start | bytes 6148
  181.9 12.5 %copy-start.6 = (f32[384,128]{1,0:T(8,128)}, f32[384,128]{1,0:T(8,128)S(1)}, u32[]{:S(2)}) copy-start(f32[384,128]{1,0:T(8,128)S(1)} %copy.38) | copy-start | bytes 589828
  181.9 2.4 copy-start.8
  184.3 13.2 %slice-start.14 = ((s8[6291456]{0:T(1024)(128)(4,1)}), s8[4194304]{0:T(1024)(128)(4,1)S(1)}, s32[]{:S(2)}) async-start(s8[6291456]{0:T(1024)(128)(4,1)} %bitcast.59), calls=%async_computation.20 | async-start | bytes 8388608
  185.6 11.9 %slice-start.15 = ((s8[6291456]{0:T(1024)(128)(4,1)}), s8[2097152]{0:T(1024)(128)(4,1)S(1)}, s32[]{:S(2)}) async-start(s8[6291456]{0:T(1024)(128)(4,1)} %bitcast.59), calls=%async_computation.21 | async-start | bytes 4194304
  194.4 3.2 copy-start.21
  194.4 16.3 %slice-start.11 = ((s8[9437184]{0:T(1024)(128)(4,1)}), s8[4194304]{0:T(1024)(128)(4,1)S(1)}, s32[]{:S(2)}) async-start(s8[9437184]{0:T(1024)(128)(4,1)} %bitcast.57), calls=%async_computation.17 | async-start | bytes 8388608
  197.5 13.2 %slice-start.12 = ((s8[9437184]{0:T(1024)(128)(4,1)}), s8[4194304]{0:T(1024)(128)(4,1)S(1)}, s32[]{:S(2)}) async-start(s8[9437184]{0:T(1024)(128)(4,1)} %bitcast.57), calls=%async_computation.18 | async-start | bytes 8388608
  197.5 13.2 %slice-start.13 = ((s8[9437184]{0:T(1024)(128)(4,1)}), s8[1048576]{0:T(1024)(128)(4,1)S(1)}, s32[]{:S(2)}) async-start(s8[9437184]{0:T(1024)(128)(4,1)} %bitcast.57), calls=%async_computation.19 | async-start | bytes 2097152
  205.8 2.1 copy-start.20
  207.9 15.4 %slice-start.8 = ((s8[9437184]{0:T(1024)(128)(4,1)}), s8[4194304]{0:T(1024)(128)(4,1)S(1)}, s32[]{:S(2)}) async-start(s8[9437184]{0:T(1024)(128)(4,1)} %bitcast.55), calls=%async_computation.14 | async-start | bytes 8388608
  210.7 12.6 %slice-start.9 = ((s8[9437184]{0:T(1024)(128)(4,1)}), s8[4194304]{0:T(1024)(128)(4,1)S(1)}, s32[]{:S(2)}) async-start(s8[9437184]{0:T(1024)(128)(4,1)} %bitcast.55), calls=%async_computation.15 | async-start | bytes 8388608
  210.7 12.6 %slice-start.10 = ((s8[9437184]{0:T(1024)(128)(4,1)}), s8[1048576]{0:T(1024)(128)(4,1)S(1)}, s32[]{:S(2)}) async-start(s8[9437184]{0:T(1024)(128)(4,1)} %bitcast.55), calls=%async_computation.16 | async-start | bytes 2097152
  218.0 17.9 %slice-start.6 = ((s8[4718592]{0:T(1024)(128)(4,1)}), s8[4194304]{0:T(1024)(128)(4,1)S(1)}, s32[]{:S(2)}) async-start(s8[4718592]{0:T(1024)(128)(4,1)} %bitcast.53), calls=%async_computation.12 | async-start | bytes 8388608
  218.0 20.7 %slice-start.4 = ((s8[4718592]{0:T(1024)(128)(4,1)}), s8[4194304]{0:T(1024)(128)(4,1)S(1)}, s32[]{:S(2)}) async-start(s8[4718592]{0:T(1024)(128)(4,1)} %bitcast.51), calls=%async_computation.10 | async-start | bytes 8388608
  223.3 12.6 %slice-start.7 = ((s8[4718592]{0:T(1024)(128)(4,1)}), s8[524288]{0:T(1024)(128)(4,1)S(1)}, s32[]{:S(2)}) async-start(s8[4718592]{0:T(1024)(128)(4,1)} %bitcast.53), calls=%async_computation.13 | async-start | bytes 1048576
  223.3 15.4 %slice-start.5 = ((s8[4718592]{0:T(1024)(128)(4,1)}), s8[524288]{0:T(1024)(128)(4,1)S(1)}, s32[]{:S(2)}) async-start(s8[4718592]{0:T(1024)(128)(4,1)} %bitcast.51), calls=%async_computation.11 | async-start | bytes 1048576
  230.7 10.7 %slice-start.2 = ((s8[4718592]{0:T(1024)(128)(4,1)}), s8[4194304]{0:T(1024)(128)(4,1)S(1)}, s32[]{:S(2)}) async-start(s8[4718592]{0:T(1024)(128)(4,1)} %bitcast.49), calls=%async_computation.8 | async-start | bytes 8388608
  235.9 5.5 %slice-start.3 = ((s8[4718592]{0:T(1024)(128)(4,1)}), s8[524288]{0:T(1024)(128)(4,1)S(1)}, s32[]{:S(2)}) async-start(s8[4718592]{0:T(1024)(128)(4,1)} %bitcast.49), calls=%async_computation.9 | async-start | bytes 1048576
  238.7 5.5 %slice-start = ((s8[4718592]{0:T(1024)(128)(4,1)}), s8[4194304]{0:T(1024)(128)(4,1)S(1)}, s32[]{:S(2)}) async-start(s8[4718592]{0:T(1024)(128)(4,1)} %bitcast.47), calls=%async_computation.6 | async-start | bytes 8388608
  241.4 2.8 slice-start.1
  342.4 11.4 %slice-start.16 = ((s8[4718592]{0:T(1024)(128)(4,1)}), s8[4194304]{0:T(1024)(128)(4,1)S(1)}, s32[]{:S(2)}) async-start(s8[4718592]{0:T(1024)(128)(4,1)} %bitcast.68), calls=%async_computation.22 | async-start | bytes 8388608
  343.4 10.4 %slice-start.17 = ((s8[4718592]{0:T(1024)(128)(4,1)}), s8[524288]{0:T(1024)(128)(4,1)S(1)}, s32[]{:S(2)}) async-start(s8[4718592]{0:T(1024)(128)(4,1)} %bitcast.68), calls=%async_computation.23 | async-start | bytes 1048576
  343.4 13.9 %slice-start.18 = ((s8[4718592]{0:T(1024)(128)(4,1)}), s8[4194304]{0:T(1024)(128)(4,1)S(1)}, s32[]{:S(2)}) async-start(s8[4718592]{0:T(1024)(128)(4,1)} %bitcast.70), calls=%async_computation.24 | async-start | bytes 8388608
  348.9 8.5 %slice-start.19 = ((s8[4718592]{0:T(1024)(128)(4,1)}), s8[524288]{0:T(1024)(128)(4,1)S(1)}, s32[]{:S(2)}) async-start(s8[4718592]{0:T(1024)(128)(4,1)} %bitcast.70), calls=%async_computation.25 | async-start | bytes 1048576
  357.4 5.0 %copy-start.3 = (bf16[384,512]{1,0:T(8,128)(2,1)S(1)}, bf16[384,512]{1,0:T(8,128)(2,1)}, u32[]{:S(2)}) copy-start(bf16[384,512]{1,0:T(8,128)(2,1)} %copy-done.2) | copy-start | bytes 1179652
  357.4 5.0 %copy-start.10 = (f32[384]{0:T(512)S(1)}, f32[384]{0:T(512)}, u32[]{:S(2)}) copy-start(f32[384]{0:T(512)} %copy-done.9) | copy-start | bytes 4612
  357.4 5.0 %copy-start.12 = (f32[384]{0:T(512)S(1)}, f32[384]{0:T(512)}, u32[]{:S(2)}) copy-start(f32[384]{0:T(512)} %copy-done.11) | copy-start | bytes 4612
  357.4 5.0 %copy-start.19 = (f32[512]{0:T(512)S(1)}, f32[512]{0:T(512)}, u32[]{:S(2)}) copy-start(f32[512]{0:T(512)} %param.19) | copy-start | bytes 6148
  357.4 4.9 %copy-start.22 = (f32[384,2048]{1,0:T(8,128)S(1)}, f32[384,2048]{1,0:T(8,128)}, u32[]{:S(2)}) copy-start(f32[384,2048]{1,0:T(8,128)} %get-tuple-element.20) | copy-start | bytes 9437188
  373.1 18.7 %all-to-all-start.1 = ((bf16[128,2,512]{2,1,0:T(2,128)(2,1)}), bf16[128,2,512]{2,1,0:T(2,128)(2,1)S(1)}, u32[]{:S(2)}, u32[]{:S(2)}) async-start(bf16[128,2,512]{2,1,0:T(2,128)(2,1)} %all_to_all.17), calls=%async_computation.2 | async-start | bytes 524288 | tf_op jit(solution)/shard_map/all_to_all | solution.py:158
Sparse Core Ops, SparseCore 0:
  43.0 57.3 all-gather.2
  103.1 60.9 all-gather.4
  247.0 94.0 reduce-scatter.1
where the time goes:
time: 411 us; the launch traced here: 404 us
  waiting for transfers between devices  195 us (47%)
  matrix products  149 us (36%)
  starting transfers between devices  19.1 us (5%)
  between operations  14.7 us (4%)
  local copies, waits for them, and re-layouts  13.9 us (3%)
  other arithmetic  11.8 us (3%)
    reduce_scatter x1, waiting for transfers between devices, per_device(): lax.psum_scatter(jnp.concatenate([key_part, value_part], axis=1).astype(j...  94.2 us
    all_gather x1, waiting for transfers between devices, per_device(): lax.all_gather(key, 'seq', axis=0, tiled=True)  56 us
    dot_general x4, matrix products, attend(): jnp.dot(query[:, cols], key[:, cols].T, preferred_element_type=jnp.float32)  38.9 us
    dot_general x4, matrix products, attend_back(): jnp.dot(d_mixed[:, cols], value[:, cols].T, preferred_element_type=jnp.fl...  31.6 us
    all_gather x1, waiting for transfers between devices, per_device(): lax.all_gather(value, 'seq', axis=0, tiled=True)  24.5 us
    dot_general x4, matrix products, attend_back(): jnp.dot(d_scores, key[:, cols], preferred_element_type=jnp.float32) * scale  17.6 us
    dot_general x4, matrix products, attend(): jnp.dot(weights, value[:, cols], preferred_element_type=jnp.float32)  17.1 us
    dot_general x4, matrix products, attend_back(): jnp.dot(d_scores.T, query[:, cols], preferred_element_type=jnp.float32)  16 us
  transfers between devices with their start and end apart: 5, of which 5 were waited for; matrix products, arithmetic and copies ran while one was open for 10% of the time, Pallas kernels for 0%

commit v1 on v0

v1 whole, which is shorter than its diff:
```python
import jax
import jax.numpy as jnp
from jax import lax
from jax.experimental import pallas as pl
from jax.experimental.pallas import tpu as pltpu
from jax.sharding import PartitionSpec as P

WIDTH = 512
HEAD = 128
HEADS = 4
BLOCK = 128
BLOCKS = 48
SEQ = 16
GROUPS = 8
PIECE = 32
TILES = 12
HALF = 192
ROWS = 384
FAR = 1 << 20
SCALE = HEAD**-0.5
MESH = pl.DeviceIdType.MESH
F32 = jnp.float32
BF16 = jnp.bfloat16


def dot_nn(a, b):
    return jnp.dot(a, b, preferred_element_type=F32)


def dot_nt(a, b):
    return lax.dot_general(a, b, (((1,), (1,)), ((), ())), preferred_element_type=F32)


def dot_tn(a, b):
    return lax.dot_general(a, b, (((0,), (0,)), ((), ())), preferred_element_type=F32)


def silu(v):
    u = 0.5 * v
    return u + u * jnp.tanh(u)


def silu_slope(v):
    u = 0.5 * v
    t = jnp.tanh(u)
    a = 1.0 + t
    return 0.5 * (a + u * a * (1.0 - t))


def normalize(values):
    mean = jnp.mean(values, axis=-1, keepdims=True)
    centred = values - mean
    spread = jnp.mean(centred * centred, axis=-1, keepdims=True)
    inverse = lax.rsqrt(spread + 1e-05)
    return centred * inverse, inverse


def iota(shape, dim):
    return lax.broadcasted_iota(jnp.int32, shape, dim)


def place():
    b, s = lax.axis_index("batch"), lax.axis_index("seq")
    return b, s, b // 2, b % 2, s // 4, s % 4


def worker_at(w, x, c):
    head, half, core = w % 4, (w // 4) % 2, w // 8
    return head, half, core, x * 2 + core, (2 * c + half) * 4 + head


def copy_to(src, dst, send, recv, batch, seq):
    return pltpu.make_async_remote_copy(
        src_ref=src, dst_ref=dst, send_sem=send, recv_sem=recv, device_id=(batch, seq), device_id_type=MESH
    )


def arrived(ref, sem):
    pltpu.make_async_copy(ref, ref, sem).wait()


def rows_of(index, size):
    return pl.ds(pl.multiple_of(index * size, size), size)


def slot_onehot(event_slot):
    e = event_slot
    wanted = ((e >> 1) & 15) * 16 + (e >> 5) * 2 + (e & 1)
    return (iota((256, ROWS), 0) == wanted).astype(BF16)


def by_seq():
    i, j = iota((256, 256), 0), iota((256, 256), 1)
    return (j == ((i >> 1) & 7) * 32 + (i >> 4) * 2 + (i & 1)).astype(BF16)


def by_batch():
    i, j = iota((256, 256), 0), iota((256, 256), 1)
    return (j == ((i >> 1) & 15) * 16 + (i >> 5) * 2 + (i & 1)).astype(BF16)


def exchange_batch(src, dst, send, recv, b, s):
    copies = []
    for k in range(1, GROUPS):
        peer = lax.rem(b + k, GROUPS)
        copy = copy_to(src.at[rows_of(peer, 32)], dst.at[rows_of(b, 32)], send.at[k], recv.at[k], peer, s)
        copy.start()
        copies.append(copy)
    dst[rows_of(b, 32), :] = src[rows_of(b, 32), :]
    return copies


def exchange_seq(src, dst, send, recv, b, s):
    copies = []
    for k in range(1, SEQ):
        peer = lax.rem(s + k, SEQ)
        copy = copy_to(src.at[rows_of(peer, 16)], dst.at[rows_of(s, 16)], send.at[k], recv.at[k], b, peer)
        copy.start()
        copies.append(copy)
    dst[rows_of(s, 16), :] = src[rows_of(s, 16), :]
    return copies


def wait_all(copies):
    for copy in copies:
        copy.wait()


def send_kernel(
    feats, item_weight, send_rows, event_slot, user_blocks, tail_len, block_order, gain_in, gain_mid, w_in, w_out, cot,
    kv_out, qp_out, tokens_out, meta_out,
    out1, in1, out2, in2, kv, qp, meta_own, meta_other,
    send1, recv1, send2, recv2, kv_send, kv_recv, pass_send, pass_recv, qp_send, qp_recv, meta_send, meta_recv,
):
    b, s, x, c, y, z = place()
    partner = x * 2 + 1 - c
    mine = y // 2

    embedded = silu(dot_nn(feats[...], item_weight[...])).astype(BF16)
    wanted = (iota((256, 256), 0) == send_rows[...]).astype(BF16)
    out1[...] = dot_tn(wanted, embedded).astype(BF16)
    first = exchange_batch(out1, in1, send1, recv1, b, s)

    meta_own[...] = jnp.zeros_like(meta_own)
    meta_own[0:1, 0:48] = block_order[...]
    meta_own[1:2, 0:4] = user_blocks[...]
    meta_own[2:3, 0:4] = tail_len[...]
    meta_copy = copy_to(meta_own, meta_other, meta_send, meta_recv, partner, s)
    meta_copy.start()

    d_gated = dot_nt(cot[...], w_out[...]).astype(BF16)
    wait_all(first)
    out2[...] = dot_nn(by_seq(), in1[...]).astype(BF16)
    second = exchange_seq(out2, in2, send2, recv2, b, s)
    onehot = slot_onehot(event_slot[...])
    wait_all(second)
    tokens = dot_tn(onehot, in2[...])
    tokens_out[...] = tokens.astype(BF16)
    normed = (normalize(tokens)[0] * gain_in[...]).astype(BF16)

    for part, first_column in ((0, 1536), (1, 512)):
        lanes = slice(part * HEAD, part * HEAD + HEAD)
        made = silu(dot_nn(normed, w_in[:, first_column : first_column + WIDTH])).astype(BF16)
        for h in range(HEADS):
            kv[h, 0, :, lanes] = made[:HALF, h * HEAD : (h + 1) * HEAD]
            kv[h, 1, :, lanes] = made[HALF:, h * HEAD : (h + 1) * HEAD]

    def each_worker(act):
        @pl.loop(0, SEQ)
        def _(i):
            w = lax.rem(i + s, SEQ)
            head, half, core, to_batch, to_seq = worker_at(w, x, c)
            here = (to_batch == b) & (to_seq == s)
            act(w, head, half, core, to_batch, to_seq, here)

    def kv_copy(w, head, core, to_batch, to_seq):
        return copy_to(kv.at[head, core], kv_out.at[s, core], kv_send.at[w], kv_recv.at[s], to_batch, to_seq)

    def start_kv(w, head, half, core, to_batch, to_seq, here):
        @pl.when(here)
        def _():
            pltpu.make_async_copy(kv.at[head, core], kv_out.at[s, core], kv_recv.at[s]).start()

        @pl.when(jnp.logical_not(here))
        def _():
            kv_copy(w, head, core, to_batch, to_seq).start()

    each_worker(start_kv)

    query = silu(dot_nn(normed, w_in[:, 1024:1536])).astype(BF16)
    gate = silu(dot_nn(normed, w_in[:, 0:WIDTH])).astype(BF16)
    upstream = (d_gated.astype(F32) * gate.astype(F32) * gain_mid[...]).astype(BF16)
    for h in range(HEADS):
        cols = slice(h * HEAD, (h + 1) * HEAD)
        qp[h, :, :, :, 0:HEAD] = query[:, cols].reshape(3, 4, PIECE, HEAD)
        qp[h, :, :, :, HEAD : 2 * HEAD] = upstream[:, cols].reshape(3, 4, PIECE, HEAD)

    def qp_copy(w, head, half, core, to_batch, to_seq):
        return copy_to(
            qp.at[head, :, half * 2 + core], qp_out.at[s], qp_send.at[w], qp_recv.at[s], to_batch, to_seq
        )

    def start_qp(w, head, half, core, to_batch, to_seq, here):
        @pl.when(here)
        def _():
            pltpu.make_async_copy(qp.at[head, :, half * 2 + core], qp_out.at[s], qp_recv.at[s]).start()

        @pl.when(jnp.logical_not(here))
        def _():
            qp_copy(w, head, half, core, to_batch, to_seq).start()

    each_worker(start_qp)

    meta_copy.wait()
    row, lane = iota((8, 128), 0), iota((8, 128), 1)
    own = (jnp.zeros((8, 128), jnp.int32) + (mine == c).astype(jnp.int32)) == 1
    meta = jnp.where(own, meta_own[...], meta_other[...])
    meta_out[...] = jnp.where(row == 3, (y % 2) * 2 + c, meta)

    def pass_on(source):
        return copy_to(
            kv_out.at[source, c], kv_out.at[source, c], pass_send.at[source], pass_recv.at[source], partner, s
        )

    @pl.loop(0, SEQ)
    def _(i):
        source = lax.rem(s - i + SEQ, SEQ)
        arrived(kv_out.at[source, c], kv_recv.at[source])
        pass_on(source).start()

    def finish(w, head, half, core, to_batch, to_seq, here):
        @pl.when(jnp.logical_not(here))
        def _():
            kv_copy(w, head, core, to_batch, to_seq).wait_send()
            qp_copy(w, head, half, core, to_batch, to_seq).wait_send()

    each_worker(finish)

    @pl.loop(0, SEQ)
    def _(source):
        pass_on(source).wait_send()
        arrived(kv_out.at[source, 1 - c], pass_recv.at[source])
        arrived(qp_out.at[source], qp_recv.at[source])


def read_meta(meta, slot_of, start_of, limit_of):
    @pl.loop(0, BLOCKS)
    def _(i):
        slot_of[meta[0, i]] = i

    first = jnp.int32(0)
    for u in range(4):
        count = meta[1, u]

        @pl.loop(first, first + count)
        def _(n, first=first, count=count, u=u):
            start_of[n] = first
            limit_of[n] = jnp.where(n == first + count - 1, meta[2, u], BLOCK)

        first = first + count


def fetch(slot_of, kv_hbm, qp_hbm, kv, qp, kv_sem, qp_sem):
    @pl.loop(0, TILES)
    def _(t):
        for i in range(4):
            n = t * 4 + i
            slot = slot_of[n]
            pltpu.make_async_copy(qp_hbm.at[slot], qp.at[n], qp_sem.at[t]).start()
            pltpu.make_async_copy(kv_hbm.at[slot], kv.at[n], kv_sem.at[t]).start()


def wait_tile(t, kv, qp, kv_sem, qp_sem):
    four = pl.ds(t * 4, 4)
    arrived(qp.at[four], qp_sem.at[t])
    arrived(kv.at[four], kv_sem.at[t])


def pick4(index, values):
    return jnp.where(index == 0, values[0], jnp.where(index == 1, values[1], jnp.where(index == 2, values[2], values[3])))


def forward_kernel(
    meta, kv_hbm, qp_hbm, mixed_out, stats_out, kv, qp, slot_of, start_of, limit_of, kv_sem, qp_sem
):
    read_meta(meta, slot_of, start_of, limit_of)
    fetch(slot_of, kv_hbm, qp_hbm, kv, qp, kv_sem, qp_sem)
    quarter = meta[3, 0]

    @pl.loop(0, TILES)
    def _(t):
        wait_tile(t, kv, qp, kv_sem, qp_sem)
        both = qp[pl.ds(t * 4, 4)].reshape(BLOCK, 2 * HEAD)
        query, upstream = both[:, :HEAD], both[:, HEAD:].astype(F32)
        r = iota((BLOCK, 1), 0)
        at = (t * 4 + (r >> 5)) * BLOCK + quarter * PIECE + (r & 31)
        since = pick4(r >> 5, [start_of[t * 4 + i] for i in range(4)]) * BLOCK

        def chunk(j, total):
            both = kv[pl.ds(j * 4, 4)].reshape(4 * BLOCK, 2 * HEAD)
            key, value = both[:, :HEAD], both[:, HEAD:]
            u = dot_nt(query, key) * (0.5 * SCALE)
            weights = u + u * jnp.tanh(u)
            lane = iota((1, BLOCK), 1)
            where = jnp.concatenate(
                [
                    jnp.where(lane < limit_of[j * 4 + i], (j * 4 + i) * BLOCK + lane, FAR)
                    for i in range(4)
                ],
                axis=1,
            )
            weights = jnp.where((where <= at) & (where >= since), weights, 0.0).astype(BF16)
            return total + dot_nn(weights, value)

        mixed = lax.fori_loop(start_of[t * 4] // 4, t + 1, chunk, jnp.zeros((BLOCK, HEAD), F32))
        mixed_out[t] = mixed
        mean = jnp.mean(mixed, axis=1, keepdims=True)
        centred = mixed - mean
        lane = iota((BLOCK, HEAD), 1)
        stats = pick4(
            lane,
            [
                mean,
                jnp.sum(centred * centred, axis=1, keepdims=True),
                jnp.sum(upstream, axis=1, keepdims=True),
                jnp.sum(upstream * centred, axis=1, keepdims=True),
            ],
        )
        stats_out[t] = jnp.transpose(stats)[0:8, :]


def stats_kernel(stats, all_stats, held, send, recv):
    b, s, x, c, y, z = place()
    copies = []
    for k in range(1, HEADS):
        peer = lax.rem(z + k, HEADS)
        copy = copy_to(stats, held.at[z], send.at[k], recv.at[k], b, y * 4 + peer)
        copy.start()
        copies.append(copy)
    held[z] = stats[...]
    wait_all(copies)
    all_stats[...] = held[...]


def backward_kernel(
    meta, kv_hbm, qp_hbm, mixed_in, stats_in, mq_hbm, dkv_hbm,
    kv, qp, mq, dkv, dkv_out, slot_of, start_of, limit_of, kv_sem, qp_sem, mq_sem, dkv_sem,
):
    read_meta(meta, slot_of, start_of, limit_of)
    fetch(slot_of, kv_hbm, qp_hbm, kv, qp, kv_sem, qp_sem)
    quarter = meta[3, 0]

    @pl.loop(0, TILES)
    def _(t):
        dkv[pl.ds(t * 4 * BLOCK, 4 * BLOCK), :] = jnp.zeros((4 * BLOCK, 2 * HEAD), F32)

    @pl.loop(0, TILES)
    def _(t):
        wait_tile(t, kv, qp, kv_sem, qp_sem)
        both = qp[pl.ds(t * 4, 4)].reshape(BLOCK, 2 * HEAD)
        query, upstream = both[:, :HEAD], both[:, HEAD:].astype(F32)
        mixed = mixed_in[t]

        stats = [stats_in[h, t] for h in range(HEADS)]
        mean = sum(v[0:1] for v in stats) * 0.25
        spread = sum(v[1:2] + HEAD * (v[0:1] - mean) * (v[0:1] - mean) for v in stats) * (1.0 / WIDTH)
        inverse = lax.rsqrt(spread + 1e-05)
        slant = sum(v[2:3] for v in stats) * (1.0 / WIDTH)
        along = sum(v[3:4] + v[2:3] * (v[0:1] - mean) for v in stats) * (1.0 / WIDTH) * inverse
        r8 = iota((BLOCK, HEAD), 0)
        columns = jnp.transpose(pick4(r8, [mean, inverse, slant, along]))
        mean, inverse, slant, along = (columns[:, i : i + 1] for i in range(4))
        normal = (mixed - mean) * inverse
        d_mixed = (inverse * (upstream - slant - normal * along)).astype(BF16)

        r = iota((1, BLOCK), 1)
        at = (t * 4 + (r >> 5)) * BLOCK + quarter * PIECE + (r & 31)
        since = pick4(r >> 5, [start_of[t * 4 + i] for i in range(4)]) * BLOCK

        def chunk(j, total):
            both = kv[pl.ds(j * 4, 4)].reshape(4 * BLOCK, 2 * HEAD)
            key, value = both[:, :HEAD], both[:, HEAD:]
            u = dot_nt(key, query) * (0.5 * SCALE)
            th = jnp.tanh(u)
            a = 1.0 + th
            weights = u * a
            slope = a + weights * (1.0 - th)
            d_scores = dot_nt(value, d_mixed) * slope
            row = iota((BLOCK, 1), 0)
            where = jnp.concatenate(
                [
                    jnp.where(row < limit_of[j * 4 + i], (j * 4 + i) * BLOCK + row, FAR)
                    for i in range(4)
                ],
                axis=0,
            )
            seen = (where <= at) & (where >= since)
            weights = jnp.where(seen, weights, 0.0).astype(BF16)
            d_scores = jnp.where(seen, d_scores, 0.0).astype(BF16)
            keys = pl.ds(pl.multiple_of(j * 4 * BLOCK, 4 * BLOCK), 4 * BLOCK)
            dkv[keys, 0:HEAD] += dot_nn(d_scores, query)
            dkv[keys, HEAD : 2 * HEAD] += dot_nn(weights, d_mixed)
            return total + dot_tn(d_scores, key)

        d_query = lax.fori_loop(start_of[t * 4] // 4, t + 1, chunk, jnp.zeros((BLOCK, HEAD), F32))
        d_query = (d_query * (0.5 * SCALE)).astype(BF16)
        mq[pl.ds(t * 4, 4), :, 0:HEAD] = mixed.astype(BF16).reshape(4, PIECE, HEAD)
        mq[pl.ds(t * 4, 4), :, HEAD : 2 * HEAD] = d_query.reshape(4, PIECE, HEAD)
        for i in range(4):
            n = t * 4 + i
            pltpu.make_async_copy(mq.at[n], mq_hbm.at[slot_of[n]], mq_sem.at[n]).start()

    @pl.loop(0, BLOCKS)
    def _(n):
        keys = pl.ds(pl.multiple_of(n * BLOCK, BLOCK), BLOCK)
        dkv_out[n, :, 0:HEAD] = (dkv[keys, 0:HEAD] * (0.5 * SCALE)).astype(BF16)
        dkv_out[n, :, HEAD : 2 * HEAD] = dkv[keys, HEAD : 2 * HEAD].astype(BF16)
        pltpu.make_async_copy(dkv_out.at[n], dkv_hbm.at[slot_of[n]], dkv_sem.at[n]).start()

    @pl.loop(0, BLOCKS)
    def _(n):
        pltpu.make_async_copy(mq.at[n], mq_hbm.at[slot_of[n]], mq_sem.at[n]).wait()
        pltpu.make_async_copy(dkv_out.at[n], dkv_hbm.at[slot_of[n]], dkv_sem.at[n]).wait()


def return_kernel(
    feats, item_weight, send_rows, event_slot, gain_in, gain_mid, w_in, w_out, cot, tokens_in, mq_in, dkv_in,
    layer_out, item_grad,
    mq, dkv, own, part, pre, d_pre, out2, in2, out1, in1,
    own_sem, part_send, part_recv, mq_send, mq_recv, dkv_send, dkv_recv, send2, recv2, send1, recv1,
):
    b, s, x, c, y, z = place()
    partner = x * 2 + 1 - c
    mine = y // 2
    half = y % 2
    to_batch = x * 2 + mine
    me = z + 4 * half + 8 * c

    def group_order(k):
        return lax.rem(k + z, 4)

    def own_copy(g):
        return pltpu.make_async_copy(dkv_in.at[pl.ds(g * 4, 4), c], own.at[pl.ds(g * 4, 4)], own_sem.at[g])

    def part_copy(g):
        return copy_to(
            dkv_in.at[pl.ds(g * 4, 4), 1 - c], part.at[pl.ds(g * 4, 4)], part_send.at[g], part_recv.at[g], partner, s
        )

    @pl.loop(0, 4)
    def _(k):
        g = group_order(k)
        own_copy(g).start()
        part_copy(g).start()

    def is_here(source):
        return (to_batch == b) & (source == s)

    def mq_copy(source):
        return copy_to(
            mq_in.at[source], mq.at[z, :, half * 2 + c], mq_send.at[source], mq_recv.at[me], to_batch, source
        )

    def dkv_copy(source):
        return copy_to(
            own.at[source], dkv.at[z, half, c], dkv_send.at[source], dkv_recv.at[me], to_batch, source
        )

    @pl.loop(0, SEQ)
    def _(i):
        source = lax.rem(i + s, SEQ)

        @pl.when(is_here(source))
        def _():
            pltpu.make_async_copy(mq_in.at[source], mq.at[z, :, half * 2 + c], mq_recv.at[me]).start()

        @pl.when(jnp.logical_not(is_here(source)))
        def _():
            mq_copy(source).start()

    @pl.loop(0, 4)
    def _(k):
        g = group_order(k)
        own_copy(g).wait()
        arrived(part.at[pl.ds(g * 4, 4)], part_recv.at[g])

        @pl.loop(0, 4)
        def _(i):
            source = g * 4 + lax.rem(i + y, 4)
            own[source] = (own[source].astype(F32) + part[source].astype(F32)).astype(BF16)

            @pl.when(is_here(source))
            def _():
                pltpu.make_async_copy(own.at[source], dkv.at[z, half, c], dkv_recv.at[me]).start()

            @pl.when(jnp.logical_not(is_here(source)))
            def _():
                dkv_copy(source).start()

    tokens = tokens_in[...].astype(F32)
    normal, inverse = normalize(tokens)
    normed = (normal * gain_in[...]).astype(BF16)
    for k in range(4):
        cols = slice(k * WIDTH, (k + 1) * WIDTH)
        pre[:, cols] = dot_nn(normed, w_in[:, cols])
    gate = silu(pre[:, 0:WIDTH]).astype(BF16).astype(F32)
    d_gated = dot_nt(cot[...], w_out[...]).astype(BF16).astype(F32)
    onehot = slot_onehot(event_slot[...])
    item_pre = dot_nn(feats[...], item_weight[...])
    item_slope = silu_slope(item_pre)

    @pl.loop(0, SEQ)
    def _(w):
        arrived(mq.at[w % 4, :, ((w // 4) % 2) * 2 + w // 8], mq_recv.at[w])

    mixed = jnp.concatenate([mq[h, :, :, :, 0:HEAD].reshape(ROWS, HEAD) for h in range(HEADS)], axis=1)
    normed_mid = normalize(mixed.astype(F32))[0] * gain_mid[...]
    gated = (normed_mid * gate).astype(BF16)
    layer_out[...] = (tokens + dot_nn(gated, w_out[...])).astype(BF16)
    d_pre[...] = (d_gated * normed_mid * silu_slope(pre[:, 0:WIDTH])).astype(BF16)
    d_normed = dot_nt(d_pre[...], w_in[:, 0:WIDTH])
    d_query = jnp.concatenate(
        [mq[h, :, :, :, HEAD : 2 * HEAD].reshape(ROWS, HEAD) for h in range(HEADS)], axis=1
    )
    d_pre[...] = (d_query.astype(F32) * silu_slope(pre[:, 1024:1536])).astype(BF16)
    d_normed += dot_nt(d_pre[...], w_in[:, 1024:1536])

    @pl.loop(0, SEQ)
    def _(w):
        arrived(dkv.at[w % 4, (w // 4) % 2, w // 8], dkv_recv.at[w])

    for lanes, first_column in ((0, 1536), (HEAD, 512)):
        grad = jnp.concatenate(
            [
                dkv[h, 0, :, :, lanes : lanes + HEAD].reshape(ROWS, HEAD).astype(F32)
                + dkv[h, 1, :, :, lanes : lanes + HEAD].reshape(ROWS, HEAD).astype(F32)
                for h in range(HEADS)
            ],
            axis=1,
        )
        d_pre[...] = (grad * silu_slope(pre[:, first_column : first_column + WIDTH])).astype(BF16)
        d_normed += dot_nt(d_pre[...], w_in[:, first_column : first_column + WIDTH])

    scaled = d_normed * gain_in[...]
    d_tokens = cot[...].astype(F32) + inverse * (
        scaled
        - jnp.mean(scaled, axis=-1, keepdims=True)
        - normal * jnp.mean(scaled * normal, axis=-1, keepdims=True)
    )
    out2[...] = dot_nn(onehot, d_tokens.astype(BF16)).astype(BF16)
    wait_all(exchange_seq(out2, in2, send2, recv2, b, s))
    out1[...] = dot_nn(by_batch(), in2[...]).astype(BF16)
    last = exchange_batch(out1, in1, send1, recv1, b, s)
    wanted = (iota((256, 256), 0) == send_rows[...]).astype(BF16)
    wait_all(last)
    d_embedded = dot_nn(wanted, in1[...])
    d_item = (d_embedded * item_slope).astype(BF16)
    item_grad[...] = dot_nt(d_item, item_weight[...])

    @pl.loop(0, 4)
    def _(g):
        part_copy(g).wait_send()

    @pl.loop(0, SEQ)
    def _(source):
        @pl.when(jnp.logical_not(is_here(source)))
        def _():
            mq_copy(source).wait_send()
            dkv_copy(source).wait_send()


def spec(space):
    return pl.BlockSpec(memory_space=space)


VMEM, SMEM, ANY = pltpu.VMEM, pltpu.SMEM, pl.ANY
DMA = pltpu.SemaphoreType.DMA


def shape(dims, dtype):
    return jax.ShapeDtypeStruct(dims, dtype)


def params(remote):
    return pltpu.CompilerParams(vmem_limit_bytes=56 << 20, has_side_effects=remote)


def per_device(
    item_feats, item_weight, send_rows, event_slot, user_blocks, tail_len, block_order, gain_in, gain_mid, w_in, w_out,
    cot_out,
):
    event_slot = event_slot.reshape(1, ROWS)
    gain_in, gain_mid = gain_in.reshape(1, WIDTH), gain_mid.reshape(1, WIDTH)
    kv, qp, tokens, meta = pl.pallas_call(
        send_kernel,
        out_shape=(
            shape((SEQ, 2, HALF, 2 * HEAD), BF16),
            shape((SEQ, 3, PIECE, 2 * HEAD), BF16),
            shape((ROWS, WIDTH), BF16),
            shape((8, 128), jnp.int32),
        ),
        in_specs=[spec(VMEM)] * 12,
        out_specs=(spec(ANY), spec(ANY), spec(VMEM), spec(VMEM)),
        scratch_shapes=[VMEM((256, WIDTH), BF16)] * 4
        + [
            VMEM((HEADS, 2, HALF, 2 * HEAD), BF16),
            VMEM((HEADS, 3, 4, PIECE, 2 * HEAD), BF16),
            VMEM((8, 128), jnp.int32),
            VMEM((8, 128), jnp.int32),
            DMA((GROUPS,)),
            DMA((GROUPS,)),
            DMA((SEQ,)),
            DMA((SEQ,)),
        ]
        + [DMA((SEQ,))] * 6
        + [DMA, DMA],
        compiler_params=params(True),
        name="send",
    )(
        item_feats, item_weight, send_rows, event_slot, user_blocks, tail_len, block_order, gain_in, gain_mid, w_in,
        w_out, cot_out,
    )
    kv = kv.reshape(BLOCKS, BLOCK, 2 * HEAD)
    qp = qp.reshape(BLOCKS, PIECE, 2 * HEAD)
    tables = [SMEM((BLOCKS,), jnp.int32)] * 3
    held = [VMEM((BLOCKS, BLOCK, 2 * HEAD), BF16), VMEM((BLOCKS, PIECE, 2 * HEAD), BF16)]
    mixed, stats = pl.pallas_call(
        forward_kernel,
        out_shape=(shape((TILES, BLOCK, HEAD), F32), shape((TILES, 8, BLOCK), F32)),
        in_specs=[spec(SMEM), spec(ANY), spec(ANY)],
        out_specs=(spec(VMEM), spec(VMEM)),
        scratch_shapes=held + tables + [DMA((TILES,))] * 2,
        compiler_params=params(False),
        name="forward",
    )(meta, kv, qp)
    stats = pl.pallas_call(
        stats_kernel,
        out_shape=shape((HEADS, TILES, 8, BLOCK), F32),
        in_specs=[spec(VMEM)],
        out_specs=spec(VMEM),
        scratch_shapes=[VMEM((HEADS, TILES, 8, BLOCK), F32), DMA((HEADS,)), DMA((HEADS,))],
        compiler_params=params(True),
        name="stats",
    )(stats)
    mq, dkv = pl.pallas_call(
        backward_kernel,
        out_shape=(shape((BLOCKS, PIECE, 2 * HEAD), BF16), shape((BLOCKS, BLOCK, 2 * HEAD), BF16)),
        in_specs=[spec(SMEM), spec(ANY), spec(ANY), spec(VMEM), spec(VMEM)],
        out_specs=(spec(ANY), spec(ANY)),
        scratch_shapes=held
        + [
            VMEM((BLOCKS, PIECE, 2 * HEAD), BF16),
            VMEM((BLOCKS * BLOCK, 2 * HEAD), F32),
            VMEM((BLOCKS, BLOCK, 2 * HEAD), BF16),
        ]
        + tables
        + [DMA((TILES,))] * 2
        + [DMA((BLOCKS,))] * 2,
        compiler_params=params(False),
        name="backward",
    )(meta, kv, qp, mixed, stats)
    mq = mq.reshape(SEQ, 3, PIECE, 2 * HEAD)
    dkv = dkv.reshape(SEQ, 2, HALF, 2 * HEAD)
    return pl.pallas_call(
        return_kernel,
        out_shape=(shape((ROWS, WIDTH), BF16), shape((256, WIDTH), F32)),
        in_specs=[spec(VMEM)] * 10 + [spec(ANY)] * 2,
        out_specs=(spec(VMEM), spec(VMEM)),
        scratch_shapes=[
            VMEM((HEADS, 3, 4, PIECE, 2 * HEAD), BF16),
            VMEM((HEADS, 2, 2, HALF, 2 * HEAD), BF16),
            VMEM((SEQ, HALF, 2 * HEAD), BF16),
            VMEM((SEQ, HALF, 2 * HEAD), BF16),
            VMEM((ROWS, 4 * WIDTH), F32),
            VMEM((ROWS, WIDTH), BF16),
        ]
        + [VMEM((256, WIDTH), BF16)] * 4
        + [DMA((4,))] * 3
        + [DMA((SEQ,))] * 6
        + [DMA((GROUPS,))] * 2,
        compiler_params=params(True),
        name="give_back",
    )(
        item_feats, item_weight, send_rows, event_slot, gain_in, gain_mid, w_in, w_out, cot_out, tokens, mq, dkv,
    )


def solution(mesh):
    rows = P(("batch", "seq"), None)
    return jax.shard_map(
        per_device,
        mesh=mesh,
        in_specs=(
            rows,
            P(),
            rows,
            P(("batch", "seq")),
            P("batch", None),
            P("batch", None),
            P("batch", None),
            P(),
            P(),
            P(),
            P(),
            rows,
        ),
        out_specs=(rows, rows),
        check_vma=False,
    )
```

time: 411 us -> 196 us (0.48); the launches traced: 404 us -> 196 us
  waiting for transfers between devices: 195 us -> 0 us
  Pallas kernels: 0 us -> 190 us
  matrix products: 149 us -> 0 us
  starting transfers between devices: 19.1 us -> 0 us
  between operations: 14.7 us -> 0.67 us
  other arithmetic: 11.8 us -> 0 us
  local copies, waits for them, and re-layouts: 13.9 us -> 4.88 us
    pallas_call x0 -> x5, Pallas kernels: none -> 190 us  [the longest x1 64.6 us: per_device(): pl.pallas_call(return_kernel, out_shape=(shape((ROWS, WIDTH), BF16), shap...]
    dot_general x30 -> x0, matrix products: 149 us -> none  [the longest x4 38.9 us: attend(): jnp.dot(query[:, cols], key[:, cols].T, preferred_element_type=jnp.float32)]
    reduce_scatter x1 -> x0, waiting for transfers between devices: 94.2 us -> none  [per_device(): lax.psum_scatter(jnp.concatenate([key_part, value_part], axis=1).astype(j...]
    all_gather x2 -> x0, waiting for transfers between devices: 80.5 us -> none  [the longest x1 56 us: per_device(): lax.all_gather(key, 'seq', axis=0, tiled=True)]
    all_to_all x2 -> x0, waiting for transfers between devices: 19.9 us -> none  [the longest x1 11.2 us: per_device(): lax.all_to_all(outgoing, ('batch', 'seq'), split_axis=0, concat_axis=0, t...]
    all_to_all x2 -> x0, starting transfers between devices: 19 us -> none  [the longest x1 11.5 us: per_device(): lax.all_to_all(outgoing, ('batch', 'seq'), split_axis=0, concat_axis=0, t...]
    scatter-add x2 -> x0, other arithmetic: 6.31 us -> none  [the longest x1 3.96 us: per_device(): slot_grads = jax.ops.segment_sum(d_tokens, event_slot, num_segments=slots)]
  transfers between devices with their start and end apart: 5 -> 0, of which waited for: 5 -> 0; matrix products, arithmetic and copies ran while one was open for 10% -> 0% of each run, Pallas kernels for 0% -> 0%
where the time goes in v1:
time: 196 us
  Pallas kernels  190 us (97%)
  local copies, waits for them, and re-layouts  4.88 us (2%)
    pallas_call x1, Pallas kernels, per_device(): pl.pallas_call(return_kernel, out_shape=(shape((ROWS, WIDTH), BF16), shap...  64.6 us
    pallas_call x1, Pallas kernels, per_device(): pl.pallas_call(send_kernel, out_shape=(shape((SEQ, 2, HALF, 2 * HEAD), BF...  60.4 us
    pallas_call x1, Pallas kernels, per_device(): pl.pallas_call(backward_kernel, out_shape=(shape((BLOCKS, PIECE, 2 * HEAD...  29 us
    pallas_call x1, Pallas kernels, per_device(): pl.pallas_call(forward_kernel, out_shape=(shape((TILES, BLOCK, HEAD), F32...  21.6 us
    pallas_call x1, Pallas kernels, per_device(): pl.pallas_call(stats_kernel, out_shape=shape((HEADS, TILES, 8, BLOCK), F3...  14.8 us

profile of v1, /device:TPU:1, one launch (start us, length us, event | category | flops | bytes accessed | tf_op | source)
XLA Modules:
  0.0 195.9 jit_solution(15628837103445420214)
XLA Ops:
  0.6 1.2 reshape.25.event_slot
  1.9 60.4 %send.1 = (bf16[16,2,192,256]{3,2,1,0:T(8,128)(2,1)}, bf16[16,3,32,256]{3,2,1,0:T(8,128)(2,1)}, bf16[384,512]{1,0:T(8,128)(2,1)}, s32[8,128]{1,0:T(8,128)}) custom-call(bf16[256,512]{1,0:T(8,128)(2,1)} %feats.3, bf16[512,512]{1,0:T(8,128)(2,1)} %item_weight.3, s32[1,256]{1,0:T(1,128)} %send_rows.3, s32[1,384]{1,0:T(1,128)} %reshape.25.event_slot, ...), custom_call_target="tpu_custom_call" | custom-call | tf_op jit(solution)/shard_map/send/pallas_call | solution.py:594
  62.3 21.6 %forward.1 = (f32[12,128,128]{2,1,0:T(8,128)}, f32[12,8,128]{2,1,0:T(8,128)}) custom-call(s32[8,128]{1,0:T(8,128)} %get-tuple-element.11.meta, bf16[48,128,256]{2,1,0:T(8,128)(2,1)} %bitcast.6, bf16[48,32,256]{2,1,0:T(8,128)(2,1)} %bitcast.9), custom_call_target="tpu_custom_call" | custom-call | tf_op jit(solution)/shard_map/forward/pallas_call | solution.py:627
  83.9 14.8 %stats.1.stats_in = f32[4,12,8,128]{3,2,1,0:T(8,128)} custom-call(f32[12,8,128]{2,1,0:T(8,128)} %get-tuple-element.15.stats), custom_call_target="tpu_custom_call" | custom-call | tf_op jit(solution)/shard_map/stats/pallas_call | solution.py:636
  98.7 29.0 %backward.1 = (bf16[48,32,256]{2,1,0:T(8,128)(2,1)}, bf16[48,128,256]{2,1,0:T(8,128)(2,1)}) custom-call(s32[8,128]{1,0:T(8,128)} %get-tuple-element.11.meta, bf16[48,128,256]{2,1,0:T(8,128)(2,1)} %bitcast.7, bf16[48,32,256]{2,1,0:T(8,128)(2,1)} %bitcast.10, f32[12,128,128]{2,1,0:T(8,128)} %get-tuple-element.14.mixed_in, f32[4,12,8,128]{3,2,1,0:T(8,128)} %stats.1.stats_in), custom_call_target="tpu_custom_call" | custom-call | tf_op jit(solution)/shard_map/backward/pallas_call | solution.py:645
  127.7 64.6 %give_back.1 = (bf16[384,512]{1,0:T(8,128)(2,1)}, f32[256,512]{1,0:T(8,128)}) custom-call(bf16[256,512]{1,0:T(8,128)(2,1)} %feats.3, bf16[512,512]{1,0:T(8,128)(2,1)} %item_weight.3, s32[1,256]{1,0:T(1,128)} %send_rows.3, s32[1,384]{1,0:T(1,128)} %reshape.25.event_slot, f32[1,512]{1,0:T(1,128)} %bitcast.13, f32[1,512]{1,0:T(1,128)} %bitcast.15, ...), custom_call_target="tpu_custom_call" | custom-call | tf_op jit(solution)/shard_map/give_back/pallas_call | solution.py:664
  192.3 1.8 copy.16
  194.0 1.9 copy.17

commit v2 on v1

--- a/solution.py
+++ b/solution.py
@@ -17,6 +17,8 @@
 HALF = 192
 ROWS = 384
 FAR = 1 << 20
+AT_ONCE = 4
+BACK_AT_ONCE = 4
 SCALE = HEAD**-0.5
 MESH = pl.DeviceIdType.MESH
 F32 = jnp.float32
@@ -121,6 +123,26 @@
     return copies
 
 
+def signal(barrier, batch, seq):
+    pl.semaphore_signal(barrier, inc=1, device_id=(batch, seq), device_id_type=MESH)
+
+
+def greet(b, s, partner):
+    barrier = pltpu.get_barrier_semaphore()
+    for k in range(1, GROUPS):
+        signal(barrier, lax.rem(b + k, GROUPS), s)
+
+    @pl.loop(1, SEQ)
+    def _(k):
+        peer = lax.rem(s + k, SEQ)
+        signal(barrier, b, peer)
+        signal(barrier, partner, peer)
+
+
+def greeted():
+    pl.semaphore_wait(pltpu.get_barrier_semaphore(), GROUPS - 1 + 2 * (SEQ - 1))
+
+
 def wait_all(copies):
     for copy in copies:
         copy.wait()
@@ -135,10 +157,12 @@
     b, s, x, c, y, z = place()
     partner = x * 2 + 1 - c
     mine = y // 2
+    greet(b, s, partner)
 
     embedded = silu(dot_nn(feats[...], item_weight[...])).astype(BF16)
     wanted = (iota((256, 256), 0) == send_rows[...]).astype(BF16)
     out1[...] = dot_tn(wanted, embedded).astype(BF16)
+    greeted()
     first = exchange_batch(out1, in1, send1, recv1, b, s)
 
     meta_own[...] = jnp.zeros_like(meta_own)
@@ -212,10 +236,8 @@
     each_worker(start_qp)
 
     meta_copy.wait()
-    row, lane = iota((8, 128), 0), iota((8, 128), 1)
     own = (jnp.zeros((8, 128), jnp.int32) + (mine == c).astype(jnp.int32)) == 1
-    meta = jnp.where(own, meta_own[...], meta_other[...])
-    meta_out[...] = jnp.where(row == 3, (y % 2) * 2 + c, meta)
+    meta_out[...] = tables_of(jnp.where(own, meta_own[...], meta_other[...]), (y % 2) * 2 + c)
 
     def pass_on(source):
         return copy_to(
@@ -243,82 +265,96 @@
         arrived(qp_out.at[source], qp_recv.at[source])
 
 
-def read_meta(meta, slot_of, start_of, limit_of):
-    @pl.loop(0, BLOCKS)
-    def _(i):
-        slot_of[meta[0, i]] = i
-
-    first = jnp.int32(0)
+def tables_of(meta, quarter):
+    slot, lane = iota((128, 128), 0), iota((1, 128), 1)
+    held = jnp.transpose(jnp.broadcast_to(meta[0:1, :].astype(F32), (128, 128)))
+    slot_of = jnp.where((held == iota((128, 128), 1).astype(F32)) & (slot < BLOCKS), slot.astype(F32), 0.0)
+    slot_of = jnp.sum(slot_of, axis=0, keepdims=True).astype(jnp.int32)
+    first = jnp.zeros((1, 1), jnp.int32)
+    start_of = jnp.zeros((1, 128), jnp.int32)
+    limit_of = jnp.full((1, 128), BLOCK, jnp.int32)
     for u in range(4):
-        count = meta[1, u]
-
-        @pl.loop(first, first + count)
-        def _(n, first=first, count=count, u=u):
-            start_of[n] = first
-            limit_of[n] = jnp.where(n == first + count - 1, meta[2, u], BLOCK)
-
-        first = first + count
-
-
-def fetch(slot_of, kv_hbm, qp_hbm, kv, qp, kv_sem, qp_sem):
-    @pl.loop(0, TILES)
-    def _(t):
-        for i in range(4):
-            n = t * 4 + i
-            slot = slot_of[n]
-            pltpu.make_async_copy(qp_hbm.at[slot], qp.at[n], qp_sem.at[t]).start()
-            pltpu.make_async_copy(kv_hbm.at[slot], kv.at[n], kv_sem.at[t]).start()
-
-
-def wait_tile(t, kv, qp, kv_sem, qp_sem):
-    four = pl.ds(t * 4, 4)
-    arrived(qp.at[four], qp_sem.at[t])
-    arrived(kv.at[four], kv_sem.at[t])
+        start_of = jnp.where(lane >= first, first, start_of)
+        first = first + meta[1:2, u : u + 1]
+        limit_of = jnp.where(lane == first - 1, meta[2:3, u : u + 1], limit_of)
+    start_of = jnp.where(lane < BLOCKS, start_of, FAR)
+    row = iota((8, 128), 0)
+    return pick4(row, [slot_of, start_of, limit_of, jnp.zeros((1, 128), jnp.int32) + quarter])
 
 
 def pick4(index, values):
     return jnp.where(index == 0, values[0], jnp.where(index == 1, values[1], jnp.where(index == 2, values[2], values[3])))
 
 
-def forward_kernel(
-    meta, kv_hbm, qp_hbm, mixed_out, stats_out, kv, qp, slot_of, start_of, limit_of, kv_sem, qp_sem
-):
-    read_meta(meta, slot_of, start_of, limit_of)
-    fetch(slot_of, kv_hbm, qp_hbm, kv, qp, kv_sem, qp_sem)
-    quarter = meta[3, 0]
-
-    @pl.loop(0, TILES)
+def first_chunk(meta, t):
+    return jnp.minimum(meta[1, 4 * t] // 4, TILES - 1)
+
+
+def walk(meta, t, j, count):
+    pairs = []
+    for _ in range(count):
+        pairs.append((t, j))
+        more = j < jnp.minimum(t, TILES - 1)
+        after = jnp.minimum(t + 1, TILES)
+        j = jnp.where(more, j + 1, first_chunk(meta, after))
+        t = jnp.where(more, t, after)
+    return pairs, t, j
+
+
+def pairs_in_all(meta):
+    return sum(t + 1 - meta[1, 4 * t] // 4 for t in range(TILES))
+
+
+def four(ref, meta, n):
+    return jnp.concatenate([ref[meta[0, 4 * n + i]] for i in range(4)], axis=0)
+
+
+def query_bounds(meta, t, r):
+    at = (t * 4 + (r >> 5)) * BLOCK + meta[3, 0] * PIECE + (r & 31)
+    return at, pick4(r >> 5, [meta[1, t * 4 + i] for i in range(4)]) * BLOCK
+
+
+def key_places(meta, j, dim):
+    size = (1, BLOCK) if dim else (BLOCK, 1)
+    e = iota(size, dim)
+    return jnp.concatenate(
+        [jnp.where(e < meta[2, j * 4 + i], (j * 4 + i) * BLOCK + e, FAR) for i in range(4)], axis=dim
+    )
+
+
+def forward_kernel(meta, kv, qp, mixed_out, stats_out, total):
+    @pl.loop(0, TILES + 1)
     def _(t):
-        wait_tile(t, kv, qp, kv_sem, qp_sem)
-        both = qp[pl.ds(t * 4, 4)].reshape(BLOCK, 2 * HEAD)
-        query, upstream = both[:, :HEAD], both[:, HEAD:].astype(F32)
-        r = iota((BLOCK, 1), 0)
-        at = (t * 4 + (r >> 5)) * BLOCK + quarter * PIECE + (r & 31)
-        since = pick4(r >> 5, [start_of[t * 4 + i] for i in range(4)]) * BLOCK
-
-        def chunk(j, total):
-            both = kv[pl.ds(j * 4, 4)].reshape(4 * BLOCK, 2 * HEAD)
-            key, value = both[:, :HEAD], both[:, HEAD:]
-            u = dot_nt(query, key) * (0.5 * SCALE)
-            weights = u + u * jnp.tanh(u)
-            lane = iota((1, BLOCK), 1)
-            where = jnp.concatenate(
-                [
-                    jnp.where(lane < limit_of[j * 4 + i], (j * 4 + i) * BLOCK + lane, FAR)
-                    for i in range(4)
-                ],
-                axis=1,
-            )
-            weights = jnp.where((where <= at) & (where >= since), weights, 0.0).astype(BF16)
-            return total + dot_nn(weights, value)
-
-        mixed = lax.fori_loop(start_of[t * 4] // 4, t + 1, chunk, jnp.zeros((BLOCK, HEAD), F32))
+        total[t] = jnp.zeros((BLOCK, HEAD), F32)
+
+    def step(_, state):
+        pairs, t, j = walk(meta, *state, AT_ONCE)
+        keyvals = [four(kv, meta, j) for _, j in pairs]
+        us = [
+            dot_nt(four(qp, meta, t)[:, :HEAD], keyval[:, :HEAD]) * (0.5 * SCALE)
+            for (t, _), keyval in zip(pairs, keyvals)
+        ]
+        weights = []
+        for (t_, j_), u in zip(pairs, us):
+            at, since = query_bounds(meta, t_, iota((BLOCK, 1), 0))
+            where = key_places(meta, j_, 1)
+            w = u + u * jnp.tanh(u)
+            weights.append(jnp.where((where <= at) & (where >= since), w, 0.0).astype(BF16))
+        for (t_, _), w, keyval in zip(pairs, weights, keyvals):
+            total[t_] += dot_nn(w, keyval[:, HEAD:])
+        return t, j
+
+    lax.fori_loop(0, (pairs_in_all(meta) + AT_ONCE - 1) // AT_ONCE, step, (jnp.int32(0), jnp.int32(0)))
+
+    @pl.loop(0, TILES, unroll=4)
+    def _(t):
+        mixed = total[t]
+        upstream = four(qp, meta, t)[:, HEAD:].astype(F32)
         mixed_out[t] = mixed
         mean = jnp.mean(mixed, axis=1, keepdims=True)
         centred = mixed - mean
-        lane = iota((BLOCK, HEAD), 1)
         stats = pick4(
-            lane,
+            iota((BLOCK, HEAD), 1),
             [
                 mean,
                 jnp.sum(centred * centred, axis=1, keepdims=True),
@@ -331,6 +367,10 @@
 
 def stats_kernel(stats, all_stats, held, send, recv):
     b, s, x, c, y, z = place()
+    barrier = pltpu.get_barrier_semaphore()
+    for k in range(1, HEADS):
+        signal(barrier, b, y * 4 + lax.rem(z + k, HEADS))
+    pl.semaphore_wait(barrier, HEADS - 1)
     copies = []
     for k in range(1, HEADS):
         peer = lax.rem(z + k, HEADS)
@@ -342,85 +382,68 @@
     all_stats[...] = held[...]
 
 
-def backward_kernel(
-    meta, kv_hbm, qp_hbm, mixed_in, stats_in, mq_hbm, dkv_hbm,
-    kv, qp, mq, dkv, dkv_out, slot_of, start_of, limit_of, kv_sem, qp_sem, mq_sem, dkv_sem,
-):
-    read_meta(meta, slot_of, start_of, limit_of)
-    fetch(slot_of, kv_hbm, qp_hbm, kv, qp, kv_sem, qp_sem)
-    quarter = meta[3, 0]
-
+def backward_kernel(meta, kv, qp, mixed_in, stats_in, mq_out, dkv_out, d_mixed, d_query, dkv):
     @pl.loop(0, TILES)
     def _(t):
         dkv[pl.ds(t * 4 * BLOCK, 4 * BLOCK), :] = jnp.zeros((4 * BLOCK, 2 * HEAD), F32)
 
-    @pl.loop(0, TILES)
+    d_mixed[TILES] = jnp.zeros((BLOCK, HEAD), BF16)
+
+    @pl.loop(0, TILES, unroll=4)
     def _(t):
-        wait_tile(t, kv, qp, kv_sem, qp_sem)
-        both = qp[pl.ds(t * 4, 4)].reshape(BLOCK, 2 * HEAD)
-        query, upstream = both[:, :HEAD], both[:, HEAD:].astype(F32)
+        d_query[t] = jnp.zeros((BLOCK, HEAD), F32)
         mixed = mixed_in[t]
-
+        upstream = four(qp, meta, t)[:, HEAD:].astype(F32)
         stats = [stats_in[h, t] for h in range(HEADS)]
         mean = sum(v[0:1] for v in stats) * 0.25
         spread = sum(v[1:2] + HEAD * (v[0:1] - mean) * (v[0:1] - mean) for v in stats) * (1.0 / WIDTH)
         inverse = lax.rsqrt(spread + 1e-05)
         slant = sum(v[2:3] for v in stats) * (1.0 / WIDTH)
         along = sum(v[3:4] + v[2:3] * (v[0:1] - mean) for v in stats) * (1.0 / WIDTH) * inverse
-        r8 = iota((BLOCK, HEAD), 0)
-        columns = jnp.transpose(pick4(r8, [mean, inverse, slant, along]))
+        columns = jnp.transpose(pick4(iota((BLOCK, HEAD), 0), [mean, inverse, slant, along]))
         mean, inverse, slant, along = (columns[:, i : i + 1] for i in range(4))
         normal = (mixed - mean) * inverse
-        d_mixed = (inverse * (upstream - slant - normal * along)).astype(BF16)
-
-        r = iota((1, BLOCK), 1)
-        at = (t * 4 + (r >> 5)) * BLOCK + quarter * PIECE + (r & 31)
-        since = pick4(r >> 5, [start_of[t * 4 + i] for i in range(4)]) * BLOCK
-
-        def chunk(j, total):
-            both = kv[pl.ds(j * 4, 4)].reshape(4 * BLOCK, 2 * HEAD)
-            key, value = both[:, :HEAD], both[:, HEAD:]
-            u = dot_nt(key, query) * (0.5 * SCALE)
+        d_mixed[t] = (inverse * (upstream - slant - normal * along)).astype(BF16)
+
+    def step(_, state):
+        pairs, t, j = walk(meta, *state, BACK_AT_ONCE)
+        keyvals = [four(kv, meta, j) for _, j in pairs]
+        queries = [four(qp, meta, t)[:, :HEAD] for t, _ in pairs]
+        d_mixeds = [d_mixed[t] for t, _ in pairs]
+        us = [dot_nt(keyval[:, :HEAD], query) * (0.5 * SCALE) for keyval, query in zip(keyvals, queries)]
+        d_weights = [dot_nt(keyval[:, HEAD:], dm) for keyval, dm in zip(keyvals, d_mixeds)]
+        made = []
+        for (t_, j_), u, dw in zip(pairs, us, d_weights):
             th = jnp.tanh(u)
             a = 1.0 + th
-            weights = u * a
-            slope = a + weights * (1.0 - th)
-            d_scores = dot_nt(value, d_mixed) * slope
-            row = iota((BLOCK, 1), 0)
-            where = jnp.concatenate(
-                [
-                    jnp.where(row < limit_of[j * 4 + i], (j * 4 + i) * BLOCK + row, FAR)
-                    for i in range(4)
-                ],
-                axis=0,
-            )
+            w = u * a
+            ds = dw * (a + w * (1.0 - th))
+            at, since = query_bounds(meta, t_, iota((1, BLOCK), 1))
+            where = key_places(meta, j_, 0)
             seen = (where <= at) & (where >= since)
-            weights = jnp.where(seen, weights, 0.0).astype(BF16)
-            d_scores = jnp.where(seen, d_scores, 0.0).astype(BF16)
-            keys = pl.ds(pl.multiple_of(j * 4 * BLOCK, 4 * BLOCK), 4 * BLOCK)
-            dkv[keys, 0:HEAD] += dot_nn(d_scores, query)
-            dkv[keys, HEAD : 2 * HEAD] += dot_nn(weights, d_mixed)
-            return total + dot_tn(d_scores, key)
-
-        d_query = lax.fori_loop(start_of[t * 4] // 4, t + 1, chunk, jnp.zeros((BLOCK, HEAD), F32))
-        d_query = (d_query * (0.5 * SCALE)).astype(BF16)
-        mq[pl.ds(t * 4, 4), :, 0:HEAD] = mixed.astype(BF16).reshape(4, PIECE, HEAD)
-        mq[pl.ds(t * 4, 4), :, HEAD : 2 * HEAD] = d_query.reshape(4, PIECE, HEAD)
+            made.append((jnp.where(seen, w, 0.0).astype(BF16), jnp.where(seen, ds, 0.0).astype(BF16)))
+        for (t_, j_), keyval, query, dm, (w, ds) in zip(pairs, keyvals, queries, d_mixeds, made):
+            keys = pl.ds(pl.multiple_of(j_ * 4 * BLOCK, 4 * BLOCK), 4 * BLOCK)
+            dkv[keys, 0:HEAD] += dot_nn(ds, query)
+            dkv[keys, HEAD : 2 * HEAD] += dot_nn(w, dm)
+            d_query[t_] += dot_tn(ds, keyval[:, :HEAD])
+        return t, j
+
+    lax.fori_loop(0, (pairs_in_all(meta) + BACK_AT_ONCE - 1) // BACK_AT_ONCE, step, (jnp.int32(0), jnp.int32(0)))
+
+    @pl.loop(0, TILES)
+    def _(t):
+        mixed = mixed_in[t].astype(BF16)
+        dq = (d_query[t] * (0.5 * SCALE)).astype(BF16)
         for i in range(4):
             n = t * 4 + i
-            pltpu.make_async_copy(mq.at[n], mq_hbm.at[slot_of[n]], mq_sem.at[n]).start()
-
-    @pl.loop(0, BLOCKS)
-    def _(n):
-        keys = pl.ds(pl.multiple_of(n * BLOCK, BLOCK), BLOCK)
-        dkv_out[n, :, 0:HEAD] = (dkv[keys, 0:HEAD] * (0.5 * SCALE)).astype(BF16)
-        dkv_out[n, :, HEAD : 2 * HEAD] = dkv[keys, HEAD : 2 * HEAD].astype(BF16)
-        pltpu.make_async_copy(dkv_out.at[n], dkv_hbm.at[slot_of[n]], dkv_sem.at[n]).start()
-
-    @pl.loop(0, BLOCKS)
-    def _(n):
-        pltpu.make_async_copy(mq.at[n], mq_hbm.at[slot_of[n]], mq_sem.at[n]).wait()
-        pltpu.make_async_copy(dkv_out.at[n], dkv_hbm.at[slot_of[n]], dkv_sem.at[n]).wait()
+            slot = meta[0, n]
+            rows = slice(i * PIECE, (i + 1) * PIECE)
+            mq_out[slot, :, 0:HEAD] = mixed[rows]
+            mq_out[slot, :, HEAD : 2 * HEAD] = dq[rows]
+            keys = pl.ds(pl.multiple_of(n * BLOCK, BLOCK), BLOCK)
+            dkv_out[slot, :, 0:HEAD] = (dkv[keys, 0:HEAD] * (0.5 * SCALE)).astype(BF16)
+            dkv_out[slot, :, HEAD : 2 * HEAD] = dkv[keys, HEAD : 2 * HEAD].astype(BF16)
 
 
 def return_kernel(
@@ -435,6 +458,8 @@
     half = y % 2
     to_batch = x * 2 + mine
     me = z + 4 * half + 8 * c
+    greet(b, s, partner)
+    greeted()
 
     def group_order(k):
         return lax.rem(k + z, 4)
@@ -581,8 +606,38 @@
     return jax.ShapeDtypeStruct(dims, dtype)
 
 
-def params(remote):
-    return pltpu.CompilerParams(vmem_limit_bytes=56 << 20, has_side_effects=remote)
+def params(remote=None):
+    return pltpu.CompilerParams(
+        vmem_limit_bytes=56 << 20, has_side_effects=remote is not None, collective_id=remote
+    )
+
+
+def forward_call(meta, kv, qp):
+    return pl.pallas_call(
+        forward_kernel,
+        out_shape=(shape((TILES, BLOCK, HEAD), F32), shape((TILES, 8, BLOCK), F32)),
+        in_specs=[spec(SMEM), spec(VMEM), spec(VMEM)],
+        out_specs=(spec(VMEM), spec(VMEM)),
+        scratch_shapes=[VMEM((TILES + 1, BLOCK, HEAD), F32)],
+        compiler_params=params(),
+        name="forward",
+    )(meta, kv, qp)
+
+
+def backward_call(meta, kv, qp, mixed, stats):
+    return pl.pallas_call(
+        backward_kernel,
+        out_shape=(shape((BLOCKS, PIECE, 2 * HEAD), BF16), shape((BLOCKS, BLOCK, 2 * HEAD), BF16)),
+        in_specs=[spec(SMEM), spec(VMEM), spec(VMEM), spec(VMEM), spec(VMEM)],
+        out_specs=(spec(VMEM), spec(VMEM)),
+        scratch_shapes=[
+            VMEM((TILES + 1, BLOCK, HEAD), BF16),
+            VMEM((TILES + 1, BLOCK, HEAD), F32),
+            VMEM((BLOCKS * BLOCK, 2 * HEAD), F32),
+        ],
+        compiler_params=params(),
+        name="backward",
+    )(meta, kv, qp, mixed, stats)
 
 
 def per_device(
@@ -614,7 +669,7 @@
         ]
         + [DMA((SEQ,))] * 6
         + [DMA, DMA],
-        compiler_params=params(True),
+        compiler_params=params(0),
         name="send",
     )(
         item_feats, item_weight, send_rows, event_slot, user_blocks, tail_len, block_order, gain_in, gain_mid, w_in,
@@ -622,43 +677,17 @@
     )
     kv = kv.reshape(BLOCKS, BLOCK, 2 * HEAD)
     qp = qp.reshape(BLOCKS, PIECE, 2 * HEAD)
-    tables = [SMEM((BLOCKS,), jnp.int32)] * 3
-    held = [VMEM((BLOCKS, BLOCK, 2 * HEAD), BF16), VMEM((BLOCKS, PIECE, 2 * HEAD), BF16)]
-    mixed, stats = pl.pallas_call(
-        forward_kernel,
-        out_shape=(shape((TILES, BLOCK, HEAD), F32), shape((TILES, 8, BLOCK), F32)),
-        in_specs=[spec(SMEM), spec(ANY), spec(ANY)],
-        out_specs=(spec(VMEM), spec(VMEM)),
-        scratch_shapes=held + tables + [DMA((TILES,))] * 2,
-        compiler_params=params(False),
-        name="forward",
-    )(meta, kv, qp)
+    mixed, stats = forward_call(meta, kv, qp)
     stats = pl.pallas_call(
         stats_kernel,
         out_shape=shape((HEADS, TILES, 8, BLOCK), F32),
         in_specs=[spec(VMEM)],
         out_specs=spec(VMEM),
         scratch_shapes=[VMEM((HEADS, TILES, 8, BLOCK), F32), DMA((HEADS,)), DMA((HEADS,))],
-        compiler_params=params(True),
+        compiler_params=params(1),
         name="stats",
     )(stats)
-    mq, dkv = pl.pallas_call(
-        backward_kernel,
-        out_shape=(shape((BLOCKS, PIECE, 2 * HEAD), BF16), shape((BLOCKS, BLOCK, 2 * HEAD), BF16)),
-        in_specs=[spec(SMEM), spec(ANY), spec(ANY), spec(VMEM), spec(VMEM)],
-        out_specs=(spec(ANY), spec(ANY)),
-        scratch_shapes=held
-        + [
-            VMEM((BLOCKS, PIECE, 2 * HEAD), BF16),
-            VMEM((BLOCKS * BLOCK, 2 * HEAD), F32),
-            VMEM((BLOCKS, BLOCK, 2 * HEAD), BF16),
-        ]
-        + tables
-        + [DMA((TILES,))] * 2
-        + [DMA((BLOCKS,))] * 2,
-        compiler_params=params(False),
-        name="backward",
-    )(meta, kv, qp, mixed, stats)
+    mq, dkv = backward_call(meta, kv, qp, mixed, stats)
     mq = mq.reshape(SEQ, 3, PIECE, 2 * HEAD)
     dkv = dkv.reshape(SEQ, 2, HALF, 2 * HEAD)
     return pl.pallas_call(
@@ -678,7 +707,7 @@
         + [DMA((4,))] * 3
         + [DMA((SEQ,))] * 6
         + [DMA((GROUPS,))] * 2,
-        compiler_params=params(True),
+        compiler_params=params(2),
         name="give_back",
     )(
         item_feats, item_weight, send_rows, event_slot, gain_in, gain_mid, w_in, w_out, cot_out, tokens, mq, dkv,

time: 196 us -> 159 us (0.81)
  Pallas kernels: 190 us -> 152 us
    pallas_call x2, Pallas kernels: 50.6 us -> 28.9 us  [the longest x1 17.6 us: backward_call(): pl.pallas_call(backward_kernel, out_shape=(shape((BLOCKS, PIECE, 2 * HEAD...]
    pallas_call x1, Pallas kernels: 14.8 us -> 8.41 us  [per_device(): pl.pallas_call(stats_kernel, out_shape=shape((HEADS, TILES, 8, BLOCK), F3...]
    pallas_call x1, Pallas kernels: 60.4 us -> 54.6 us  [per_device(): pl.pallas_call(send_kernel, out_shape=(shape((SEQ, 2, HALF, 2 * HEAD), BF...]
    pallas_call x1, Pallas kernels: 64.6 us -> 60.1 us  [per_device(): pl.pallas_call(return_kernel, out_shape=(shape((ROWS, WIDTH), BF16), shap...]
where the time goes in v2:
time: 159 us; the launch traced here: 158 us
  Pallas kernels  152 us (96%)
  local copies, waits for them, and re-layouts  4.88 us (3%)
    pallas_call x1, Pallas kernels, per_device(): pl.pallas_call(return_kernel, out_shape=(shape((ROWS, WIDTH), BF16), shap...  60.1 us
    pallas_call x1, Pallas kernels, per_device(): pl.pallas_call(send_kernel, out_shape=(shape((SEQ, 2, HALF, 2 * HEAD), BF...  54.6 us
    pallas_call x1, Pallas kernels, backward_call(): pl.pallas_call(backward_kernel, out_shape=(shape((BLOCKS, PIECE, 2 * HEAD...  17.6 us
    pallas_call x1, Pallas kernels, forward_call(): pl.pallas_call(forward_kernel, out_shape=(shape((TILES, BLOCK, HEAD), F32...  11.3 us
    pallas_call x1, Pallas kernels, per_device(): pl.pallas_call(stats_kernel, out_shape=shape((HEADS, TILES, 8, BLOCK), F3...  8.41 us
    unnamed x2, local copies, waits for them, and re-layouts  3.63 us

profile of v2, /device:TPU:1, one launch (start us, length us, event | category | flops | bytes accessed | tf_op | source)
XLA Modules:
  0.0 157.6 jit_solution(9513144813646773507)
XLA Ops:
  0.6 1.2 reshape.25.event_slot
  1.9 54.6 %send.1 = (bf16[16,2,192,256]{3,2,1,0:T(8,128)(2,1)}, bf16[16,3,32,256]{3,2,1,0:T(8,128)(2,1)}, bf16[384,512]{1,0:T(8,128)(2,1)}, s32[8,128]{1,0:T(8,128)}) custom-call(bf16[256,512]{1,0:T(8,128)(2,1)} %feats.3, bf16[512,512]{1,0:T(8,128)(2,1)} %item_weight.3, s32[1,256]{1,0:T(1,128)} %send_rows.3, s32[1,384]{1,0:T(1,128)} %reshape.25.event_slot, ...), custom_call_target="tpu_custom_call" | custom-call | tf_op jit(solution)/shard_map/send/pallas_call | solution.py:649
  56.5 11.3 %forward.1 = (f32[12,128,128]{2,1,0:T(8,128)}, f32[12,8,128]{2,1,0:T(8,128)}) custom-call(s32[8,128]{1,0:T(8,128)} %get-tuple-element.11.meta, bf16[48,128,256]{2,1,0:T(8,128)(2,1)} %bitcast.6, bf16[48,32,256]{2,1,0:T(8,128)(2,1)} %bitcast.9), custom_call_target="tpu_custom_call" | custom-call | tf_op jit(solution)/shard_map/forward/pallas_call | solution.py:616
  67.8 8.4 %stats.1.stats_in = f32[4,12,8,128]{3,2,1,0:T(8,128)} custom-call(f32[12,8,128]{2,1,0:T(8,128)} %get-tuple-element.15.stats), custom_call_target="tpu_custom_call" | custom-call | tf_op jit(solution)/shard_map/stats/pallas_call | solution.py:681
  76.2 17.6 %backward.1 = (bf16[48,32,256]{2,1,0:T(8,128)(2,1)}, bf16[48,128,256]{2,1,0:T(8,128)(2,1)}) custom-call(s32[8,128]{1,0:T(8,128)} %get-tuple-element.11.meta, bf16[48,128,256]{2,1,0:T(8,128)(2,1)} %bitcast.7, bf16[48,32,256]{2,1,0:T(8,128)(2,1)} %bitcast.10, f32[12,128,128]{2,1,0:T(8,128)} %get-tuple-element.14.mixed_in, f32[4,12,8,128]{3,2,1,0:T(8,128)} %stats.1.stats_in), custom_call_target="tpu_custom_call" | custom-call | tf_op jit(solution)/shard_map/backward/pallas_call | solution.py:628
  93.8 60.1 %give_back.1 = (bf16[384,512]{1,0:T(8,128)(2,1)}, f32[256,512]{1,0:T(8,128)}) custom-call(bf16[256,512]{1,0:T(8,128)(2,1)} %feats.3, bf16[512,512]{1,0:T(8,128)(2,1)} %item_weight.3, s32[1,256]{1,0:T(1,128)} %send_rows.3, s32[1,384]{1,0:T(1,128)} %reshape.25.event_slot, f32[1,512]{1,0:T(1,128)} %bitcast.13, f32[1,512]{1,0:T(1,128)} %bitcast.15, ...), custom_call_target="tpu_custom_call" | custom-call | tf_op jit(solution)/shard_map/give_back/pallas_call | solution.py:693
  153.9 1.8 %copy.16 = bf16[384,512]{1,0:T(8,128)(2,1)} copy(bf16[384,512]{1,0:T(8,128)(2,1)} %get-tuple-element.20) | data formatting | bytes 786432
  155.7 1.9 %copy.17 = f32[256,512]{1,0:T(8,128)} copy(f32[256,512]{1,0:T(8,128)} %get-tuple-element.21) | data formatting | bytes 1048576

commit v3 on v2

--- a/solution.py
+++ b/solution.py
@@ -14,7 +14,8 @@
 GROUPS = 8
 PIECE = 32
 TILES = 12
-HALF = 192
+SLOTS = 256
+HALF = 128
 ROWS = 384
 FAR = 1 << 20
 AT_ONCE = 4
@@ -85,10 +86,13 @@
     return pl.ds(pl.multiple_of(index * size, size), size)
 
 
-def slot_onehot(event_slot):
+def slot_rows(event_slot):
     e = event_slot
-    wanted = ((e >> 1) & 15) * 16 + (e >> 5) * 2 + (e & 1)
-    return (iota((256, ROWS), 0) == wanted).astype(BF16)
+    return ((e >> 1) & 15) * 16 + (e >> 5) * 2 + (e & 1)
+
+
+def slot_onehot(wanted):
+    return (iota((SLOTS, wanted.shape[1]), 0) == wanted).astype(BF16)
 
 
 def by_seq():
@@ -149,45 +153,34 @@
 
 
 def send_kernel(
-    feats, item_weight, send_rows, event_slot, user_blocks, tail_len, block_order, gain_in, gain_mid, w_in, w_out, cot,
-    kv_out, qp_out, tokens_out, meta_out,
-    out1, in1, out2, in2, kv, qp, meta_own, meta_other,
-    send1, recv1, send2, recv2, kv_send, kv_recv, pass_send, pass_recv, qp_send, qp_recv, meta_send, meta_recv,
+    feats, item_weight, send_rows, event_slot, user_blocks, tail_len, block_order, gain_in, gain_mid,
+    w_in_hbm, w_out_hbm, cot_hbm,
+    kv_out, qp_out, slots_out, ids_out, meta_out,
+    w_in, w_out, cot, out1, in1, out2, in2, kv, qp, ids, ids_in,
+    load_sem, send1, recv1, send2, recv2, kv_send, kv_recv, pass_send, pass_recv, qp_send, qp_recv, ids_send, ids_recv,
 ):
     b, s, x, c, y, z = place()
     partner = x * 2 + 1 - c
-    mine = y // 2
     greet(b, s, partner)
+    loads = [
+        pltpu.make_async_copy(src, dst, load_sem.at[k])
+        for k, (src, dst) in enumerate(((w_out_hbm, w_out), (cot_hbm, cot), (w_in_hbm, w_in)))
+    ]
+    for load in loads:
+        load.start()
 
     embedded = silu(dot_nn(feats[...], item_weight[...])).astype(BF16)
     wanted = (iota((256, 256), 0) == send_rows[...]).astype(BF16)
     out1[...] = dot_tn(wanted, embedded).astype(BF16)
+    slot_of_event = slot_rows(event_slot[...].reshape(1, ROWS))
+    ids[...] = jnp.zeros_like(ids)
+    for k in range(3):
+        ids[k : k + 1, :] = slot_of_event[:, k * BLOCK : (k + 1) * BLOCK]
+    ids[3:4, 0:BLOCKS] = block_order[...]
+    ids[4:5, 0:4] = user_blocks[...]
+    ids[5:6, 0:4] = tail_len[...]
     greeted()
     first = exchange_batch(out1, in1, send1, recv1, b, s)
-
-    meta_own[...] = jnp.zeros_like(meta_own)
-    meta_own[0:1, 0:48] = block_order[...]
-    meta_own[1:2, 0:4] = user_blocks[...]
-    meta_own[2:3, 0:4] = tail_len[...]
-    meta_copy = copy_to(meta_own, meta_other, meta_send, meta_recv, partner, s)
-    meta_copy.start()
-
-    d_gated = dot_nt(cot[...], w_out[...]).astype(BF16)
-    wait_all(first)
-    out2[...] = dot_nn(by_seq(), in1[...]).astype(BF16)
-    second = exchange_seq(out2, in2, send2, recv2, b, s)
-    onehot = slot_onehot(event_slot[...])
-    wait_all(second)
-    tokens = dot_tn(onehot, in2[...])
-    tokens_out[...] = tokens.astype(BF16)
-    normed = (normalize(tokens)[0] * gain_in[...]).astype(BF16)
-
-    for part, first_column in ((0, 1536), (1, 512)):
-        lanes = slice(part * HEAD, part * HEAD + HEAD)
-        made = silu(dot_nn(normed, w_in[:, first_column : first_column + WIDTH])).astype(BF16)
-        for h in range(HEADS):
-            kv[h, 0, :, lanes] = made[:HALF, h * HEAD : (h + 1) * HEAD]
-            kv[h, 1, :, lanes] = made[HALF:, h * HEAD : (h + 1) * HEAD]
 
     def each_worker(act):
         @pl.loop(0, SEQ)
@@ -197,23 +190,57 @@
             here = (to_batch == b) & (to_seq == s)
             act(w, head, half, core, to_batch, to_seq, here)
 
+    def start(here, src, dst, recv, remote):
+        @pl.when(here)
+        def _():
+            pltpu.make_async_copy(src, dst, recv).start()
+
+        @pl.when(jnp.logical_not(here))
+        def _():
+            remote.start()
+
+    def ids_copy(w, to_batch, to_seq):
+        return copy_to(ids, ids_in.at[s], ids_send.at[w], ids_recv.at[s], to_batch, to_seq)
+
+    def start_ids(w, head, half, core, to_batch, to_seq, here):
+        start(here, ids, ids_in.at[s], ids_recv.at[s], ids_copy(w, to_batch, to_seq))
+
+    each_worker(start_ids)
+
+    loads[0].wait()
+    loads[1].wait()
+    d_gated = dot_nt(cot[...], w_out[...]).astype(BF16)
+    wait_all(first)
+    out2[...] = dot_nn(by_seq(), in1[...]).astype(BF16)
+    second = exchange_seq(out2, in2, send2, recv2, b, s)
+    onehot = slot_onehot(slot_of_event)
+    loads[2].wait()
+    wait_all(second)
+    slots_out[...] = in2[...]
+    normed = (normalize(in2[...].astype(F32))[0] * gain_in[...]).astype(BF16)
+
+    for part, first_column in ((0, 1536), (1, 512)):
+        lanes = slice(part * HEAD, part * HEAD + HEAD)
+        made = silu(dot_nn(normed, w_in[:, first_column : first_column + WIDTH])).astype(BF16)
+        for h in range(HEADS):
+            kv[h, 0, :, lanes] = made[:HALF, h * HEAD : (h + 1) * HEAD]
+            kv[h, 1, :, lanes] = made[HALF:, h * HEAD : (h + 1) * HEAD]
+
     def kv_copy(w, head, core, to_batch, to_seq):
         return copy_to(kv.at[head, core], kv_out.at[s, core], kv_send.at[w], kv_recv.at[s], to_batch, to_seq)
 
     def start_kv(w, head, half, core, to_batch, to_seq, here):
-        @pl.when(here)
-        def _():
-            pltpu.make_async_copy(kv.at[head, core], kv_out.at[s, core], kv_recv.at[s]).start()
-
-        @pl.when(jnp.logical_not(here))
-        def _():
-            kv_copy(w, head, core, to_batch, to_seq).start()
+        start(
+            here, kv.at[head, core], kv_out.at[s, core], kv_recv.at[s], kv_copy(w, head, core, to_batch, to_seq)
+        )
 
     each_worker(start_kv)
 
     query = silu(dot_nn(normed, w_in[:, 1024:1536])).astype(BF16)
+    query = dot_tn(onehot, query).astype(BF16)
     gate = silu(dot_nn(normed, w_in[:, 0:WIDTH])).astype(BF16)
-    upstream = (d_gated.astype(F32) * gate.astype(F32) * gain_mid[...]).astype(BF16)
+    gate = dot_tn(onehot, gate)
+    upstream = (d_gated.astype(F32) * gate * gain_mid[...]).astype(BF16)
     for h in range(HEADS):
         cols = slice(h * HEAD, (h + 1) * HEAD)
         qp[h, :, :, :, 0:HEAD] = query[:, cols].reshape(3, 4, PIECE, HEAD)
@@ -225,19 +252,19 @@
         )
 
     def start_qp(w, head, half, core, to_batch, to_seq, here):
-        @pl.when(here)
-        def _():
-            pltpu.make_async_copy(qp.at[head, :, half * 2 + core], qp_out.at[s], qp_recv.at[s]).start()
-
-        @pl.when(jnp.logical_not(here))
-        def _():
-            qp_copy(w, head, half, core, to_batch, to_seq).start()
+        start(
+            here, qp.at[head, :, half * 2 + core], qp_out.at[s], qp_recv.at[s],
+            qp_copy(w, head, half, core, to_batch, to_seq),
+        )
 
     each_worker(start_qp)
 
-    meta_copy.wait()
-    own = (jnp.zeros((8, 128), jnp.int32) + (mine == c).astype(jnp.int32)) == 1
-    meta_out[...] = tables_of(jnp.where(own, meta_own[...], meta_other[...]), (y % 2) * 2 + c)
+    @pl.loop(0, SEQ)
+    def _(source):
+        arrived(ids_in.at[source], ids_recv.at[source])
+
+    ids_out[...] = ids_in[...]
+    meta_out[...] = tables_of(ids_in[s], (y % 2) * 2 + c)
 
     def pass_on(source):
         return copy_to(
@@ -253,6 +280,7 @@
     def finish(w, head, half, core, to_batch, to_seq, here):
         @pl.when(jnp.logical_not(here))
         def _():
+            ids_copy(w, to_batch, to_seq).wait_send()
             kv_copy(w, head, core, to_batch, to_seq).wait_send()
             qp_copy(w, head, half, core, to_batch, to_seq).wait_send()
 
@@ -267,7 +295,7 @@
 
 def tables_of(meta, quarter):
     slot, lane = iota((128, 128), 0), iota((1, 128), 1)
-    held = jnp.transpose(jnp.broadcast_to(meta[0:1, :].astype(F32), (128, 128)))
+    held = jnp.transpose(jnp.broadcast_to(meta[3:4, :].astype(F32), (128, 128)))
     slot_of = jnp.where((held == iota((128, 128), 1).astype(F32)) & (slot < BLOCKS), slot.astype(F32), 0.0)
     slot_of = jnp.sum(slot_of, axis=0, keepdims=True).astype(jnp.int32)
     first = jnp.zeros((1, 1), jnp.int32)
@@ -275,11 +303,12 @@
     limit_of = jnp.full((1, 128), BLOCK, jnp.int32)
     for u in range(4):
         start_of = jnp.where(lane >= first, first, start_of)
-        first = first + meta[1:2, u : u + 1]
-        limit_of = jnp.where(lane == first - 1, meta[2:3, u : u + 1], limit_of)
+        first = first + meta[4:5, u : u + 1]
+        limit_of = jnp.where(lane == first - 1, meta[5:6, u : u + 1], limit_of)
     start_of = jnp.where(lane < BLOCKS, start_of, FAR)
     row = iota((8, 128), 0)
-    return pick4(row, [slot_of, start_of, limit_of, jnp.zeros((1, 128), jnp.int32) + quarter])
+    picked = pick4(row, [slot_of, start_of, limit_of, jnp.zeros((1, 128), jnp.int32) + quarter])
+    return jnp.where(row == 4, meta[3:4, :], picked)
 
 
 def pick4(index, values):
@@ -314,6 +343,10 @@
     return at, pick4(r >> 5, [meta[1, t * 4 + i] for i in range(4)]) * BLOCK
 
 
+def chunk_of(kv, j):
+    return kv[pl.ds(j * 4, 4)].reshape(4 * BLOCK, 2 * HEAD)
+
+
 def key_places(meta, j, dim):
     size = (1, BLOCK) if dim else (BLOCK, 1)
     e = iota(size, dim)
@@ -322,14 +355,25 @@
     )
 
 
-def forward_kernel(meta, kv, qp, mixed_out, stats_out, total):
+def forward_kernel(meta, ids, kv_slots, qp, kv_out, mixed_out, stats_out, kv, total, kv_sem):
+    @pl.loop(0, SEQ, unroll=4)
+    def _(s):
+        rows = jnp.concatenate([ids[s].astype(F32), jnp.zeros((120, 128), F32)], axis=0)
+        columns = jnp.transpose(rows)
+        for k in range(3):
+            onehot = (iota((BLOCK, SLOTS), 1).astype(F32) == columns[:, k : k + 1]).astype(BF16)
+            kv[meta[4, s * 3 + k]] = dot_nn(onehot, kv_slots[s]).astype(BF16)
+
+    save = pltpu.make_async_copy(kv, kv_out, kv_sem)
+    save.start()
+
     @pl.loop(0, TILES + 1)
     def _(t):
         total[t] = jnp.zeros((BLOCK, HEAD), F32)
 
     def step(_, state):
         pairs, t, j = walk(meta, *state, AT_ONCE)
-        keyvals = [four(kv, meta, j) for _, j in pairs]
+        keyvals = [chunk_of(kv, j) for _, j in pairs]
         us = [
             dot_nt(four(qp, meta, t)[:, :HEAD], keyval[:, :HEAD]) * (0.5 * SCALE)
             for (t, _), keyval in zip(pairs, keyvals)
@@ -364,6 +408,8 @@
         )
         stats_out[t] = jnp.transpose(stats)[0:8, :]
 
+    save.wait()
+
 
 def stats_kernel(stats, all_stats, held, send, recv):
     b, s, x, c, y, z = place()
@@ -382,7 +428,7 @@
     all_stats[...] = held[...]
 
 
-def backward_kernel(meta, kv, qp, mixed_in, stats_in, mq_out, dkv_out, d_mixed, d_query, dkv):
+def backward_kernel(meta, ids, kv, qp, mixed_in, stats_in, mq_out, dkv_out, d_mixed, d_query, dkv):
     @pl.loop(0, TILES)
     def _(t):
         dkv[pl.ds(t * 4 * BLOCK, 4 * BLOCK), :] = jnp.zeros((4 * BLOCK, 2 * HEAD), F32)
@@ -407,7 +453,7 @@
 
     def step(_, state):
         pairs, t, j = walk(meta, *state, BACK_AT_ONCE)
-        keyvals = [four(kv, meta, j) for _, j in pairs]
+        keyvals = [chunk_of(kv, j) for _, j in pairs]
         queries = [four(qp, meta, t)[:, :HEAD] for t, _ in pairs]
         d_mixeds = [d_mixed[t] for t, _ in pairs]
         us = [dot_nt(keyval[:, :HEAD], query) * (0.5 * SCALE) for keyval, query in zip(keyvals, queries)]
@@ -441,16 +487,23 @@
             rows = slice(i * PIECE, (i + 1) * PIECE)
             mq_out[slot, :, 0:HEAD] = mixed[rows]
             mq_out[slot, :, HEAD : 2 * HEAD] = dq[rows]
-            keys = pl.ds(pl.multiple_of(n * BLOCK, BLOCK), BLOCK)
-            dkv_out[slot, :, 0:HEAD] = (dkv[keys, 0:HEAD] * (0.5 * SCALE)).astype(BF16)
-            dkv_out[slot, :, HEAD : 2 * HEAD] = dkv[keys, HEAD : 2 * HEAD].astype(BF16)
+
+    @pl.loop(0, SEQ, unroll=4)
+    def _(s):
+        total = jnp.zeros((SLOTS, 2 * HEAD), F32)
+        for k in range(3):
+            keys = pl.ds(pl.multiple_of(meta[4, s * 3 + k] * BLOCK, BLOCK), BLOCK)
+            total += dot_nn(slot_onehot(ids[s, k : k + 1, :]), dkv[keys, :].astype(BF16))
+        dkv_out[s, :, 0:HEAD] = (total[:, 0:HEAD] * (0.5 * SCALE)).astype(BF16)
+        dkv_out[s, :, HEAD : 2 * HEAD] = total[:, HEAD : 2 * HEAD].astype(BF16)
 
 
 def return_kernel(
-    feats, item_weight, send_rows, event_slot, gain_in, gain_mid, w_in, w_out, cot, tokens_in, mq_in, dkv_in,
-    layer_out, item_grad,
-    mq, dkv, own, part, pre, d_pre, out2, in2, out1, in1,
-    own_sem, part_send, part_recv, mq_send, mq_recv, dkv_send, dkv_recv, send2, recv2, send1, recv1,
+    send_rows, event_slot, gain_in, gain_mid, slots_in,
+    feats_hbm, item_weight_hbm, w_in_hbm, w_out_hbm, cot_hbm, mq_in, dkv_in,
+    layer_out, d_item_out,
+    feats, item_weight, w_in, w_out, cot, mq, dkv, own, part, pre, d_pre, out2, in2, out1, in1,
+    load_sem, own_sem, part_send, part_recv, mq_send, mq_recv, dkv_send, dkv_recv, send2, recv2, send1, recv1,
 ):
     b, s, x, c, y, z = place()
     partner = x * 2 + 1 - c
@@ -459,6 +512,18 @@
     to_batch = x * 2 + mine
     me = z + 4 * half + 8 * c
     greet(b, s, partner)
+    loads = [
+        pltpu.make_async_copy(src, dst, load_sem.at[k])
+        for k, (src, dst) in enumerate(
+            (
+                (w_in_hbm, w_in),
+                (w_out_hbm, w_out),
+                (cot_hbm, cot),
+                (feats_hbm, feats),
+                (item_weight_hbm, item_weight),
+            )
+        )
+    ]
     greeted()
 
     def group_order(k):
@@ -522,17 +587,24 @@
             def _():
                 dkv_copy(source).start()
 
-    tokens = tokens_in[...].astype(F32)
-    normal, inverse = normalize(tokens)
+    for load in loads:
+        load.start()
+    onehot = slot_onehot(slot_rows(event_slot[...].reshape(1, ROWS)))
+    normal, inverse = normalize(slots_in[...].astype(F32))
     normed = (normal * gain_in[...]).astype(BF16)
+    loads[0].wait()
     for k in range(4):
         cols = slice(k * WIDTH, (k + 1) * WIDTH)
         pre[:, cols] = dot_nn(normed, w_in[:, cols])
-    gate = silu(pre[:, 0:WIDTH]).astype(BF16).astype(F32)
+    tokens = dot_tn(onehot, slots_in[...])
+    gate = dot_tn(onehot, silu(pre[:, 0:WIDTH]).astype(BF16))
+    loads[1].wait()
+    loads[2].wait()
     d_gated = dot_nt(cot[...], w_out[...]).astype(BF16).astype(F32)
-    onehot = slot_onehot(event_slot[...])
-    item_pre = dot_nn(feats[...], item_weight[...])
-    item_slope = silu_slope(item_pre)
+    slot_cot = dot_nn(onehot, cot[...])
+    loads[3].wait()
+    loads[4].wait()
+    item_slope = silu_slope(dot_nn(feats[...], item_weight[...]))
 
     @pl.loop(0, SEQ)
     def _(w):
@@ -542,45 +614,49 @@
     normed_mid = normalize(mixed.astype(F32))[0] * gain_mid[...]
     gated = (normed_mid * gate).astype(BF16)
     layer_out[...] = (tokens + dot_nn(gated, w_out[...])).astype(BF16)
-    d_pre[...] = (d_gated * normed_mid * silu_slope(pre[:, 0:WIDTH])).astype(BF16)
+    d_gate = dot_nn(onehot, (d_gated * normed_mid).astype(BF16))
+    d_pre[...] = (d_gate * silu_slope(pre[:, 0:WIDTH])).astype(BF16)
     d_normed = dot_nt(d_pre[...], w_in[:, 0:WIDTH])
     d_query = jnp.concatenate(
         [mq[h, :, :, :, HEAD : 2 * HEAD].reshape(ROWS, HEAD) for h in range(HEADS)], axis=1
     )
-    d_pre[...] = (d_query.astype(F32) * silu_slope(pre[:, 1024:1536])).astype(BF16)
+    d_pre[...] = (dot_nn(onehot, d_query) * silu_slope(pre[:, 1024:1536])).astype(BF16)
     d_normed += dot_nt(d_pre[...], w_in[:, 1024:1536])
+    for first_column in (512, 1536):
+        cols = slice(first_column, first_column + WIDTH)
+        pre[:, cols] = silu_slope(pre[:, cols])
 
     @pl.loop(0, SEQ)
     def _(w):
         arrived(dkv.at[w % 4, (w // 4) % 2, w // 8], dkv_recv.at[w])
 
     for lanes, first_column in ((0, 1536), (HEAD, 512)):
+        cols = slice(first_column, first_column + WIDTH)
         grad = jnp.concatenate(
             [
-                dkv[h, 0, :, :, lanes : lanes + HEAD].reshape(ROWS, HEAD).astype(F32)
-                + dkv[h, 1, :, :, lanes : lanes + HEAD].reshape(ROWS, HEAD).astype(F32)
+                dkv[h, 0, :, :, lanes : lanes + HEAD].reshape(SLOTS, HEAD).astype(F32)
+                + dkv[h, 1, :, :, lanes : lanes + HEAD].reshape(SLOTS, HEAD).astype(F32)
                 for h in range(HEADS)
             ],
             axis=1,
         )
-        d_pre[...] = (grad * silu_slope(pre[:, first_column : first_column + WIDTH])).astype(BF16)
-        d_normed += dot_nt(d_pre[...], w_in[:, first_column : first_column + WIDTH])
+        d_pre[...] = (grad * pre[:, cols]).astype(BF16)
+        d_normed += dot_nt(d_pre[...], w_in[:, cols])
 
     scaled = d_normed * gain_in[...]
-    d_tokens = cot[...].astype(F32) + inverse * (
+    d_slots = slot_cot + inverse * (
         scaled
         - jnp.mean(scaled, axis=-1, keepdims=True)
         - normal * jnp.mean(scaled * normal, axis=-1, keepdims=True)
     )
-    out2[...] = dot_nn(onehot, d_tokens.astype(BF16)).astype(BF16)
+    out2[...] = d_slots.astype(BF16)
     wait_all(exchange_seq(out2, in2, send2, recv2, b, s))
     out1[...] = dot_nn(by_batch(), in2[...]).astype(BF16)
     last = exchange_batch(out1, in1, send1, recv1, b, s)
     wanted = (iota((256, 256), 0) == send_rows[...]).astype(BF16)
     wait_all(last)
     d_embedded = dot_nn(wanted, in1[...])
-    d_item = (d_embedded * item_slope).astype(BF16)
-    item_grad[...] = dot_nt(d_item, item_weight[...])
+    d_item_out[...] = (d_embedded * item_slope).astype(BF16)
 
     @pl.loop(0, 4)
     def _(g):
@@ -594,6 +670,11 @@
             dkv_copy(source).wait_send()
 
 
+def result_kernel(layer, d_item, item_weight, layer_out, item_grad):
+    layer_out[...] = layer[...]
+    item_grad[...] = dot_nt(d_item[...], item_weight[...])
+
+
 def spec(space):
     return pl.BlockSpec(memory_space=space)
 
@@ -612,23 +693,27 @@
     )
 
 
-def forward_call(meta, kv, qp):
+def forward_call(meta, ids, kv, qp):
     return pl.pallas_call(
         forward_kernel,
-        out_shape=(shape((TILES, BLOCK, HEAD), F32), shape((TILES, 8, BLOCK), F32)),
-        in_specs=[spec(SMEM), spec(VMEM), spec(VMEM)],
-        out_specs=(spec(VMEM), spec(VMEM)),
-        scratch_shapes=[VMEM((TILES + 1, BLOCK, HEAD), F32)],
+        out_shape=(
+            shape((BLOCKS, BLOCK, 2 * HEAD), BF16),
+            shape((TILES, BLOCK, HEAD), F32),
+            shape((TILES, 8, BLOCK), F32),
+        ),
+        in_specs=[spec(SMEM), spec(VMEM), spec(VMEM), spec(VMEM)],
+        out_specs=(spec(ANY), spec(VMEM), spec(VMEM)),
+        scratch_shapes=[VMEM((BLOCKS, BLOCK, 2 * HEAD), BF16), VMEM((TILES + 1, BLOCK, HEAD), F32), DMA],
         compiler_params=params(),
         name="forward",
-    )(meta, kv, qp)
-
-
-def backward_call(meta, kv, qp, mixed, stats):
+    )(meta, ids, kv, qp)
+
+
+def backward_call(meta, ids, kv, qp, mixed, stats):
     return pl.pallas_call(
         backward_kernel,
-        out_shape=(shape((BLOCKS, PIECE, 2 * HEAD), BF16), shape((BLOCKS, BLOCK, 2 * HEAD), BF16)),
-        in_specs=[spec(SMEM), spec(VMEM), spec(VMEM), spec(VMEM), spec(VMEM)],
+        out_shape=(shape((BLOCKS, PIECE, 2 * HEAD), BF16), shape((SEQ, SLOTS, 2 * HEAD), BF16)),
+        in_specs=[spec(SMEM)] + [spec(VMEM)] * 5,
         out_specs=(spec(VMEM), spec(VMEM)),
         scratch_shapes=[
             VMEM((TILES + 1, BLOCK, HEAD), BF16),
@@ -637,47 +722,46 @@
         ],
         compiler_params=params(),
         name="backward",
-    )(meta, kv, qp, mixed, stats)
+    )(meta, ids, kv, qp, mixed, stats)
 
 
 def per_device(
     item_feats, item_weight, send_rows, event_slot, user_blocks, tail_len, block_order, gain_in, gain_mid, w_in, w_out,
     cot_out,
 ):
-    event_slot = event_slot.reshape(1, ROWS)
     gain_in, gain_mid = gain_in.reshape(1, WIDTH), gain_mid.reshape(1, WIDTH)
-    kv, qp, tokens, meta = pl.pallas_call(
+    kv, qp, slots, ids, meta = pl.pallas_call(
         send_kernel,
         out_shape=(
             shape((SEQ, 2, HALF, 2 * HEAD), BF16),
             shape((SEQ, 3, PIECE, 2 * HEAD), BF16),
-            shape((ROWS, WIDTH), BF16),
+            shape((SLOTS, WIDTH), BF16),
+            shape((SEQ, 8, 128), jnp.int32),
             shape((8, 128), jnp.int32),
         ),
-        in_specs=[spec(VMEM)] * 12,
-        out_specs=(spec(ANY), spec(ANY), spec(VMEM), spec(VMEM)),
-        scratch_shapes=[VMEM((256, WIDTH), BF16)] * 4
+        in_specs=[spec(VMEM)] * 9 + [spec(ANY)] * 3,
+        out_specs=(spec(ANY), spec(ANY), spec(VMEM), spec(VMEM), spec(VMEM)),
+        scratch_shapes=[VMEM((WIDTH, 4 * WIDTH), BF16), VMEM((WIDTH, WIDTH), BF16), VMEM((ROWS, WIDTH), BF16)]
+        + [VMEM((256, WIDTH), BF16)] * 4
         + [
             VMEM((HEADS, 2, HALF, 2 * HEAD), BF16),
             VMEM((HEADS, 3, 4, PIECE, 2 * HEAD), BF16),
             VMEM((8, 128), jnp.int32),
-            VMEM((8, 128), jnp.int32),
+            VMEM((SEQ, 8, 128), jnp.int32),
+            DMA((3,)),
             DMA((GROUPS,)),
             DMA((GROUPS,)),
-            DMA((SEQ,)),
-            DMA((SEQ,)),
         ]
-        + [DMA((SEQ,))] * 6
-        + [DMA, DMA],
+        + [DMA((SEQ,))] * 10,
         compiler_params=params(0),
         name="send",
     )(
         item_feats, item_weight, send_rows, event_slot, user_blocks, tail_len, block_order, gain_in, gain_mid, w_in,
         w_out, cot_out,
     )
-    kv = kv.reshape(BLOCKS, BLOCK, 2 * HEAD)
+    kv = kv.reshape(SEQ, SLOTS, 2 * HEAD)
     qp = qp.reshape(BLOCKS, PIECE, 2 * HEAD)
-    mixed, stats = forward_call(meta, kv, qp)
+    kv, mixed, stats = forward_call(meta, ids, kv, qp)
     stats = pl.pallas_call(
         stats_kernel,
         out_shape=shape((HEADS, TILES, 8, BLOCK), F32),
@@ -687,31 +771,45 @@
         compiler_params=params(1),
         name="stats",
     )(stats)
-    mq, dkv = backward_call(meta, kv, qp, mixed, stats)
+    mq, dkv = backward_call(meta, ids, kv, qp, mixed, stats)
     mq = mq.reshape(SEQ, 3, PIECE, 2 * HEAD)
     dkv = dkv.reshape(SEQ, 2, HALF, 2 * HEAD)
-    return pl.pallas_call(
+    layer, d_item = pl.pallas_call(
         return_kernel,
-        out_shape=(shape((ROWS, WIDTH), BF16), shape((256, WIDTH), F32)),
-        in_specs=[spec(VMEM)] * 10 + [spec(ANY)] * 2,
+        out_shape=(shape((ROWS, WIDTH), BF16), shape((256, WIDTH), BF16)),
+        in_specs=[spec(VMEM)] * 5 + [spec(ANY)] * 7,
         out_specs=(spec(VMEM), spec(VMEM)),
         scratch_shapes=[
+            VMEM((256, WIDTH), BF16),
+            VMEM((WIDTH, WIDTH), BF16),
+            VMEM((WIDTH, 4 * WIDTH), BF16),
+            VMEM((WIDTH, WIDTH), BF16),
+            VMEM((ROWS, WIDTH), BF16),
             VMEM((HEADS, 3, 4, PIECE, 2 * HEAD), BF16),
             VMEM((HEADS, 2, 2, HALF, 2 * HEAD), BF16),
             VMEM((SEQ, HALF, 2 * HEAD), BF16),
             VMEM((SEQ, HALF, 2 * HEAD), BF16),
-            VMEM((ROWS, 4 * WIDTH), F32),
-            VMEM((ROWS, WIDTH), BF16),
+            VMEM((SLOTS, 4 * WIDTH), F32),
+            VMEM((SLOTS, WIDTH), BF16),
         ]
         + [VMEM((256, WIDTH), BF16)] * 4
+        + [DMA((5,))]
         + [DMA((4,))] * 3
         + [DMA((SEQ,))] * 6
         + [DMA((GROUPS,))] * 2,
         compiler_params=params(2),
         name="give_back",
     )(
-        item_feats, item_weight, send_rows, event_slot, gain_in, gain_mid, w_in, w_out, cot_out, tokens, mq, dkv,
+        send_rows, event_slot, gain_in, gain_mid, slots, item_feats, item_weight, w_in, w_out, cot_out, mq, dkv,
     )
+    return pl.pallas_call(
+        result_kernel,
+        out_shape=(shape((ROWS, WIDTH), BF16), shape((256, WIDTH), F32)),
+        in_specs=[spec(VMEM)] * 3,
+        out_specs=(spec(VMEM), spec(VMEM)),
+        compiler_params=params(),
+        name="results",
+    )(layer, d_item, item_weight)
 
 
 def solution(mesh):

time: 159 us -> 141 us (0.89)
  Pallas kernels: 152 us -> 140 us
  local copies, waits for them, and re-layouts: 4.88 us -> 0 us
    pallas_call x1, Pallas kernels: 60.1 us -> 42.6 us  [per_device(): pl.pallas_call(return_kernel, out_shape=(shape((ROWS, WIDTH), BF16), shap...]
    pallas_call x1 -> x2, Pallas kernels: 11.3 us -> 18.6 us  [the longest x1 16.2 us: forward_call(): pl.pallas_call(forward_kernel, out_shape=(shape((BLOCKS, BLOCK, 2 * HEAD)...]
    pallas_call x1, Pallas kernels: 54.6 us -> 48 us  [per_device(): pl.pallas_call(send_kernel, out_shape=(shape((SEQ, 2, HALF, 2 * HEAD), BF...]
    pallas_call x1, Pallas kernels: 17.6 us -> 22.7 us  [backward_call(): pl.pallas_call(backward_kernel, out_shape=(shape((BLOCKS, PIECE, 2 * HEAD...]
    unnamed x2 -> x0, local copies, waits for them, and re-layouts: 3.63 us -> none
where the time goes in v3:
time: 141 us
  Pallas kernels  140 us (99%)
    pallas_call x1, Pallas kernels, per_device(): pl.pallas_call(send_kernel, out_shape=(shape((SEQ, 2, HALF, 2 * HEAD), BF...  48 us
    pallas_call x1, Pallas kernels, per_device(): pl.pallas_call(return_kernel, out_shape=(shape((ROWS, WIDTH), BF16), shap...  42.6 us
    pallas_call x1, Pallas kernels, backward_call(): pl.pallas_call(backward_kernel, out_shape=(shape((BLOCKS, PIECE, 2 * HEAD...  22.7 us
    pallas_call x1, Pallas kernels, forward_call(): pl.pallas_call(forward_kernel, out_shape=(shape((BLOCKS, BLOCK, 2 * HEAD)...  16.2 us
    pallas_call x1, Pallas kernels, per_device(): pl.pallas_call(stats_kernel, out_shape=shape((HEADS, TILES, 8, BLOCK), F3...  8.26 us

profile of v3, /device:TPU:1, one launch (start us, length us, event | category | flops | bytes accessed | tf_op | source)
XLA Modules:
  0.0 140.8 jit_solution(15747256024029206089)
XLA Ops:
  0.6 48.0 %send.1 = (bf16[16,2,128,256]{3,2,1,0:T(8,128)(2,1)}, bf16[16,3,32,256]{3,2,1,0:T(8,128)(2,1)}, bf16[256,512]{1,0:T(8,128)(2,1)}, s32[16,8,128]{2,1,0:T(8,128)}, s32[8,128]{1,0:T(8,128)}) custom-call(bf16[256,512]{1,0:T(8,128)(2,1)} %feats_hbm.1, bf16[512,512]{1,0:T(8,128)(2,1)} %item_weight.3, s32[1,256]{1,0:T(1,128)} %send_rows.3, s32[384]{0:T(512)} %event_slot.3, ...), custom_call_target="tpu_custom_call" | custom-call | tf_op jit(solution)/shard_map/send/pallas_call | solution.py:733
  48.7 16.2 %forward.1 = (bf16[48,128,256]{2,1,0:T(8,128)(2,1)}, f32[12,128,128]{2,1,0:T(8,128)}, f32[12,8,128]{2,1,0:T(8,128)}) custom-call(s32[8,128]{1,0:T(8,128)} %get-tuple-element.15.meta, s32[16,8,128]{2,1,0:T(8,128)} %get-tuple-element.16.ids, bf16[16,256,256]{2,1,0:T(8,128)(2,1)} %bitcast.9, bf16[48,32,256]{2,1,0:T(8,128)(2,1)} %bitcast.6), custom_call_target="tpu_custom_call" | custom-call | tf_op jit(solution)/shard_map/forward/pallas_call | solution.py:697
  64.9 8.3 %stats.1.stats_in = f32[4,12,8,128]{3,2,1,0:T(8,128)} custom-call(f32[12,8,128]{2,1,0:T(8,128)} %get-tuple-element.21.stats), custom_call_target="tpu_custom_call" | custom-call | tf_op jit(solution)/shard_map/stats/pallas_call | solution.py:765
  73.1 22.7 %backward.1 = (bf16[48,32,256]{2,1,0:T(8,128)(2,1)}, bf16[16,256,256]{2,1,0:T(8,128)(2,1)}) custom-call(s32[8,128]{1,0:T(8,128)} %get-tuple-element.15.meta, s32[16,8,128]{2,1,0:T(8,128)} %get-tuple-element.16.ids, bf16[48,128,256]{2,1,0:T(8,128)(2,1)} %get-tuple-element.19.kv, bf16[48,32,256]{2,1,0:T(8,128)(2,1)} %bitcast.7, ...), custom_call_target="tpu_custom_call" | custom-call | tf_op jit(solution)/shard_map/backward/pallas_call | solution.py:713
  95.9 42.6 %give_back.1 = (bf16[384,512]{1,0:T(8,128)(2,1)}, bf16[256,512]{1,0:T(8,128)(2,1)}) custom-call(s32[1,256]{1,0:T(1,128)} %send_rows.3, s32[384]{0:T(512)} %event_slot.3, f32[1,512]{1,0:T(1,128)} %bitcast.12, f32[1,512]{1,0:T(1,128)} %bitcast.14, bf16[256,512]{1,0:T(8,128)(2,1)} %get-tuple-element.14.slots_in, bf16[256,512]{1,0:T(8,128)(2,1)} %feats_hbm.1, ...), custom_call_target="tpu_custom_call" | custom-call | tf_op jit(solution)/shard_map/give_back/pallas_call | solution.py:777
  138.5 2.4 %results.1 = (bf16[384,512]{1,0:T(8,128)(2,1)}, f32[256,512]{1,0:T(8,128)}) custom-call(bf16[384,512]{1,0:T(8,128)(2,1)} %get-tuple-element.24.layer, bf16[256,512]{1,0:T(8,128)(2,1)} %get-tuple-element.25.d_item, bf16[512,512]{1,0:T(8,128)(2,1)} %item_weight.3), custom_call_target="tpu_custom_call" | custom-call | tf_op jit(solution)/shard_map/results/pallas_call | solution.py:805

commit v4 on v3

--- a/solution.py
+++ b/solution.py
@@ -17,7 +17,8 @@
 SLOTS = 256
 HALF = 128
 ROWS = 384
-FAR = 1 << 20
+FAR = 30000
+NO_BLOCK = 200
 AT_ONCE = 4
 BACK_AT_ONCE = 4
 SCALE = HEAD**-0.5
@@ -156,8 +157,8 @@
     feats, item_weight, send_rows, event_slot, user_blocks, tail_len, block_order, gain_in, gain_mid,
     w_in_hbm, w_out_hbm, cot_hbm,
     kv_out, qp_out, slots_out, ids_out, meta_out,
-    w_in, w_out, cot, out1, in1, out2, in2, kv, qp, ids, ids_in,
-    load_sem, send1, recv1, send2, recv2, kv_send, kv_recv, pass_send, pass_recv, qp_send, qp_recv, ids_send, ids_recv,
+    w_in, w_out, cot, out1, in1, out2, in2, kv, qp, ids, ids_in, kv_in, kv_events,
+    load_sem, save_sem, send1, recv1, send2, recv2, kv_send, kv_recv, pass_send, pass_recv, qp_send, qp_recv, ids_send, ids_recv,
 ):
     b, s, x, c, y, z = place()
     partner = x * 2 + 1 - c
@@ -227,16 +228,16 @@
             kv[h, 1, :, lanes] = made[HALF:, h * HEAD : (h + 1) * HEAD]
 
     def kv_copy(w, head, core, to_batch, to_seq):
-        return copy_to(kv.at[head, core], kv_out.at[s, core], kv_send.at[w], kv_recv.at[s], to_batch, to_seq)
+        return copy_to(kv.at[head, core], kv_in.at[s, core], kv_send.at[w], kv_recv.at[s], to_batch, to_seq)
 
     def start_kv(w, head, half, core, to_batch, to_seq, here):
         start(
-            here, kv.at[head, core], kv_out.at[s, core], kv_recv.at[s], kv_copy(w, head, core, to_batch, to_seq)
+            here, kv.at[head, core], kv_in.at[s, core], kv_recv.at[s], kv_copy(w, head, core, to_batch, to_seq)
         )
 
     each_worker(start_kv)
 
-    query = silu(dot_nn(normed, w_in[:, 1024:1536])).astype(BF16)
+    query = (silu(dot_nn(normed, w_in[:, 1024:1536])) * (0.5 * SCALE)).astype(BF16)
     query = dot_tn(onehot, query).astype(BF16)
     gate = silu(dot_nn(normed, w_in[:, 0:WIDTH])).astype(BF16)
     gate = dot_tn(onehot, gate)
@@ -268,14 +269,31 @@
 
     def pass_on(source):
         return copy_to(
-            kv_out.at[source, c], kv_out.at[source, c], pass_send.at[source], pass_recv.at[source], partner, s
-        )
-
-    @pl.loop(0, SEQ)
+            kv_in.at[source, c], kv_in.at[source, c], pass_send.at[source], pass_recv.at[source], partner, s
+        )
+
+    def save(source):
+        return pltpu.make_async_copy(kv_events.at[source], kv_out.at[source], save_sem.at[source])
+
+    @pl.loop(0, SEQ + 2)
     def _(i):
-        source = lax.rem(s - i + SEQ, SEQ)
-        arrived(kv_out.at[source, c], kv_recv.at[source])
-        pass_on(source).start()
+        @pl.when(i < SEQ)
+        def _():
+            source = lax.rem(s - i + SEQ, SEQ)
+            arrived(kv_in.at[source, c], kv_recv.at[source])
+            pass_on(source).start()
+
+        @pl.when(i >= 2)
+        def _():
+            source = lax.rem(s - i + 2 + SEQ, SEQ)
+            arrived(kv_in.at[source, 1 - c], pass_recv.at[source])
+            rows = jnp.concatenate([ids_in[source].astype(F32), jnp.zeros((120, 128), F32)], axis=0)
+            columns = jnp.transpose(rows)
+            lane = iota((BLOCK, SLOTS), 1).astype(F32)
+            read = jnp.concatenate([(lane == columns[:, k : k + 1]).astype(BF16) for k in range(3)], axis=0)
+            slots = kv_in[source].reshape(SLOTS, 2 * HEAD)
+            kv_events[source] = dot_nn(read, slots).astype(BF16).reshape(3, BLOCK, 2 * HEAD)
+            save(source).start()
 
     def finish(w, head, half, core, to_batch, to_seq, here):
         @pl.when(jnp.logical_not(here))
@@ -289,8 +307,8 @@
     @pl.loop(0, SEQ)
     def _(source):
         pass_on(source).wait_send()
-        arrived(kv_out.at[source, 1 - c], pass_recv.at[source])
         arrived(qp_out.at[source], qp_recv.at[source])
+        save(source).wait()
 
 
 def tables_of(meta, quarter):
@@ -305,7 +323,7 @@
         start_of = jnp.where(lane >= first, first, start_of)
         first = first + meta[4:5, u : u + 1]
         limit_of = jnp.where(lane == first - 1, meta[5:6, u : u + 1], limit_of)
-    start_of = jnp.where(lane < BLOCKS, start_of, FAR)
+    start_of = jnp.where(lane < BLOCKS, start_of, NO_BLOCK)
     row = iota((8, 128), 0)
     picked = pick4(row, [slot_of, start_of, limit_of, jnp.zeros((1, 128), jnp.int32) + quarter])
     return jnp.where(row == 4, meta[3:4, :], picked)
@@ -338,52 +356,30 @@
     return jnp.concatenate([ref[meta[0, 4 * n + i]] for i in range(4)], axis=0)
 
 
-def query_bounds(meta, t, r):
+def visible(meta, t, j):
+    r, lane = iota((BLOCK, 1), 0), iota((1, BLOCK), 1)
     at = (t * 4 + (r >> 5)) * BLOCK + meta[3, 0] * PIECE + (r & 31)
-    return at, pick4(r >> 5, [meta[1, t * 4 + i] for i in range(4)]) * BLOCK
-
-
-def chunk_of(kv, j):
-    return kv[pl.ds(j * 4, 4)].reshape(4 * BLOCK, 2 * HEAD)
-
-
-def key_places(meta, j, dim):
-    size = (1, BLOCK) if dim else (BLOCK, 1)
-    e = iota(size, dim)
-    return jnp.concatenate(
-        [jnp.where(e < meta[2, j * 4 + i], (j * 4 + i) * BLOCK + e, FAR) for i in range(4)], axis=dim
+    since = pick4(r >> 5, [meta[1, t * 4 + i] for i in range(4)]) * BLOCK
+    where = jnp.concatenate(
+        [jnp.where(lane < meta[2, j * 4 + i], (j * 4 + i) * BLOCK + lane, FAR) for i in range(4)], axis=1
     )
-
-
-def forward_kernel(meta, ids, kv_slots, qp, kv_out, mixed_out, stats_out, kv, total, kv_sem):
-    @pl.loop(0, SEQ, unroll=4)
-    def _(s):
-        rows = jnp.concatenate([ids[s].astype(F32), jnp.zeros((120, 128), F32)], axis=0)
-        columns = jnp.transpose(rows)
-        for k in range(3):
-            onehot = (iota((BLOCK, SLOTS), 1).astype(F32) == columns[:, k : k + 1]).astype(BF16)
-            kv[meta[4, s * 3 + k]] = dot_nn(onehot, kv_slots[s]).astype(BF16)
-
-    save = pltpu.make_async_copy(kv, kv_out, kv_sem)
-    save.start()
-
+    where, at, since = (v.astype(jnp.int16) for v in (where, at, since))
+    return (where <= at) & (where >= since)
+
+
+def forward_kernel(meta, kv, qp, mixed_out, stats_out, total):
     @pl.loop(0, TILES + 1)
     def _(t):
         total[t] = jnp.zeros((BLOCK, HEAD), F32)
 
     def step(_, state):
         pairs, t, j = walk(meta, *state, AT_ONCE)
-        keyvals = [chunk_of(kv, j) for _, j in pairs]
-        us = [
-            dot_nt(four(qp, meta, t)[:, :HEAD], keyval[:, :HEAD]) * (0.5 * SCALE)
-            for (t, _), keyval in zip(pairs, keyvals)
-        ]
+        keyvals = [four(kv, meta, j) for _, j in pairs]
+        us = [dot_nt(four(qp, meta, t)[:, :HEAD], keyval[:, :HEAD]) for (t, _), keyval in zip(pairs, keyvals)]
         weights = []
         for (t_, j_), u in zip(pairs, us):
-            at, since = query_bounds(meta, t_, iota((BLOCK, 1), 0))
-            where = key_places(meta, j_, 1)
-            w = u + u * jnp.tanh(u)
-            weights.append(jnp.where((where <= at) & (where >= since), w, 0.0).astype(BF16))
+            w = u.astype(BF16) * (1.0 + jnp.tanh(u)).astype(BF16)
+            weights.append(jnp.where(visible(meta, t_, j_), w, jnp.zeros_like(w)))
         for (t_, _), w, keyval in zip(pairs, weights, keyvals):
             total[t_] += dot_nn(w, keyval[:, HEAD:])
         return t, j
@@ -408,8 +404,6 @@
         )
         stats_out[t] = jnp.transpose(stats)[0:8, :]
 
-    save.wait()
-
 
 def stats_kernel(stats, all_stats, held, send, recv):
     b, s, x, c, y, z = place()
@@ -428,18 +422,23 @@
     all_stats[...] = held[...]
 
 
-def backward_kernel(meta, ids, kv, qp, mixed_in, stats_in, mq_out, dkv_out, d_mixed, d_query, dkv):
-    @pl.loop(0, TILES)
-    def _(t):
-        dkv[pl.ds(t * 4 * BLOCK, 4 * BLOCK), :] = jnp.zeros((4 * BLOCK, 2 * HEAD), F32)
-
+def backward_kernel(
+    meta, ids, qp, mixed_in, stats_in, kv_hbm, mq_hbm, dkv_hbm,
+    kv, mq, dkv_slots, d_mixed, query_t, d_mixed_t, d_query, dkv, kv_sem, mq_sem, dkv_sem,
+):
+    load = pltpu.make_async_copy(kv_hbm, kv, kv_sem)
+    load.start()
     d_mixed[TILES] = jnp.zeros((BLOCK, HEAD), BF16)
+    d_mixed_t[TILES] = jnp.zeros((BLOCK, HEAD), BF16)
+    query_t[TILES] = jnp.zeros((BLOCK, HEAD), BF16)
 
     @pl.loop(0, TILES, unroll=4)
     def _(t):
         d_query[t] = jnp.zeros((BLOCK, HEAD), F32)
+        dkv[pl.ds(t * 4, 4)] = jnp.zeros((4, 2 * HEAD, BLOCK), F32)
         mixed = mixed_in[t]
-        upstream = four(qp, meta, t)[:, HEAD:].astype(F32)
+        both = four(qp, meta, t)
+        upstream = both[:, HEAD:].astype(F32)
         stats = [stats_in[h, t] for h in range(HEADS)]
         mean = sum(v[0:1] for v in stats) * 0.25
         spread = sum(v[1:2] + HEAD * (v[0:1] - mean) * (v[0:1] - mean) for v in stats) * (1.0 / WIDTH)
@@ -449,53 +448,65 @@
         columns = jnp.transpose(pick4(iota((BLOCK, HEAD), 0), [mean, inverse, slant, along]))
         mean, inverse, slant, along = (columns[:, i : i + 1] for i in range(4))
         normal = (mixed - mean) * inverse
-        d_mixed[t] = (inverse * (upstream - slant - normal * along)).astype(BF16)
+        made = (inverse * (upstream - slant - normal * along)).astype(BF16)
+        d_mixed[t] = made
+        d_mixed_t[t] = jnp.transpose(made)
+        query_t[t] = jnp.transpose(both[:, :HEAD])
+        mixed = mixed.astype(BF16)
+        for i in range(4):
+            mq[meta[0, t * 4 + i], :, 0:HEAD] = mixed[i * PIECE : (i + 1) * PIECE]
+
+    load.wait()
 
     def step(_, state):
         pairs, t, j = walk(meta, *state, BACK_AT_ONCE)
-        keyvals = [chunk_of(kv, j) for _, j in pairs]
-        queries = [four(qp, meta, t)[:, :HEAD] for t, _ in pairs]
-        d_mixeds = [d_mixed[t] for t, _ in pairs]
-        us = [dot_nt(keyval[:, :HEAD], query) * (0.5 * SCALE) for keyval, query in zip(keyvals, queries)]
-        d_weights = [dot_nt(keyval[:, HEAD:], dm) for keyval, dm in zip(keyvals, d_mixeds)]
+        keyvals = [four(kv, meta, j) for _, j in pairs]
+        us = [dot_nt(four(qp, meta, t)[:, :HEAD], keyval[:, :HEAD]) for (t, _), keyval in zip(pairs, keyvals)]
+        d_weights = [dot_nt(d_mixed[t], keyval[:, HEAD:]) for (t, _), keyval in zip(pairs, keyvals)]
         made = []
         for (t_, j_), u, dw in zip(pairs, us, d_weights):
             th = jnp.tanh(u)
-            a = 1.0 + th
-            w = u * a
-            ds = dw * (a + w * (1.0 - th))
-            at, since = query_bounds(meta, t_, iota((1, BLOCK), 1))
-            where = key_places(meta, j_, 0)
-            seen = (where <= at) & (where >= since)
-            made.append((jnp.where(seen, w, 0.0).astype(BF16), jnp.where(seen, ds, 0.0).astype(BF16)))
-        for (t_, j_), keyval, query, dm, (w, ds) in zip(pairs, keyvals, queries, d_mixeds, made):
-            keys = pl.ds(pl.multiple_of(j_ * 4 * BLOCK, 4 * BLOCK), 4 * BLOCK)
-            dkv[keys, 0:HEAD] += dot_nn(ds, query)
-            dkv[keys, HEAD : 2 * HEAD] += dot_nn(w, dm)
-            d_query[t_] += dot_tn(ds, keyval[:, :HEAD])
+            a = (1.0 + th).astype(BF16)
+            w = u.astype(BF16) * a
+            ds = dw.astype(BF16) * (a + w * (1.0 - th).astype(BF16))
+            seen = visible(meta, t_, j_)
+            made.append((jnp.where(seen, w, jnp.zeros_like(w)), jnp.where(seen, ds, jnp.zeros_like(ds))))
+        for (t_, j_), keyval, (w, ds) in zip(pairs, keyvals, made):
+            d_key = dot_nn(query_t[t_], ds)
+            d_value = dot_nn(d_mixed_t[t_], w)
+            for i in range(4):
+                dkv[j_ * 4 + i, 0:HEAD] += d_key[:, i * BLOCK : (i + 1) * BLOCK]
+                dkv[j_ * 4 + i, HEAD : 2 * HEAD] += d_value[:, i * BLOCK : (i + 1) * BLOCK]
+            d_query[t_] += dot_nn(ds, keyval[:, :HEAD])
         return t, j
 
     lax.fori_loop(0, (pairs_in_all(meta) + BACK_AT_ONCE - 1) // BACK_AT_ONCE, step, (jnp.int32(0), jnp.int32(0)))
 
     @pl.loop(0, TILES)
     def _(t):
-        mixed = mixed_in[t].astype(BF16)
         dq = (d_query[t] * (0.5 * SCALE)).astype(BF16)
         for i in range(4):
-            n = t * 4 + i
-            slot = meta[0, n]
-            rows = slice(i * PIECE, (i + 1) * PIECE)
-            mq_out[slot, :, 0:HEAD] = mixed[rows]
-            mq_out[slot, :, HEAD : 2 * HEAD] = dq[rows]
+            mq[meta[0, t * 4 + i], :, HEAD : 2 * HEAD] = dq[i * PIECE : (i + 1) * PIECE]
+
+    mq_save = pltpu.make_async_copy(mq, mq_hbm, mq_sem)
+    mq_save.start()
+
+    def save(s):
+        return pltpu.make_async_copy(dkv_slots.at[s], dkv_hbm.at[s], dkv_sem.at[s])
 
     @pl.loop(0, SEQ, unroll=4)
     def _(s):
-        total = jnp.zeros((SLOTS, 2 * HEAD), F32)
-        for k in range(3):
-            keys = pl.ds(pl.multiple_of(meta[4, s * 3 + k] * BLOCK, BLOCK), BLOCK)
-            total += dot_nn(slot_onehot(ids[s, k : k + 1, :]), dkv[keys, :].astype(BF16))
-        dkv_out[s, :, 0:HEAD] = (total[:, 0:HEAD] * (0.5 * SCALE)).astype(BF16)
-        dkv_out[s, :, HEAD : 2 * HEAD] = total[:, HEAD : 2 * HEAD].astype(BF16)
+        total = sum(
+            dot_nt(slot_onehot(ids[s, k : k + 1, :]), dkv[meta[4, s * 3 + k]].astype(BF16)) for k in range(3)
+        )
+        dkv_slots[s] = total.astype(BF16)
+        save(s).start()
+
+    mq_save.wait()
+
+    @pl.loop(0, SEQ)
+    def _(s):
+        save(s).wait()
 
 
 def return_kernel(
@@ -693,36 +704,40 @@
     )
 
 
-def forward_call(meta, ids, kv, qp):
+def forward_call(meta, kv, qp):
     return pl.pallas_call(
         forward_kernel,
-        out_shape=(
-            shape((BLOCKS, BLOCK, 2 * HEAD), BF16),
-            shape((TILES, BLOCK, HEAD), F32),
-            shape((TILES, 8, BLOCK), F32),
-        ),
-        in_specs=[spec(SMEM), spec(VMEM), spec(VMEM), spec(VMEM)],
-        out_specs=(spec(ANY), spec(VMEM), spec(VMEM)),
-        scratch_shapes=[VMEM((BLOCKS, BLOCK, 2 * HEAD), BF16), VMEM((TILES + 1, BLOCK, HEAD), F32), DMA],
+        out_shape=(shape((TILES, BLOCK, HEAD), F32), shape((TILES, 8, BLOCK), F32)),
+        in_specs=[spec(SMEM), spec(VMEM), spec(VMEM)],
+        out_specs=(spec(VMEM), spec(VMEM)),
+        scratch_shapes=[VMEM((TILES + 1, BLOCK, HEAD), F32)],
         compiler_params=params(),
         name="forward",
-    )(meta, ids, kv, qp)
+    )(meta, kv, qp)
 
 
 def backward_call(meta, ids, kv, qp, mixed, stats):
     return pl.pallas_call(
         backward_kernel,
         out_shape=(shape((BLOCKS, PIECE, 2 * HEAD), BF16), shape((SEQ, SLOTS, 2 * HEAD), BF16)),
-        in_specs=[spec(SMEM)] + [spec(VMEM)] * 5,
-        out_specs=(spec(VMEM), spec(VMEM)),
+        in_specs=[spec(SMEM)] + [spec(VMEM)] * 4 + [spec(ANY)],
+        out_specs=(spec(ANY), spec(ANY)),
         scratch_shapes=[
+            VMEM((BLOCKS, BLOCK, 2 * HEAD), BF16),
+            VMEM((BLOCKS, PIECE, 2 * HEAD), BF16),
+            VMEM((SEQ, SLOTS, 2 * HEAD), BF16),
             VMEM((TILES + 1, BLOCK, HEAD), BF16),
+            VMEM((TILES + 1, HEAD, BLOCK), BF16),
+            VMEM((TILES + 1, HEAD, BLOCK), BF16),
             VMEM((TILES + 1, BLOCK, HEAD), F32),
-            VMEM((BLOCKS * BLOCK, 2 * HEAD), F32),
+            VMEM((BLOCKS, 2 * HEAD, BLOCK), F32),
+            DMA,
+            DMA,
+            DMA((SEQ,)),
         ],
         compiler_params=params(),
         name="backward",
-    )(meta, ids, kv, qp, mixed, stats)
+    )(meta, ids, qp, mixed, stats, kv)
 
 
 def per_device(
@@ -733,7 +748,7 @@
     kv, qp, slots, ids, meta = pl.pallas_call(
         send_kernel,
         out_shape=(
-            shape((SEQ, 2, HALF, 2 * HEAD), BF16),
+            shape((SEQ, 3, BLOCK, 2 * HEAD), BF16),
             shape((SEQ, 3, PIECE, 2 * HEAD), BF16),
             shape((SLOTS, WIDTH), BF16),
             shape((SEQ, 8, 128), jnp.int32),
@@ -748,7 +763,10 @@
             VMEM((HEADS, 3, 4, PIECE, 2 * HEAD), BF16),
             VMEM((8, 128), jnp.int32),
             VMEM((SEQ, 8, 128), jnp.int32),
+            VMEM((SEQ, 2, HALF, 2 * HEAD), BF16),
+            VMEM((SEQ, 3, BLOCK, 2 * HEAD), BF16),
             DMA((3,)),
+            DMA((SEQ,)),
             DMA((GROUPS,)),
             DMA((GROUPS,)),
         ]
@@ -759,9 +777,9 @@
         item_feats, item_weight, send_rows, event_slot, user_blocks, tail_len, block_order, gain_in, gain_mid, w_in,
         w_out, cot_out,
     )
-    kv = kv.reshape(SEQ, SLOTS, 2 * HEAD)
+    kv = kv.reshape(BLOCKS, BLOCK, 2 * HEAD)
     qp = qp.reshape(BLOCKS, PIECE, 2 * HEAD)
-    kv, mixed, stats = forward_call(meta, ids, kv, qp)
+    mixed, stats = forward_call(meta, kv, qp)
     stats = pl.pallas_call(
         stats_kernel,
         out_shape=shape((HEADS, TILES, 8, BLOCK), F32),

time: 141 us -> 133 us (0.943)
  Pallas kernels: 140 us -> 132 us
    pallas_call x2, Pallas kernels: 64.2 us -> 58.5 us  [the longest x1 48.2 us: per_device(): pl.pallas_call(send_kernel, out_shape=(shape((SEQ, 3, BLOCK, 2 * HEAD), B...]
    pallas_call x1, Pallas kernels: 22.7 us -> 17.8 us  [backward_call(): pl.pallas_call(backward_kernel, out_shape=(shape((BLOCKS, PIECE, 2 * HEAD...]
    pallas_call x1, Pallas kernels: 42.6 us -> 44.8 us  [per_device(): pl.pallas_call(return_kernel, out_shape=(shape((ROWS, WIDTH), BF16), shap...]
where the time goes in v4:
time: 133 us; the launch traced here: 132 us
  Pallas kernels  132 us (99%)
    pallas_call x1, Pallas kernels, per_device(): pl.pallas_call(send_kernel, out_shape=(shape((SEQ, 3, BLOCK, 2 * HEAD), B...  48.2 us
    pallas_call x1, Pallas kernels, per_device(): pl.pallas_call(return_kernel, out_shape=(shape((ROWS, WIDTH), BF16), shap...  44.8 us
    pallas_call x1, Pallas kernels, backward_call(): pl.pallas_call(backward_kernel, out_shape=(shape((BLOCKS, PIECE, 2 * HEAD...  17.8 us
    pallas_call x1, Pallas kernels, forward_call(): pl.pallas_call(forward_kernel, out_shape=(shape((TILES, BLOCK, HEAD), F32...  10.3 us
    pallas_call x1, Pallas kernels, per_device(): pl.pallas_call(stats_kernel, out_shape=shape((HEADS, TILES, 8, BLOCK), F3...  8.21 us

profile of v4, /device:TPU:1, one launch (start us, length us, event | category | flops | bytes accessed | tf_op | source)
XLA Modules:
  0.0 132.3 jit_solution(10478772247388986316)
XLA Ops:
  0.6 48.2 %send.1 = (bf16[16,3,128,256]{3,2,1,0:T(8,128)(2,1)}, bf16[16,3,32,256]{3,2,1,0:T(8,128)(2,1)}, bf16[256,512]{1,0:T(8,128)(2,1)}, s32[16,8,128]{2,1,0:T(8,128)}, s32[8,128]{1,0:T(8,128)}) custom-call(bf16[256,512]{1,0:T(8,128)(2,1)} %feats_hbm.1, bf16[512,512]{1,0:T(8,128)(2,1)} %item_weight.3, s32[1,256]{1,0:T(1,128)} %send_rows.3, s32[384]{0:T(512)} %event_slot.3, ...), custom_call_target="tpu_custom_call" | custom-call | tf_op jit(solution)/shard_map/send/pallas_call | solution.py:748
  48.8 10.3 %forward.1 = (f32[12,128,128]{2,1,0:T(8,128)}, f32[12,8,128]{2,1,0:T(8,128)}) custom-call(s32[8,128]{1,0:T(8,128)} %get-tuple-element.14.meta, bf16[48,128,256]{2,1,0:T(8,128)(2,1)} %bitcast.6, bf16[48,32,256]{2,1,0:T(8,128)(2,1)} %bitcast.8), custom_call_target="tpu_custom_call" | custom-call | tf_op jit(solution)/shard_map/forward/pallas_call | solution.py:708
  59.2 8.2 %stats.1.stats_in = f32[4,12,8,128]{3,2,1,0:T(8,128)} custom-call(f32[12,8,128]{2,1,0:T(8,128)} %get-tuple-element.19.stats), custom_call_target="tpu_custom_call" | custom-call | tf_op jit(solution)/shard_map/stats/pallas_call | solution.py:783
  67.4 17.8 %backward.1 = (bf16[48,32,256]{2,1,0:T(8,128)(2,1)}, bf16[16,256,256]{2,1,0:T(8,128)(2,1)}) custom-call(s32[8,128]{1,0:T(8,128)} %get-tuple-element.14.meta, s32[16,8,128]{2,1,0:T(8,128)} %get-tuple-element.15.ids, bf16[48,32,256]{2,1,0:T(8,128)(2,1)} %bitcast.9, f32[12,128,128]{2,1,0:T(8,128)} %get-tuple-element.18.mixed_in, ...), custom_call_target="tpu_custom_call" | custom-call | tf_op jit(solution)/shard_map/backward/pallas_call | solution.py:720
  85.2 44.8 %give_back.1 = (bf16[384,512]{1,0:T(8,128)(2,1)}, bf16[256,512]{1,0:T(8,128)(2,1)}) custom-call(s32[1,256]{1,0:T(1,128)} %send_rows.3, s32[384]{0:T(512)} %event_slot.3, f32[1,512]{1,0:T(1,128)} %bitcast.13, f32[1,512]{1,0:T(1,128)} %bitcast.15, bf16[256,512]{1,0:T(8,128)(2,1)} %get-tuple-element.13.slots_in, bf16[256,512]{1,0:T(8,128)(2,1)} %feats_hbm.1, ...), custom_call_target="tpu_custom_call" | custom-call | tf_op jit(solution)/shard_map/give_back/pallas_call | solution.py:795
  129.9 2.4 %results.1 = (bf16[384,512]{1,0:T(8,128)(2,1)}, f32[256,512]{1,0:T(8,128)}) custom-call(bf16[384,512]{1,0:T(8,128)(2,1)} %get-tuple-element.22.layer, bf16[256,512]{1,0:T(8,128)(2,1)} %get-tuple-element.23.d_item, bf16[512,512]{1,0:T(8,128)(2,1)} %item_weight.3), custom_call_target="tpu_custom_call" | custom-call | tf_op jit(solution)/shard_map/results/pallas_call | solution.py:823

commit v5 on v4

--- a/solution.py
+++ b/solution.py
@@ -20,6 +20,8 @@
 FAR = 30000
 NO_BLOCK = 200
 AT_ONCE = 4
+MOST_PAIRS = 48
+MOST_CHUNKS = 7
 BACK_AT_ONCE = 4
 SCALE = HEAD**-0.5
 MESH = pl.DeviceIdType.MESH
@@ -156,9 +158,10 @@
 def send_kernel(
     feats, item_weight, send_rows, event_slot, user_blocks, tail_len, block_order, gain_in, gain_mid,
     w_in_hbm, w_out_hbm, cot_hbm,
-    kv_out, qp_out, slots_out, ids_out, meta_out,
-    w_in, w_out, cot, out1, in1, out2, in2, kv, qp, ids, ids_in, kv_in, kv_events,
-    load_sem, save_sem, send1, recv1, send2, recv2, kv_send, kv_recv, pass_send, pass_recv, qp_send, qp_recv, ids_send, ids_recv,
+    kv_out, q_out, p_out, slots_out, ids_out, meta_out, mixed_out, stats_out,
+    w_in, w_out, cot, out1, in1, out2, in2, kv, q, p, ids, ids_in, kv_in, kv_events, q_in, p_in, tables, products, stats,
+    load_sem, save_sem, out_sem, table_sem, send1, recv1, send2, recv2, kv_send, kv_recv, pass_send, pass_recv,
+    q_send, q_recv, p_send, p_recv, ids_send, ids_recv, stats_send, stats_recv,
 ):
     b, s, x, c, y, z = place()
     partner = x * 2 + 1 - c
@@ -239,26 +242,31 @@
 
     query = (silu(dot_nn(normed, w_in[:, 1024:1536])) * (0.5 * SCALE)).astype(BF16)
     query = dot_tn(onehot, query).astype(BF16)
+    for h in range(HEADS):
+        q[h] = query[:, h * HEAD : (h + 1) * HEAD].reshape(3, 4, PIECE, HEAD)
+
+    def piece_copy(src, dst, send, recv, w, head, half, core, to_batch, to_seq):
+        three = pl.ds(s * 3, 3)
+        return copy_to(
+            src.at[head, :, half * 2 + core], dst.at[three], send.at[w], recv.at[s], to_batch, to_seq
+        )
+
+    def start_piece(src, dst, send, recv):
+        def act(w, head, half, core, to_batch, to_seq, here):
+            start(
+                here, src.at[head, :, half * 2 + core], dst.at[pl.ds(s * 3, 3)], recv.at[s],
+                piece_copy(src, dst, send, recv, w, head, half, core, to_batch, to_seq),
+            )
+
+        each_worker(act)
+
+    start_piece(q, q_in, q_send, q_recv)
     gate = silu(dot_nn(normed, w_in[:, 0:WIDTH])).astype(BF16)
     gate = dot_tn(onehot, gate)
     upstream = (d_gated.astype(F32) * gate * gain_mid[...]).astype(BF16)
     for h in range(HEADS):
-        cols = slice(h * HEAD, (h + 1) * HEAD)
-        qp[h, :, :, :, 0:HEAD] = query[:, cols].reshape(3, 4, PIECE, HEAD)
-        qp[h, :, :, :, HEAD : 2 * HEAD] = upstream[:, cols].reshape(3, 4, PIECE, HEAD)
-
-    def qp_copy(w, head, half, core, to_batch, to_seq):
-        return copy_to(
-            qp.at[head, :, half * 2 + core], qp_out.at[s], qp_send.at[w], qp_recv.at[s], to_batch, to_seq
-        )
-
-    def start_qp(w, head, half, core, to_batch, to_seq, here):
-        start(
-            here, qp.at[head, :, half * 2 + core], qp_out.at[s], qp_recv.at[s],
-            qp_copy(w, head, half, core, to_batch, to_seq),
-        )
-
-    each_worker(start_qp)
+        p[h] = upstream[:, h * HEAD : (h + 1) * HEAD].reshape(3, 4, PIECE, HEAD)
+    start_piece(p, p_in, p_send, p_recv)
 
     @pl.loop(0, SEQ)
     def _(source):
@@ -266,6 +274,8 @@
 
     ids_out[...] = ids_in[...]
     meta_out[...] = tables_of(ids_in[s], (y % 2) * 2 + c)
+    table_copy = pltpu.make_async_copy(meta_out, tables, table_sem)
+    table_copy.start()
 
     def pass_on(source):
         return copy_to(
@@ -273,7 +283,8 @@
         )
 
     def save(source):
-        return pltpu.make_async_copy(kv_events.at[source], kv_out.at[source], save_sem.at[source])
+        three = pl.ds(source * 3, 3)
+        return pltpu.make_async_copy(kv_events.at[three], kv_out.at[three], save_sem.at[source])
 
     @pl.loop(0, SEQ + 2)
     def _(i):
@@ -292,30 +303,97 @@
             lane = iota((BLOCK, SLOTS), 1).astype(F32)
             read = jnp.concatenate([(lane == columns[:, k : k + 1]).astype(BF16) for k in range(3)], axis=0)
             slots = kv_in[source].reshape(SLOTS, 2 * HEAD)
-            kv_events[source] = dot_nn(read, slots).astype(BF16).reshape(3, BLOCK, 2 * HEAD)
+            made = dot_nn(read, slots).astype(BF16).reshape(3, BLOCK, 2 * HEAD)
+            kv_events[pl.ds(source * 3, 3)] = made
             save(source).start()
+
+    table_copy.wait()
+
+    @pl.loop(0, SEQ)
+    def _(source):
+        arrived(q_in.at[pl.ds(source * 3, 3)], q_recv.at[source])
+
+    def step(k, state):
+        pairs, t, j = walk(tables, *state, AT_ONCE)
+        keyvals = [four(kv_events, tables, j) for _, j in pairs]
+        us = [dot_nt(four(q_in, tables, t), keyval[:, :HEAD]) for (t, _), keyval in zip(pairs, keyvals)]
+        weights = []
+        for (t_, j_), u in zip(pairs, us):
+            w = u.astype(BF16) * (1.0 + jnp.tanh(u)).astype(BF16)
+            weights.append(jnp.where(visible(tables, t_, j_), w, jnp.zeros_like(w)))
+        for n, (w, keyval) in enumerate(zip(weights, keyvals)):
+            products[k * AT_ONCE + n] = dot_nn(w, keyval[:, HEAD:])
+        return t, j
+
+    lax.fori_loop(0, MOST_PAIRS // AT_ONCE, step, (jnp.int32(0), jnp.int32(0)))
+
+    @pl.loop(0, SEQ)
+    def _(source):
+        arrived(p_in.at[pl.ds(source * 3, 3)], p_recv.at[source])
+
+    outs = [
+        pltpu.make_async_copy(src, dst, out_sem.at[k]) for k, (src, dst) in enumerate(((q_in, q_out), (p_in, p_out)))
+    ]
+    for out in outs:
+        out.start()
+
+    first_pair = jnp.int32(0)
+    for t in range(TILES):
+        count = t + 1 - tables[1, 4 * t] // 4
+        mixed = products[jnp.minimum(first_pair, MOST_PAIRS - 1)]
+        for k in range(1, min(t + 1, MOST_CHUNKS)):
+            more = products[jnp.minimum(first_pair + k, MOST_PAIRS - 1)]
+            mixed = mixed + jnp.where(k < count, more, jnp.zeros_like(more))
+        first_pair = first_pair + count
+        upstream = four(p_in, tables, t).astype(F32)
+        mixed_out[t] = mixed
+        mean = jnp.mean(mixed, axis=1, keepdims=True)
+        centred = mixed - mean
+        sums = pick4(
+            iota((BLOCK, HEAD), 1) & 3,
+            [
+                mean,
+                jnp.sum(centred * centred, axis=1, keepdims=True),
+                jnp.sum(upstream, axis=1, keepdims=True),
+                jnp.sum(upstream * centred, axis=1, keepdims=True),
+            ],
+        )
+        rows = slice(4 * (t % 2), 4 * (t % 2) + 4)
+        stats[z, t // 2, rows, :] = jnp.transpose(sums)[rows, :]
+
+    copies = []
+    for k in range(1, HEADS):
+        peer = lax.rem(z + k, HEADS)
+        copy = copy_to(stats.at[z], stats.at[z], stats_send.at[k], stats_recv.at[k], b, y * 4 + peer)
+        copy.start()
+        copies.append(copy)
 
     def finish(w, head, half, core, to_batch, to_seq, here):
         @pl.when(jnp.logical_not(here))
         def _():
             ids_copy(w, to_batch, to_seq).wait_send()
             kv_copy(w, head, core, to_batch, to_seq).wait_send()
-            qp_copy(w, head, half, core, to_batch, to_seq).wait_send()
+            piece_copy(q, q_in, q_send, q_recv, w, head, half, core, to_batch, to_seq).wait_send()
+            piece_copy(p, p_in, p_send, p_recv, w, head, half, core, to_batch, to_seq).wait_send()
 
     each_worker(finish)
 
     @pl.loop(0, SEQ)
     def _(source):
         pass_on(source).wait_send()
-        arrived(qp_out.at[source], qp_recv.at[source])
         save(source).wait()
+
+    for out in outs:
+        out.wait()
+    wait_all(copies)
+    stats_out[...] = stats[...]
 
 
 def tables_of(meta, quarter):
     slot, lane = iota((128, 128), 0), iota((1, 128), 1)
-    held = jnp.transpose(jnp.broadcast_to(meta[3:4, :].astype(F32), (128, 128)))
-    slot_of = jnp.where((held == iota((128, 128), 1).astype(F32)) & (slot < BLOCKS), slot.astype(F32), 0.0)
-    slot_of = jnp.sum(slot_of, axis=0, keepdims=True).astype(jnp.int32)
+    held = jnp.transpose(jnp.broadcast_to(meta[3:4, :], (128, 128)))
+    slot_of = jnp.where((held == iota((128, 128), 1)) & (slot < BLOCKS), slot, 0)
+    slot_of = jnp.minimum(jnp.sum(slot_of, axis=0, keepdims=True), BLOCKS - 1)
     first = jnp.zeros((1, 1), jnp.int32)
     start_of = jnp.zeros((1, 128), jnp.int32)
     limit_of = jnp.full((1, 128), BLOCK, jnp.int32)
@@ -334,7 +412,7 @@
 
 
 def first_chunk(meta, t):
-    return jnp.minimum(meta[1, 4 * t] // 4, TILES - 1)
+    return jnp.clip(meta[1, 4 * t] // 4, 0, TILES - 1)
 
 
 def walk(meta, t, j, count):
@@ -367,63 +445,8 @@
     return (where <= at) & (where >= since)
 
 
-def forward_kernel(meta, kv, qp, mixed_out, stats_out, total):
-    @pl.loop(0, TILES + 1)
-    def _(t):
-        total[t] = jnp.zeros((BLOCK, HEAD), F32)
-
-    def step(_, state):
-        pairs, t, j = walk(meta, *state, AT_ONCE)
-        keyvals = [four(kv, meta, j) for _, j in pairs]
-        us = [dot_nt(four(qp, meta, t)[:, :HEAD], keyval[:, :HEAD]) for (t, _), keyval in zip(pairs, keyvals)]
-        weights = []
-        for (t_, j_), u in zip(pairs, us):
-            w = u.astype(BF16) * (1.0 + jnp.tanh(u)).astype(BF16)
-            weights.append(jnp.where(visible(meta, t_, j_), w, jnp.zeros_like(w)))
-        for (t_, _), w, keyval in zip(pairs, weights, keyvals):
-            total[t_] += dot_nn(w, keyval[:, HEAD:])
-        return t, j
-
-    lax.fori_loop(0, (pairs_in_all(meta) + AT_ONCE - 1) // AT_ONCE, step, (jnp.int32(0), jnp.int32(0)))
-
-    @pl.loop(0, TILES, unroll=4)
-    def _(t):
-        mixed = total[t]
-        upstream = four(qp, meta, t)[:, HEAD:].astype(F32)
-        mixed_out[t] = mixed
-        mean = jnp.mean(mixed, axis=1, keepdims=True)
-        centred = mixed - mean
-        stats = pick4(
-            iota((BLOCK, HEAD), 1),
-            [
-                mean,
-                jnp.sum(centred * centred, axis=1, keepdims=True),
-                jnp.sum(upstream, axis=1, keepdims=True),
-                jnp.sum(upstream * centred, axis=1, keepdims=True),
-            ],
-        )
-        stats_out[t] = jnp.transpose(stats)[0:8, :]
-
-
-def stats_kernel(stats, all_stats, held, send, recv):
-    b, s, x, c, y, z = place()
-    barrier = pltpu.get_barrier_semaphore()
-    for k in range(1, HEADS):
-        signal(barrier, b, y * 4 + lax.rem(z + k, HEADS))
-    pl.semaphore_wait(barrier, HEADS - 1)
-    copies = []
-    for k in range(1, HEADS):
-        peer = lax.rem(z + k, HEADS)
-        copy = copy_to(stats, held.at[z], send.at[k], recv.at[k], b, y * 4 + peer)
-        copy.start()
-        copies.append(copy)
-    held[z] = stats[...]
-    wait_all(copies)
-    all_stats[...] = held[...]
-
-
 def backward_kernel(
-    meta, ids, qp, mixed_in, stats_in, kv_hbm, mq_hbm, dkv_hbm,
+    meta, ids, q, p, mixed_in, stats_in, kv_hbm, mq_hbm, dkv_hbm,
     kv, mq, dkv_slots, d_mixed, query_t, d_mixed_t, d_query, dkv, kv_sem, mq_sem, dkv_sem,
 ):
     load = pltpu.make_async_copy(kv_hbm, kv, kv_sem)
@@ -432,14 +455,11 @@
     d_mixed_t[TILES] = jnp.zeros((BLOCK, HEAD), BF16)
     query_t[TILES] = jnp.zeros((BLOCK, HEAD), BF16)
 
-    @pl.loop(0, TILES, unroll=4)
-    def _(t):
+    def prepare(t, stats):
         d_query[t] = jnp.zeros((BLOCK, HEAD), F32)
         dkv[pl.ds(t * 4, 4)] = jnp.zeros((4, 2 * HEAD, BLOCK), F32)
         mixed = mixed_in[t]
-        both = four(qp, meta, t)
-        upstream = both[:, HEAD:].astype(F32)
-        stats = [stats_in[h, t] for h in range(HEADS)]
+        upstream = four(p, meta, t).astype(F32)
         mean = sum(v[0:1] for v in stats) * 0.25
         spread = sum(v[1:2] + HEAD * (v[0:1] - mean) * (v[0:1] - mean) for v in stats) * (1.0 / WIDTH)
         inverse = lax.rsqrt(spread + 1e-05)
@@ -451,17 +471,23 @@
         made = (inverse * (upstream - slant - normal * along)).astype(BF16)
         d_mixed[t] = made
         d_mixed_t[t] = jnp.transpose(made)
-        query_t[t] = jnp.transpose(both[:, :HEAD])
+        query_t[t] = jnp.transpose(four(q, meta, t))
         mixed = mixed.astype(BF16)
         for i in range(4):
             mq[meta[0, t * 4 + i], :, 0:HEAD] = mixed[i * PIECE : (i + 1) * PIECE]
 
+    @pl.loop(0, TILES // 2, unroll=2)
+    def _(pair):
+        both = [stats_in[h, pair] for h in range(HEADS)]
+        prepare(pair * 2, [v[0:4] for v in both])
+        prepare(pair * 2 + 1, [v[4:8] for v in both])
+
     load.wait()
 
     def step(_, state):
         pairs, t, j = walk(meta, *state, BACK_AT_ONCE)
         keyvals = [four(kv, meta, j) for _, j in pairs]
-        us = [dot_nt(four(qp, meta, t)[:, :HEAD], keyval[:, :HEAD]) for (t, _), keyval in zip(pairs, keyvals)]
+        us = [dot_nt(four(q, meta, t), keyval[:, :HEAD]) for (t, _), keyval in zip(pairs, keyvals)]
         d_weights = [dot_nt(d_mixed[t], keyval[:, HEAD:]) for (t, _), keyval in zip(pairs, keyvals)]
         made = []
         for (t_, j_), u, dw in zip(pairs, us, d_weights):
@@ -494,12 +520,11 @@
     def save(s):
         return pltpu.make_async_copy(dkv_slots.at[s], dkv_hbm.at[s], dkv_sem.at[s])
 
-    @pl.loop(0, SEQ, unroll=4)
+    @pl.loop(0, SEQ, unroll=8)
     def _(s):
-        total = sum(
-            dot_nt(slot_onehot(ids[s, k : k + 1, :]), dkv[meta[4, s * 3 + k]].astype(BF16)) for k in range(3)
-        )
-        dkv_slots[s] = total.astype(BF16)
+        wanted = jnp.concatenate([ids[s, k : k + 1, :] for k in range(3)], axis=1)
+        grads = jnp.concatenate([dkv[meta[4, s * 3 + k]].astype(BF16) for k in range(3)], axis=1)
+        dkv_slots[s] = dot_nt(slot_onehot(wanted), grads).astype(BF16)
         save(s).start()
 
     mq_save.wait()
@@ -704,23 +729,11 @@
     )
 
 
-def forward_call(meta, kv, qp):
-    return pl.pallas_call(
-        forward_kernel,
-        out_shape=(shape((TILES, BLOCK, HEAD), F32), shape((TILES, 8, BLOCK), F32)),
-        in_specs=[spec(SMEM), spec(VMEM), spec(VMEM)],
-        out_specs=(spec(VMEM), spec(VMEM)),
-        scratch_shapes=[VMEM((TILES + 1, BLOCK, HEAD), F32)],
-        compiler_params=params(),
-        name="forward",
-    )(meta, kv, qp)
-
-
-def backward_call(meta, ids, kv, qp, mixed, stats):
+def backward_call(meta, ids, kv, q, p, mixed, stats):
     return pl.pallas_call(
         backward_kernel,
         out_shape=(shape((BLOCKS, PIECE, 2 * HEAD), BF16), shape((SEQ, SLOTS, 2 * HEAD), BF16)),
-        in_specs=[spec(SMEM)] + [spec(VMEM)] * 4 + [spec(ANY)],
+        in_specs=[spec(SMEM)] + [spec(VMEM)] * 5 + [spec(ANY)],
         out_specs=(spec(ANY), spec(ANY)),
         scratch_shapes=[
             VMEM((BLOCKS, BLOCK, 2 * HEAD), BF16),
@@ -737,7 +750,7 @@
         ],
         compiler_params=params(),
         name="backward",
-    )(meta, ids, qp, mixed, stats, kv)
+    )(meta, ids, q, p, mixed, stats, kv)
 
 
 def per_device(
@@ -745,51 +758,51 @@
     cot_out,
 ):
     gain_in, gain_mid = gain_in.reshape(1, WIDTH), gain_mid.reshape(1, WIDTH)
-    kv, qp, slots, ids, meta = pl.pallas_call(
+    kv, q, p, slots, ids, meta, mixed, stats = pl.pallas_call(
         send_kernel,
         out_shape=(
-            shape((SEQ, 3, BLOCK, 2 * HEAD), BF16),
-            shape((SEQ, 3, PIECE, 2 * HEAD), BF16),
+            shape((BLOCKS, BLOCK, 2 * HEAD), BF16),
+            shape((BLOCKS, PIECE, HEAD), BF16),
+            shape((BLOCKS, PIECE, HEAD), BF16),
             shape((SLOTS, WIDTH), BF16),
             shape((SEQ, 8, 128), jnp.int32),
             shape((8, 128), jnp.int32),
+            shape((TILES, BLOCK, HEAD), F32),
+            shape((HEADS, TILES // 2, 8, BLOCK), F32),
         ),
         in_specs=[spec(VMEM)] * 9 + [spec(ANY)] * 3,
-        out_specs=(spec(ANY), spec(ANY), spec(VMEM), spec(VMEM), spec(VMEM)),
+        out_specs=(spec(ANY), spec(ANY), spec(ANY)) + (spec(VMEM),) * 5,
         scratch_shapes=[VMEM((WIDTH, 4 * WIDTH), BF16), VMEM((WIDTH, WIDTH), BF16), VMEM((ROWS, WIDTH), BF16)]
         + [VMEM((256, WIDTH), BF16)] * 4
         + [
             VMEM((HEADS, 2, HALF, 2 * HEAD), BF16),
-            VMEM((HEADS, 3, 4, PIECE, 2 * HEAD), BF16),
+            VMEM((HEADS, 3, 4, PIECE, HEAD), BF16),
+            VMEM((HEADS, 3, 4, PIECE, HEAD), BF16),
             VMEM((8, 128), jnp.int32),
             VMEM((SEQ, 8, 128), jnp.int32),
             VMEM((SEQ, 2, HALF, 2 * HEAD), BF16),
-            VMEM((SEQ, 3, BLOCK, 2 * HEAD), BF16),
+            VMEM((BLOCKS, BLOCK, 2 * HEAD), BF16),
+            VMEM((BLOCKS, PIECE, HEAD), BF16),
+            VMEM((BLOCKS, PIECE, HEAD), BF16),
+            SMEM((8, 128), jnp.int32),
+            VMEM((MOST_PAIRS, BLOCK, HEAD), F32),
+            VMEM((HEADS, TILES // 2, 8, BLOCK), F32),
             DMA((3,)),
             DMA((SEQ,)),
+            DMA((2,)),
+            DMA,
             DMA((GROUPS,)),
             DMA((GROUPS,)),
         ]
-        + [DMA((SEQ,))] * 10,
+        + [DMA((SEQ,))] * 12
+        + [DMA((HEADS,))] * 2,
         compiler_params=params(0),
         name="send",
     )(
         item_feats, item_weight, send_rows, event_slot, user_blocks, tail_len, block_order, gain_in, gain_mid, w_in,
         w_out, cot_out,
     )
-    kv = kv.reshape(BLOCKS, BLOCK, 2 * HEAD)
-    qp = qp.reshape(BLOCKS, PIECE, 2 * HEAD)
-    mixed, stats = forward_call(meta, kv, qp)
-    stats = pl.pallas_call(
-        stats_kernel,
-        out_shape=shape((HEADS, TILES, 8, BLOCK), F32),
-        in_specs=[spec(VMEM)],
-        out_specs=spec(VMEM),
-        scratch_shapes=[VMEM((HEADS, TILES, 8, BLOCK), F32), DMA((HEADS,)), DMA((HEADS,))],
-        compiler_params=params(1),
-        name="stats",
-    )(stats)
-    mq, dkv = backward_call(meta, ids, kv, qp, mixed, stats)
+    mq, dkv = backward_call(meta, ids, kv, q, p, mixed, stats)
     mq = mq.reshape(SEQ, 3, PIECE, 2 * HEAD)
     dkv = dkv.reshape(SEQ, 2, HALF, 2 * HEAD)
     layer, d_item = pl.pallas_call(

time: 133 us -> 127 us (0.955)
  Pallas kernels: 132 us -> 126 us
    pallas_call x3 -> x1, Pallas kernels: 66.7 us -> 60.7 us  [per_device(): pl.pallas_call(send_kernel, out_shape=(shape((BLOCKS, BLOCK, 2 * HEAD), B...]
    pallas_call x1, Pallas kernels: 44.8 us -> 47.1 us  [per_device(): pl.pallas_call(return_kernel, out_shape=(shape((ROWS, WIDTH), BF16), shap...]
    pallas_call x1, Pallas kernels: 17.8 us -> 16.1 us  [backward_call(): pl.pallas_call(backward_kernel, out_shape=(shape((BLOCKS, PIECE, 2 * HEAD...]
where the time goes in v5:
time: 127 us
  Pallas kernels  126 us (99%)
    pallas_call x1, Pallas kernels, per_device(): pl.pallas_call(send_kernel, out_shape=(shape((BLOCKS, BLOCK, 2 * HEAD), B...  60.7 us
    pallas_call x1, Pallas kernels, per_device(): pl.pallas_call(return_kernel, out_shape=(shape((ROWS, WIDTH), BF16), shap...  47.1 us
    pallas_call x1, Pallas kernels, backward_call(): pl.pallas_call(backward_kernel, out_shape=(shape((BLOCKS, PIECE, 2 * HEAD...  16.1 us

profile of v5, /device:TPU:1, one launch (start us, length us, event | category | flops | bytes accessed | tf_op | source)
XLA Modules:
  0.0 126.9 jit_solution(10913194926237713849)
XLA Ops:
  0.6 60.7 %send.1 = (bf16[48,128,256]{2,1,0:T(8,128)(2,1)}, bf16[48,32,128]{2,1,0:T(8,128)(2,1)}, bf16[48,32,128]{2,1,0:T(8,128)(2,1)}, bf16[256,512]{1,0:T(8,128)(2,1)}, ...) custom-call(bf16[256,512]{1,0:T(8,128)(2,1)} %feats_hbm.1, ...), custom_call_target="tpu_custom_call" | custom-call | tf_op jit(solution)/shard_map/send/pallas_call | solution.py:761
  61.3 16.1 %backward.1 = (bf16[48,32,256]{2,1,0:T(8,128)(2,1)}, bf16[16,256,256]{2,1,0:T(8,128)(2,1)}) custom-call(s32[8,128]{1,0:T(8,128)} %get-tuple-element.15.meta, s32[16,8,128]{2,1,0:T(8,128)} %get-tuple-element.16.ids, bf16[48,32,128]{2,1,0:T(8,128)(2,1)} %get-tuple-element.17.q, bf16[48,32,128]{2,1,0:T(8,128)(2,1)} %get-tuple-element.18.p, ...), custom_call_target="tpu_custom_call" | custom-call | tf_op jit(solution)/shard_map/backward/pallas_call | solution.py:733
  77.4 47.1 %give_back.1 = (bf16[384,512]{1,0:T(8,128)(2,1)}, bf16[256,512]{1,0:T(8,128)(2,1)}) custom-call(s32[1,256]{1,0:T(1,128)} %send_rows.3, s32[384]{0:T(512)} %event_slot.3, f32[1,512]{1,0:T(1,128)} %bitcast.7, f32[1,512]{1,0:T(1,128)} %bitcast.9, bf16[256,512]{1,0:T(8,128)(2,1)} %get-tuple-element.14.slots_in, bf16[256,512]{1,0:T(8,128)(2,1)} %feats_hbm.1, ...), custom_call_target="tpu_custom_call" | custom-call | tf_op jit(solution)/shard_map/give_back/pallas_call | solution.py:808
  124.5 2.4 %results.1 = (bf16[384,512]{1,0:T(8,128)(2,1)}, f32[256,512]{1,0:T(8,128)}) custom-call(bf16[384,512]{1,0:T(8,128)(2,1)} %get-tuple-element.24.layer, bf16[256,512]{1,0:T(8,128)(2,1)} %get-tuple-element.25.d_item, bf16[512,512]{1,0:T(8,128)(2,1)} %item_weight.3), custom_call_target="tpu_custom_call" | custom-call | tf_op jit(solution)/shard_map/results/pallas_call | solution.py:836

commit v6 on v5

v6 whole, which is shorter than its diff:
```python
import jax
import jax.numpy as jnp
from jax import lax
from jax.experimental import pallas as pl
from jax.experimental.pallas import tpu as pltpu
from jax.sharding import PartitionSpec as P

WIDTH = 512
HEAD = 128
HEADS = 4
BLOCK = 128
BLOCKS = 48
SEQ = 16
GROUPS = 8
PIECE = 32
TILES = 12
SLOTS = 256
HALF = 128
ROWS = 384
FAR = 30000
NO_BLOCK = 200
AT_ONCE = 4
MOST_PAIRS = 48
MOST_CHUNKS = 7
BACK_AT_ONCE = 4
SCALE = HEAD**-0.5
MESH = pl.DeviceIdType.MESH
F32 = jnp.float32
BF16 = jnp.bfloat16


def dot_nn(a, b):
    return jnp.dot(a, b, preferred_element_type=F32)


def dot_nt(a, b):
    return lax.dot_general(a, b, (((1,), (1,)), ((), ())), preferred_element_type=F32)


def dot_tn(a, b):
    return lax.dot_general(a, b, (((0,), (0,)), ((), ())), preferred_element_type=F32)


def silu(v):
    u = 0.5 * v
    return u + u * jnp.tanh(u)


def silu_slope(v):
    u = 0.5 * v
    t = jnp.tanh(u)
    a = 1.0 + t
    return 0.5 * (a + u * a * (1.0 - t))


def normalize(values):
    mean = jnp.mean(values, axis=-1, keepdims=True)
    centred = values - mean
    spread = jnp.mean(centred * centred, axis=-1, keepdims=True)
    inverse = lax.rsqrt(spread + 1e-05)
    return centred * inverse, inverse


def iota(shape, dim):
    return lax.broadcasted_iota(jnp.int32, shape, dim)


def place():
    b, s = lax.axis_index("batch"), lax.axis_index("seq")
    return b, s, b // 2, b % 2, s // 4, s % 4


def worker_at(w, x, c):
    head, half, core = w % 4, (w // 4) % 2, w // 8
    return head, half, core, x * 2 + core, (2 * c + half) * 4 + head


def copy_to(src, dst, send, recv, batch, seq):
    return pltpu.make_async_remote_copy(
        src_ref=src, dst_ref=dst, send_sem=send, recv_sem=recv, device_id=(batch, seq), device_id_type=MESH
    )


def arrived(ref, sem):
    pltpu.make_async_copy(ref, ref, sem).wait()


def rows_of(index, size):
    return pl.ds(pl.multiple_of(index * size, size), size)


def slot_rows(event_slot):
    e = event_slot
    return ((e >> 1) & 15) * 16 + (e >> 5) * 2 + (e & 1)


def slot_onehot(wanted):
    return (iota((SLOTS, wanted.shape[1]), 0) == wanted).astype(BF16)


def by_seq():
    i, j = iota((256, 256), 0), iota((256, 256), 1)
    return (j == ((i >> 1) & 7) * 32 + (i >> 4) * 2 + (i & 1)).astype(BF16)


def by_batch():
    i, j = iota((256, 256), 0), iota((256, 256), 1)
    return (j == ((i >> 1) & 15) * 16 + (i >> 5) * 2 + (i & 1)).astype(BF16)


def exchange_batch(src, dst, send, recv, b, s):
    copies = []
    for k in range(1, GROUPS):
        peer = lax.rem(b + k, GROUPS)
        copy = copy_to(src.at[rows_of(peer, 32)], dst.at[rows_of(b, 32)], send.at[k], recv.at[k], peer, s)
        copy.start()
        copies.append(copy)
    dst[rows_of(b, 32), :] = src[rows_of(b, 32), :]
    return copies


def exchange_seq(src, dst, send, recv, b, s):
    copies = []
    for k in range(1, SEQ):
        peer = lax.rem(s + k, SEQ)
        copy = copy_to(src.at[rows_of(peer, 16)], dst.at[rows_of(s, 16)], send.at[k], recv.at[k], b, peer)
        copy.start()
        copies.append(copy)
    dst[rows_of(s, 16), :] = src[rows_of(s, 16), :]
    return copies


def signal(barrier, batch, seq):
    pl.semaphore_signal(barrier, inc=1, device_id=(batch, seq), device_id_type=MESH)


def greet(b, s, partner):
    barrier = pltpu.get_barrier_semaphore()
    for k in range(1, GROUPS):
        signal(barrier, lax.rem(b + k, GROUPS), s)

    @pl.loop(1, SEQ)
    def _(k):
        peer = lax.rem(s + k, SEQ)
        signal(barrier, b, peer)
        signal(barrier, partner, peer)


def greeted():
    pl.semaphore_wait(pltpu.get_barrier_semaphore(), GROUPS - 1 + 2 * (SEQ - 1))


def wait_all(copies):
    for copy in copies:
        copy.wait()


def layer_kernel(
    feats, item_weight, send_rows, event_slot, user_blocks, tail_len, block_order, gain_in, gain_mid,
    w_in_hbm, w_out_hbm, cot_hbm, layer_out, d_item_out, *scratch,
):
    (
        w_in, w_out, cot, out1, in1, out2, in2, kv, q, p, ids, ids_in, kv_in, kv_events, q_in, p_in, tables_vmem, tables,
        spans, products, kv_products, stats, mixed_of, mixed_sorted, dq_sorted, mixed_slots, dq_slots, mixed_home,
        dq_home, d_mixed, d_mixed_t, query_t, own, give, part, summed, dkv_home, pre, d_pre, gate_of, d_gated_of, normal_of,
        inverse_of, back2, home2, back1, home1,
    ) = scratch[:47]
    (
        load_sem, table_sem, send1, recv1, send2, recv2, kv_send, kv_recv, pass_send, pass_recv, q_send, q_recv, p_send,
        p_recv, ids_send, ids_recv, stats_send, stats_recv, mixed_send, mixed_recv, dq_send, dq_recv, part_send,
        part_recv, dkv_send, dkv_recv, back2_send, back2_recv, back1_send, back1_recv,
    ) = scratch[47:]
    b, s, x, c, y, z = place()
    partner = x * 2 + 1 - c
    half = y % 2
    to_batch = x * 2 + y // 2
    me = z + 4 * half + 8 * c
    greet(b, s, partner)
    loads = [
        pltpu.make_async_copy(src, dst, load_sem.at[k])
        for k, (src, dst) in enumerate(((w_out_hbm, w_out), (cot_hbm, cot), (w_in_hbm, w_in)))
    ]
    for load in loads:
        load.start()

    embedded = silu(dot_nn(feats[...], item_weight[...])).astype(BF16)
    wanted = (iota((256, 256), 0) == send_rows[...]).astype(BF16)
    out1[...] = dot_tn(wanted, embedded).astype(BF16)
    slot_of_event = slot_rows(event_slot[...].reshape(1, ROWS))
    ids[...] = jnp.zeros_like(ids)
    for k in range(3):
        ids[k : k + 1, :] = slot_of_event[:, k * BLOCK : (k + 1) * BLOCK]
    ids[3:4, 0:BLOCKS] = block_order[...]
    ids[4:5, 0:4] = user_blocks[...]
    ids[5:6, 0:4] = tail_len[...]
    greeted()
    first = exchange_batch(out1, in1, send1, recv1, b, s)

    def each_worker(act):
        @pl.loop(0, SEQ)
        def _(i):
            w = lax.rem(i + s, SEQ)
            head, half, core, to_batch, to_seq = worker_at(w, x, c)
            here = (to_batch == b) & (to_seq == s)
            act(w, head, half, core, to_batch, to_seq, here)

    def start(here, src, dst, recv, remote):
        @pl.when(here)
        def _():
            pltpu.make_async_copy(src, dst, recv).start()

        @pl.when(jnp.logical_not(here))
        def _():
            remote.start()

    def ids_copy(w, to_batch, to_seq):
        return copy_to(ids, ids_in.at[s], ids_send.at[w], ids_recv.at[s], to_batch, to_seq)

    def start_ids(w, head, half, core, to_batch, to_seq, here):
        start(here, ids, ids_in.at[s], ids_recv.at[s], ids_copy(w, to_batch, to_seq))

    each_worker(start_ids)

    loads[0].wait()
    loads[1].wait()
    d_gated_of[...] = dot_nt(cot[...], w_out[...]).astype(BF16)
    wait_all(first)
    out2[...] = dot_nn(by_seq(), in1[...]).astype(BF16)
    second = exchange_seq(out2, in2, send2, recv2, b, s)
    onehot = slot_onehot(slot_of_event)
    loads[2].wait()
    wait_all(second)
    normal, inverse = normalize(in2[...].astype(F32))
    normal_of[...] = normal
    inverse_of[...] = jnp.broadcast_to(inverse, (SLOTS, 128))
    normed = (normal * gain_in[...]).astype(BF16)

    def project(first_column):
        cols = slice(first_column, first_column + WIDTH)
        made = dot_nn(normed, w_in[:, cols])
        pre[:, cols] = made
        return silu(made)

    for side, first_column in ((0, 1536), (1, 512)):
        lanes = slice(side * HEAD, side * HEAD + HEAD)
        made = project(first_column).astype(BF16)
        for h in range(HEADS):
            kv[h, 0, :, lanes] = made[:HALF, h * HEAD : (h + 1) * HEAD]
            kv[h, 1, :, lanes] = made[HALF:, h * HEAD : (h + 1) * HEAD]

    def kv_copy(w, head, core, to_batch, to_seq):
        return copy_to(kv.at[head, core], kv_in.at[s, core], kv_send.at[w], kv_recv.at[s], to_batch, to_seq)

    def start_kv(w, head, half, core, to_batch, to_seq, here):
        start(
            here, kv.at[head, core], kv_in.at[s, core], kv_recv.at[s], kv_copy(w, head, core, to_batch, to_seq)
        )

    each_worker(start_kv)

    query = (project(1024) * (0.5 * SCALE)).astype(BF16)
    query = dot_tn(onehot, query).astype(BF16)
    for h in range(HEADS):
        q[h] = query[:, h * HEAD : (h + 1) * HEAD].reshape(3, 4, PIECE, HEAD)

    def piece_copy(src, dst, send, recv, w, head, half, core, to_batch, to_seq):
        three = pl.ds(s * 3, 3)
        return copy_to(
            src.at[head, :, half * 2 + core], dst.at[three], send.at[w], recv.at[s], to_batch, to_seq
        )

    def start_piece(src, dst, send, recv):
        def act(w, head, half, core, to_batch, to_seq, here):
            start(
                here, src.at[head, :, half * 2 + core], dst.at[pl.ds(s * 3, 3)], recv.at[s],
                piece_copy(src, dst, send, recv, w, head, half, core, to_batch, to_seq),
            )

        each_worker(act)

    start_piece(q, q_in, q_send, q_recv)
    gate = dot_tn(onehot, project(0).astype(BF16))
    gate_of[...] = gate
    upstream = (d_gated_of[...].astype(F32) * gate * gain_mid[...]).astype(BF16)
    for h in range(HEADS):
        p[h] = upstream[:, h * HEAD : (h + 1) * HEAD].reshape(3, 4, PIECE, HEAD)
    start_piece(p, p_in, p_send, p_recv)

    @pl.loop(0, SEQ)
    def _(source):
        arrived(ids_in.at[source], ids_recv.at[source])

    tables_vmem[...] = tables_of(ids_in[s], half * 2 + c)
    table_copy = pltpu.make_async_copy(tables_vmem, tables, table_sem)
    table_copy.start()

    def pass_on(source):
        return copy_to(
            kv_in.at[source, c], kv_in.at[source, c], pass_send.at[source], pass_recv.at[source], partner, s
        )

    @pl.loop(0, SEQ + 2)
    def _(i):
        @pl.when(i < SEQ)
        def _():
            source = lax.rem(s - i + SEQ, SEQ)
            arrived(kv_in.at[source, c], kv_recv.at[source])
            pass_on(source).start()

        @pl.when(i >= 2)
        def _():
            source = lax.rem(s - i + 2 + SEQ, SEQ)
            arrived(kv_in.at[source, 1 - c], pass_recv.at[source])
            rows = jnp.concatenate([ids_in[source].astype(F32), jnp.zeros((120, 128), F32)], axis=0)
            columns = jnp.transpose(rows)
            lane = iota((BLOCK, SLOTS), 1).astype(F32)
            read = jnp.concatenate([(lane == columns[:, k : k + 1]).astype(BF16) for k in range(3)], axis=0)
            slots = kv_in[source].reshape(SLOTS, 2 * HEAD)
            made = dot_nn(read, slots).astype(BF16).reshape(3, BLOCK, 2 * HEAD)
            kv_events[pl.ds(source * 3, 3)] = made

    table_copy.wait()

    @pl.loop(0, SEQ)
    def _(source):
        arrived(q_in.at[pl.ds(source * 3, 3)], q_recv.at[source])

    def step(k, state):
        pairs, t, j = walk(tables, *state, AT_ONCE)
        keyvals = [four(kv_events, tables, j) for _, j in pairs]
        us = [dot_nt(four(q_in, tables, t), keyval[:, :HEAD]) for (t, _), keyval in zip(pairs, keyvals)]
        weights = []
        for (t_, j_), u in zip(pairs, us):
            w = u.astype(BF16) * (1.0 + jnp.tanh(u)).astype(BF16)
            weights.append(jnp.where(visible(tables, t_, j_), w, jnp.zeros_like(w)))
        for n, (w, keyval) in enumerate(zip(weights, keyvals)):
            products[k * AT_ONCE + n] = dot_nn(w, keyval[:, HEAD:])
        return t, j

    lax.fori_loop(0, MOST_PAIRS // AT_ONCE, step, (jnp.int32(0), jnp.int32(0)))

    @pl.loop(0, SEQ)
    def _(source):
        arrived(p_in.at[pl.ds(source * 3, 3)], p_recv.at[source])

    def sum_pairs(t, first, count):
        summed = products[jnp.minimum(first, MOST_PAIRS - 1)]
        for k in range(1, min(t + 1, MOST_CHUNKS)):
            more = products[jnp.minimum(first + k, MOST_PAIRS - 1)]
            summed = summed + jnp.where(k < count, more, jnp.zeros_like(more))
        return summed

    starts = []
    first_pair = jnp.int32(0)
    for t in range(TILES):
        count = t + 1 - tables[1, 4 * t] // 4
        starts.append((first_pair, count))
        spans[0, t] = first_pair
        spans[1, t] = tables[1, 4 * t] // 4
        mixed = sum_pairs(t, first_pair, count)
        first_pair = first_pair + count
        upstream = four(p_in, tables, t).astype(F32)
        mixed_of[t] = mixed
        mixed_sorted[4 * t : 4 * t + 4] = mixed.astype(BF16).reshape(4, PIECE, HEAD)
        mean = jnp.mean(mixed, axis=1, keepdims=True)
        centred = mixed - mean
        sums = pick4(
            iota((BLOCK, HEAD), 1) & 3,
            [
                mean,
                jnp.sum(centred * centred, axis=1, keepdims=True),
                jnp.sum(upstream, axis=1, keepdims=True),
                jnp.sum(upstream * centred, axis=1, keepdims=True),
            ],
        )
        rows = slice(4 * (t % 2), 4 * (t % 2) + 4)
        stats[z, t // 2, rows, :] = jnp.transpose(sums)[rows, :]

    copies = []
    for k in range(1, HEADS):
        peer = lax.rem(z + k, HEADS)
        copy = copy_to(stats.at[z], stats.at[z], stats_send.at[k], stats_recv.at[k], b, y * 4 + peer)
        copy.start()
        copies.append(copy)

    def is_here(source):
        return (to_batch == b) & (source == s)

    def home_copy(src, dst, send, recv, source):
        three = pl.ds(source * 3, 3)
        return copy_to(
            src.at[three], dst.at[z, :, half * 2 + c], send.at[source], recv.at[me], to_batch, source
        )

    def send_home(src, dst, send, recv):
        @pl.loop(0, SEQ)
        def _(i):
            source = lax.rem(i + s, SEQ)
            start(
                is_here(source), src.at[pl.ds(source * 3, 3)], dst.at[z, :, half * 2 + c], recv.at[me],
                home_copy(src, dst, send, recv, source),
            )

    @pl.loop(0, BLOCKS)
    def _(i):
        mixed_slots[i] = mixed_sorted[tables[4, i]]

    send_home(mixed_slots, mixed_home, mixed_send, mixed_recv)

    d_mixed[TILES] = jnp.zeros((BLOCK, HEAD), BF16)
    d_mixed_t[TILES] = jnp.zeros((HEAD, BLOCK), BF16)
    query_t[TILES] = jnp.zeros((HEAD, BLOCK), BF16)
    for t in range(TILES):
        query_t[t] = jnp.transpose(four(q_in, tables, t))
    wait_all(copies)
    for t in range(TILES):
        rows = slice(4 * (t % 2), 4 * (t % 2) + 4)
        of = [stats[h, t // 2, rows, :] for h in range(HEADS)]
        mean = sum(v[0:1] for v in of) * 0.25
        spread = sum(v[1:2] + HEAD * (v[0:1] - mean) * (v[0:1] - mean) for v in of) * (1.0 / WIDTH)
        inverse = lax.rsqrt(spread + 1e-05)
        slant = sum(v[2:3] for v in of) * (1.0 / WIDTH)
        along = sum(v[3:4] + v[2:3] * (v[0:1] - mean) for v in of) * (1.0 / WIDTH) * inverse
        columns = jnp.transpose(pick4(iota((BLOCK, HEAD), 0), [mean, inverse, slant, along]))
        mean, inverse, slant, along = (columns[:, i : i + 1] for i in range(4))
        made = (mixed_of[t] - mean) * inverse
        made = (inverse * (four(p_in, tables, t).astype(F32) - slant - made * along)).astype(BF16)
        d_mixed[t] = made
        d_mixed_t[t] = jnp.transpose(made)

    def back_step(k, state):
        pairs, t, j = walk(tables, *state, BACK_AT_ONCE)
        keyvals = [four(kv_events, tables, j) for _, j in pairs]
        us = [dot_nt(four(q_in, tables, t), keyval[:, :HEAD]) for (t, _), keyval in zip(pairs, keyvals)]
        d_weights = [dot_nt(d_mixed[t], keyval[:, HEAD:]) for (t, _), keyval in zip(pairs, keyvals)]
        made = []
        for (t_, j_), u, dw in zip(pairs, us, d_weights):
            th = jnp.tanh(u)
            a = (1.0 + th).astype(BF16)
            w = u.astype(BF16) * a
            ds = dw.astype(BF16) * (a + w * (1.0 - th).astype(BF16))
            seen = visible(tables, t_, j_)
            made.append((jnp.where(seen, w, jnp.zeros_like(w)), jnp.where(seen, ds, jnp.zeros_like(ds))))
        for n, ((t_, _), keyval, (w, ds)) in enumerate(zip(pairs, keyvals, made)):
            pair = k * BACK_AT_ONCE + n
            d_key = dot_nn(query_t[t_], ds).astype(BF16)
            d_value = dot_nn(d_mixed_t[t_], w).astype(BF16)
            for i in range(4):
                kv_products[pair, i, 0:HEAD] = d_key[:, i * BLOCK : (i + 1) * BLOCK]
                kv_products[pair, i, HEAD : 2 * HEAD] = d_value[:, i * BLOCK : (i + 1) * BLOCK]
            products[pair] = dot_nn(ds, keyval[:, :HEAD])
        return t, j

    lax.fori_loop(0, MOST_PAIRS // BACK_AT_ONCE, back_step, (jnp.int32(0), jnp.int32(0)))

    for t in range(TILES):
        dq = (sum_pairs(t, *starts[t]) * (0.5 * SCALE)).astype(BF16)
        dq_sorted[4 * t : 4 * t + 4] = dq.reshape(4, PIECE, HEAD)

    @pl.loop(0, BLOCKS)
    def _(i):
        dq_slots[i] = dq_sorted[tables[4, i]]

    send_home(dq_slots, dq_home, dq_send, dq_recv)

    def block_grad(n):
        j = n // 4
        total = jnp.zeros((2 * HEAD, BLOCK), F32)
        for k in range(MOST_CHUNKS):
            t = jnp.minimum(j + k, TILES - 1)
            since = spans[1, t]
            pair = jnp.clip(spans[0, t] + j - since, 0, MOST_PAIRS - 1)
            more = kv_products[pair, n % 4].astype(F32)
            total += jnp.where((j + k < TILES) & (since <= j), more, jnp.zeros_like(more))
        return total.astype(BF16)

    def part_copy(source):
        return copy_to(
            give.at[source], part.at[source], part_send.at[source], part_recv.at[source], partner, s
        )

    def dkv_copy(source):
        return copy_to(
            summed.at[source], dkv_home.at[z, half, c], dkv_send.at[source], dkv_recv.at[me], to_batch, source
        )

    @pl.loop(0, SEQ + 2)
    def _(i):
        @pl.when(i < SEQ)
        def _():
            source = lax.rem(s + i, SEQ)
            wanted = jnp.concatenate([ids_in[source, m : m + 1, :] for m in range(3)], axis=1)
            grads = jnp.concatenate([block_grad(tables[4, source * 3 + m]) for m in range(3)], axis=1)
            made = dot_nt(slot_onehot(wanted), grads).astype(BF16)
            own[source] = jnp.where(c == 0, made[:HALF], made[HALF:])
            give[source] = jnp.where(c == 0, made[HALF:], made[:HALF])
            part_copy(source).start()

        @pl.when(i >= 2)
        def _():
            source = lax.rem(s + i - 2, SEQ)
            arrived(part.at[source], part_recv.at[source])
            summed[source] = (own[source].astype(F32) + part[source].astype(F32)).astype(BF16)
            start(
                is_here(source), summed.at[source], dkv_home.at[z, half, c], dkv_recv.at[me], dkv_copy(source)
            )

    tokens = dot_tn(onehot, in2[...])
    slot_cot = dot_nn(onehot, cot[...])
    item_slope = silu_slope(dot_nn(feats[...], item_weight[...]))
    for first_column in range(0, 4 * WIDTH, WIDTH):
        cols = slice(first_column, first_column + WIDTH)
        pre[:, cols] = silu_slope(pre[:, cols])

    @pl.loop(0, SEQ)
    def _(w):
        arrived(mixed_home.at[w % 4, :, ((w // 4) % 2) * 2 + w // 8], mixed_recv.at[w])

    mixed = jnp.concatenate([mixed_home[h].reshape(ROWS, HEAD) for h in range(HEADS)], axis=1)
    normed_mid = normalize(mixed.astype(F32))[0] * gain_mid[...]
    gated = (normed_mid * gate_of[...]).astype(BF16)
    layer_out[...] = (tokens + dot_nn(gated, w_out[...])).astype(BF16)
    d_gate = dot_nn(onehot, (d_gated_of[...].astype(F32) * normed_mid).astype(BF16))
    d_pre[...] = (d_gate * pre[:, 0:WIDTH]).astype(BF16)
    d_normed = dot_nt(d_pre[...], w_in[:, 0:WIDTH])

    @pl.loop(0, SEQ)
    def _(w):
        arrived(dq_home.at[w % 4, :, ((w // 4) % 2) * 2 + w // 8], dq_recv.at[w])

    d_query = jnp.concatenate([dq_home[h].reshape(ROWS, HEAD) for h in range(HEADS)], axis=1)
    d_pre[...] = (dot_nn(onehot, d_query) * pre[:, 1024:1536]).astype(BF16)
    d_normed += dot_nt(d_pre[...], w_in[:, 1024:1536])

    @pl.loop(0, SEQ)
    def _(w):
        arrived(dkv_home.at[w % 4, (w // 4) % 2, w // 8], dkv_recv.at[w])

    for lanes, first_column in ((0, 1536), (HEAD, 512)):
        cols = slice(first_column, first_column + WIDTH)
        grad = jnp.concatenate(
            [
                dkv_home[h, 0, :, :, lanes : lanes + HEAD].reshape(SLOTS, HEAD).astype(F32)
                + dkv_home[h, 1, :, :, lanes : lanes + HEAD].reshape(SLOTS, HEAD).astype(F32)
                for h in range(HEADS)
            ],
            axis=1,
        )
        d_pre[...] = (grad * pre[:, cols]).astype(BF16)
        d_normed += dot_nt(d_pre[...], w_in[:, cols])

    scaled = d_normed * gain_in[...]
    normal = normal_of[...]
    d_slots = slot_cot + inverse_of[:, 0:1] * (
        scaled
        - jnp.mean(scaled, axis=-1, keepdims=True)
        - normal * jnp.mean(scaled * normal, axis=-1, keepdims=True)
    )
    back2[...] = d_slots.astype(BF16)
    wait_all(exchange_seq(back2, home2, back2_send, back2_recv, b, s))
    back1[...] = dot_nn(by_batch(), home2[...]).astype(BF16)
    last = exchange_batch(back1, home1, back1_send, back1_recv, b, s)
    wanted = (iota((256, 256), 0) == send_rows[...]).astype(BF16)
    wait_all(last)
    d_embedded = dot_nn(wanted, home1[...])
    d_item_out[...] = (d_embedded * item_slope).astype(BF16)

    def finish(w, head, half, core, to_batch, to_seq, here):
        @pl.when(jnp.logical_not(here))
        def _():
            ids_copy(w, to_batch, to_seq).wait_send()
            kv_copy(w, head, core, to_batch, to_seq).wait_send()
            piece_copy(q, q_in, q_send, q_recv, w, head, half, core, to_batch, to_seq).wait_send()
            piece_copy(p, p_in, p_send, p_recv, w, head, half, core, to_batch, to_seq).wait_send()

    each_worker(finish)

    @pl.loop(0, SEQ)
    def _(source):
        pass_on(source).wait_send()
        part_copy(source).wait_send()

        @pl.when(jnp.logical_not(is_here(source)))
        def _():
            home_copy(mixed_slots, mixed_home, mixed_send, mixed_recv, source).wait_send()
            home_copy(dq_slots, dq_home, dq_send, dq_recv, source).wait_send()
            dkv_copy(source).wait_send()


def tables_of(meta, quarter):
    slot, lane = iota((128, 128), 0), iota((1, 128), 1)
    held = jnp.transpose(jnp.broadcast_to(meta[3:4, :], (128, 128)))
    slot_of = jnp.where((held == iota((128, 128), 1)) & (slot < BLOCKS), slot, 0)
    slot_of = jnp.minimum(jnp.sum(slot_of, axis=0, keepdims=True), BLOCKS - 1)
    first = jnp.zeros((1, 1), jnp.int32)
    start_of = jnp.zeros((1, 128), jnp.int32)
    limit_of = jnp.full((1, 128), BLOCK, jnp.int32)
    for u in range(4):
        start_of = jnp.where(lane >= first, first, start_of)
        first = first + meta[4:5, u : u + 1]
        limit_of = jnp.where(lane == first - 1, meta[5:6, u : u + 1], limit_of)
    start_of = jnp.where(lane < BLOCKS, start_of, NO_BLOCK)
    row = iota((8, 128), 0)
    picked = pick4(row, [slot_of, start_of, limit_of, jnp.zeros((1, 128), jnp.int32) + quarter])
    return jnp.where(row == 4, meta[3:4, :], picked)


def pick4(index, values):
    return jnp.where(index == 0, values[0], jnp.where(index == 1, values[1], jnp.where(index == 2, values[2], values[3])))


def first_chunk(meta, t):
    return jnp.clip(meta[1, 4 * t] // 4, 0, TILES - 1)


def walk(meta, t, j, count):
    pairs = []
    for _ in range(count):
        pairs.append((t, j))
        more = j < jnp.minimum(t, TILES - 1)
        after = jnp.minimum(t + 1, TILES)
        j = jnp.where(more, j + 1, first_chunk(meta, after))
        t = jnp.where(more, t, after)
    return pairs, t, j


def pairs_in_all(meta):
    return sum(t + 1 - meta[1, 4 * t] // 4 for t in range(TILES))


def four(ref, meta, n):
    return jnp.concatenate([ref[meta[0, 4 * n + i]] for i in range(4)], axis=0)


def visible(meta, t, j):
    r, lane = iota((BLOCK, 1), 0), iota((1, BLOCK), 1)
    at = (t * 4 + (r >> 5)) * BLOCK + meta[3, 0] * PIECE + (r & 31)
    since = pick4(r >> 5, [meta[1, t * 4 + i] for i in range(4)]) * BLOCK
    where = jnp.concatenate(
        [jnp.where(lane < meta[2, j * 4 + i], (j * 4 + i) * BLOCK + lane, FAR) for i in range(4)], axis=1
    )
    where, at, since = (v.astype(jnp.int16) for v in (where, at, since))
    return (where <= at) & (where >= since)


def result_kernel(layer, d_item, item_weight, layer_out, item_grad):
    layer_out[...] = layer[...]
    item_grad[...] = dot_nt(d_item[...], item_weight[...])


def spec(space):
    return pl.BlockSpec(memory_space=space)


VMEM, SMEM, ANY = pltpu.VMEM, pltpu.SMEM, pl.ANY
DMA = pltpu.SemaphoreType.DMA


def shape(dims, dtype):
    return jax.ShapeDtypeStruct(dims, dtype)


def params(remote=None):
    return pltpu.CompilerParams(
        vmem_limit_bytes=56 << 20, has_side_effects=remote is not None, collective_id=remote
    )


def per_device(
    item_feats, item_weight, send_rows, event_slot, user_blocks, tail_len, block_order, gain_in, gain_mid, w_in, w_out,
    cot_out,
):
    gain_in, gain_mid = gain_in.reshape(1, WIDTH), gain_mid.reshape(1, WIDTH)
    wide = VMEM((256, WIDTH), BF16)
    pieces = VMEM((BLOCKS, PIECE, HEAD), BF16)
    by_head = VMEM((HEADS, 3, 4, PIECE, HEAD), BF16)
    tiles = VMEM((TILES + 1, BLOCK, HEAD), BF16)
    each, one = DMA((SEQ,)), DMA((GROUPS,))
    layer, d_item = pl.pallas_call(
        layer_kernel,
        out_shape=(shape((ROWS, WIDTH), BF16), shape((256, WIDTH), BF16)),
        in_specs=[spec(VMEM)] * 9 + [spec(ANY)] * 3,
        out_specs=(spec(VMEM), spec(VMEM)),
        scratch_shapes=[
            VMEM((WIDTH, 4 * WIDTH), BF16),
            VMEM((WIDTH, WIDTH), BF16),
            VMEM((ROWS, WIDTH), BF16),
            wide,
            wide,
            wide,
            wide,
            VMEM((HEADS, 2, HALF, 2 * HEAD), BF16),
            by_head,
            by_head,
            VMEM((8, 128), jnp.int32),
            VMEM((SEQ, 8, 128), jnp.int32),
            VMEM((SEQ, 2, HALF, 2 * HEAD), BF16),
            VMEM((BLOCKS, BLOCK, 2 * HEAD), BF16),
            pieces,
            pieces,
            VMEM((8, 128), jnp.int32),
            SMEM((8, 128), jnp.int32),
            SMEM((2, 16), jnp.int32),
            VMEM((MOST_PAIRS, BLOCK, HEAD), F32),
            VMEM((MOST_PAIRS, 4, 2 * HEAD, BLOCK), BF16),
            VMEM((HEADS, TILES // 2, 8, BLOCK), F32),
            VMEM((TILES, BLOCK, HEAD), F32),
            pieces,
            pieces,
            pieces,
            pieces,
            by_head,
            by_head,
            tiles,
            tiles,
            tiles,
            VMEM((SEQ, HALF, 2 * HEAD), BF16),
            VMEM((SEQ, HALF, 2 * HEAD), BF16),
            VMEM((SEQ, HALF, 2 * HEAD), BF16),
            VMEM((SEQ, HALF, 2 * HEAD), BF16),
            VMEM((HEADS, 2, 2, HALF, 2 * HEAD), BF16),
            VMEM((SLOTS, 4 * WIDTH), F32),
            VMEM((SLOTS, WIDTH), BF16),
            VMEM((ROWS, WIDTH), F32),
            VMEM((ROWS, WIDTH), BF16),
            VMEM((SLOTS, WIDTH), F32),
            VMEM((SLOTS, 128), F32),
            wide,
            wide,
            wide,
            wide,
            DMA((3,)),
            DMA,
            one,
            one,
            *([each] * 12),
            DMA((HEADS,)),
            DMA((HEADS,)),
            *([each] * 4),
            *([each] * 6),
            one,
            one,
        ],
        compiler_params=params(0),
        name="layer",
    )(
        item_feats, item_weight, send_rows, event_slot, user_blocks, tail_len, block_order, gain_in, gain_mid, w_in,
        w_out, cot_out,
    )
    return pl.pallas_call(
        result_kernel,
        out_shape=(shape((ROWS, WIDTH), BF16), shape((256, WIDTH), F32)),
        in_specs=[spec(VMEM)] * 3,
        out_specs=(spec(VMEM), spec(VMEM)),
        compiler_params=params(),
        name="results",
    )(layer, d_item, item_weight)


def solution(mesh):
    rows = P(("batch", "seq"), None)
    return jax.shard_map(
        per_device,
        mesh=mesh,
        in_specs=(
            rows,
            P(),
            rows,
            P(("batch", "seq")),
            P("batch", None),
            P("batch", None),
            P("batch", None),
            P(),
            P(),
            P(),
            P(),
            rows,
        ),
        out_specs=(rows, rows),
        check_vma=False,
    )
```

time: 127 us -> 116 us (0.913)
  Pallas kernels: 126 us -> 116 us
    pallas_call x3 -> x1, Pallas kernels: 124 us -> 113 us  [per_device(): pl.pallas_call(layer_kernel, out_shape=(shape((ROWS, WIDTH), BF16), shape...]
where the time goes in v6:
time: 116 us
  Pallas kernels  116 us (100%)
    pallas_call x1, Pallas kernels, per_device(): pl.pallas_call(layer_kernel, out_shape=(shape((ROWS, WIDTH), BF16), shape...  113 us
    pallas_call x1, Pallas kernels, per_device(): pl.pallas_call(result_kernel, out_shape=(shape((ROWS, WIDTH), BF16), shap...  2.38 us

profile of v6, /device:TPU:1, one launch (start us, length us, event | category | flops | bytes accessed | tf_op | source)
XLA Modules:
  0.0 116.2 jit_solution(16919282443305678615)
XLA Ops:
  0.6 113.2 %layer.1 = (bf16[384,512]{1,0:T(8,128)(2,1)}, bf16[256,512]{1,0:T(8,128)(2,1)}) custom-call(bf16[256,512]{1,0:T(8,128)(2,1)} %feats.1, bf16[512,512]{1,0:T(8,128)(2,1)} %item_weight.3, s32[1,256]{1,0:T(1,128)} %send_rows.1, s32[384]{0:T(512)} %event_slot.1, s32[1,4]{1,0:T(1,128)} %user_blocks.1, s32[1,4]{1,0:T(1,128)} %tail_len.1, s32[1,48]{1,0:T(1,128)} %block_order.1, ...), custom_call_target="tpu_custom_call" | custom-call | tf_op jit(solution)/shard_map/layer/pallas_call | solution.py:679
  113.8 2.4 %results.1 = (bf16[384,512]{1,0:T(8,128)(2,1)}, f32[256,512]{1,0:T(8,128)}) custom-call(bf16[384,512]{1,0:T(8,128)(2,1)} %get-tuple-element.4.layer, bf16[256,512]{1,0:T(8,128)(2,1)} %get-tuple-element.5.d_item, bf16[512,512]{1,0:T(8,128)(2,1)} %item_weight.3), custom_call_target="tpu_custom_call" | custom-call | tf_op jit(solution)/shard_map/results/pallas_call | solution.py:750

commit v7 on v6

--- a/solution.py
+++ b/solution.py
@@ -19,10 +19,10 @@
 ROWS = 384
 FAR = 30000
 NO_BLOCK = 200
-AT_ONCE = 4
+AT_ONCE = 6
 MOST_PAIRS = 48
 MOST_CHUNKS = 7
-BACK_AT_ONCE = 4
+BACK_AT_ONCE = 6
 SCALE = HEAD**-0.5
 MESH = pl.DeviceIdType.MESH
 F32 = jnp.float32
@@ -401,7 +401,7 @@
                 home_copy(src, dst, send, recv, source),
             )
 
-    @pl.loop(0, BLOCKS)
+    @pl.loop(0, BLOCKS, unroll=4)
     def _(i):
         mixed_slots[i] = mixed_sorted[tables[4, i]]
 
@@ -457,7 +457,7 @@
         dq = (sum_pairs(t, *starts[t]) * (0.5 * SCALE)).astype(BF16)
         dq_sorted[4 * t : 4 * t + 4] = dq.reshape(4, PIECE, HEAD)
 
-    @pl.loop(0, BLOCKS)
+    @pl.loop(0, BLOCKS, unroll=4)
     def _(i):
         dq_slots[i] = dq_sorted[tables[4, i]]
 

time: 116 us -> 116 us (level)
  no operation moved by 1% of the time
where the time goes in v7:
time: 116 us; the launch traced here: 115 us
  Pallas kernels  115 us (99%)
    pallas_call x1, Pallas kernels, per_device(): pl.pallas_call(layer_kernel, out_shape=(shape((ROWS, WIDTH), BF16), shape...  112 us
    pallas_call x1, Pallas kernels, per_device(): pl.pallas_call(result_kernel, out_shape=(shape((ROWS, WIDTH), BF16), shap...  2.38 us

profile of v7, /device:TPU:1, one launch (start us, length us, event | category | flops | bytes accessed | tf_op | source)
XLA Modules:
  0.0 115.4 jit_solution(5821124690852910130)
XLA Ops:
  0.6 112.4 %layer.1 = (bf16[384,512]{1,0:T(8,128)(2,1)}, bf16[256,512]{1,0:T(8,128)(2,1)}) custom-call(bf16[256,512]{1,0:T(8,128)(2,1)} %feats.1, bf16[512,512]{1,0:T(8,128)(2,1)} %item_weight.3, s32[1,256]{1,0:T(1,128)} %send_rows.1, s32[384]{0:T(512)} %event_slot.1, s32[1,4]{1,0:T(1,128)} %user_blocks.1, s32[1,4]{1,0:T(1,128)} %tail_len.1, s32[1,48]{1,0:T(1,128)} %block_order.1, ...), custom_call_target="tpu_custom_call" | custom-call | tf_op jit(solution)/shard_map/layer/pallas_call | solution.py:679
  113.0 2.4 %results.1 = (bf16[384,512]{1,0:T(8,128)(2,1)}, f32[256,512]{1,0:T(8,128)}) custom-call(bf16[384,512]{1,0:T(8,128)(2,1)} %get-tuple-element.4.layer, bf16[256,512]{1,0:T(8,128)(2,1)} %get-tuple-element.5.d_item, bf16[512,512]{1,0:T(8,128)(2,1)} %item_weight.3), custom_call_target="tpu_custom_call" | custom-call | tf_op jit(solution)/shard_map/results/pallas_call | solution.py:750

commit v8 on v7

--- a/solution.py
+++ b/solution.py
@@ -405,14 +405,13 @@
     def _(i):
         mixed_slots[i] = mixed_sorted[tables[4, i]]
 
-    send_home(mixed_slots, mixed_home, mixed_send, mixed_recv)
-
     d_mixed[TILES] = jnp.zeros((BLOCK, HEAD), BF16)
     d_mixed_t[TILES] = jnp.zeros((HEAD, BLOCK), BF16)
     query_t[TILES] = jnp.zeros((HEAD, BLOCK), BF16)
     for t in range(TILES):
         query_t[t] = jnp.transpose(four(q_in, tables, t))
     wait_all(copies)
+    send_home(mixed_slots, mixed_home, mixed_send, mixed_recv)
     for t in range(TILES):
         rows = slice(4 * (t % 2), 4 * (t % 2) + 4)
         of = [stats[h, t // 2, rows, :] for h in range(HEADS)]

time: 116 us -> 113 us (0.974)
  Pallas kernels: 115 us -> 112 us
    pallas_call x1, Pallas kernels: 112 us -> 110 us  [per_device(): pl.pallas_call(layer_kernel, out_shape=(shape((ROWS, WIDTH), BF16), shape...]
where the time goes in v8:
time: 113 us
  Pallas kernels  112 us (99%)
    pallas_call x1, Pallas kernels, per_device(): pl.pallas_call(layer_kernel, out_shape=(shape((ROWS, WIDTH), BF16), shape...  110 us
    pallas_call x1, Pallas kernels, per_device(): pl.pallas_call(result_kernel, out_shape=(shape((ROWS, WIDTH), BF16), shap...  2.38 us

profile of v8, /device:TPU:1, one launch (start us, length us, event | category | flops | bytes accessed | tf_op | source)
XLA Modules:
  0.0 113.1 jit_solution(11563817455045280344)
XLA Ops:
  0.6 110.0 %layer.1 = (bf16[384,512]{1,0:T(8,128)(2,1)}, bf16[256,512]{1,0:T(8,128)(2,1)}) custom-call(bf16[256,512]{1,0:T(8,128)(2,1)} %feats.1, bf16[512,512]{1,0:T(8,128)(2,1)} %item_weight.3, s32[1,256]{1,0:T(1,128)} %send_rows.1, s32[384]{0:T(512)} %event_slot.1, s32[1,4]{1,0:T(1,128)} %user_blocks.1, s32[1,4]{1,0:T(1,128)} %tail_len.1, s32[1,48]{1,0:T(1,128)} %block_order.1, ...), custom_call_target="tpu_custom_call" | custom-call | tf_op jit(solution)/shard_map/layer/pallas_call | solution.py:678
  110.7 2.4 %results.1 = (bf16[384,512]{1,0:T(8,128)(2,1)}, f32[256,512]{1,0:T(8,128)}) custom-call(bf16[384,512]{1,0:T(8,128)(2,1)} %get-tuple-element.4.layer, bf16[256,512]{1,0:T(8,128)(2,1)} %get-tuple-element.5.d_item, bf16[512,512]{1,0:T(8,128)(2,1)} %item_weight.3), custom_call_target="tpu_custom_call" | custom-call | tf_op jit(solution)/shard_map/results/pallas_call | solution.py:749
